TPU v7x, 256 devices: a whole 4x4x8 slice. The times are simulated.
256 devices in a mesh: chan: 32 (over y, z_hi, x), win: 8 (over z_lo, core).
Axes of the slice: x: 4, y: 4, z: 8 (z_hi: 2, z_lo: 4; z = z_hi * 4 + z_lo), core: 2. Of those that a mesh axis runs over, the one named last changes fastest.
Arguments:
- spectra: bfloat16 [8, 4096, 2, 2048], P('win', 'chan'), may hold values from -400 to 400
- pair_first: int32 [32, 1024], P('chan'), may hold values from 0 to 127
- pair_second: int32 [32, 1024], P('chan'), may hold values from 0 to 511, as said below
- pair_count: int32 [32], P('chan'), may hold values from 128 to 1024, as said below
- pair_owner: int32 [32, 1024, 1], P('chan'), may hold values from 0 to 31; in each aligned block of 1024 rows (0 to 1023, 1024 to 2047, ..., all dimensions but the last counted through in order) at most 64 rows name the same one
Outputs:
- stacks: float32 [32, 32, 64, 512], P('chan', None, None, 'win')
Inputs may be any that keep to these rules, and one draw needn't show every extreme that they name: pair_second[b, s] lies between pair_first[b, s] and pair_first[b, s] + 384, and b * 128 + pair_second[b, s] is below 4096. `pair_count`: some block has 1024 listed pairs. `pair_owner`: among the 1024 slots of one block no owner is named more than 64 times.
All inputs are finite; a program needn't handle non-finite values.
Results may differ from a plain program's by a relative error of at most 0.017.
Values may be sent and summed in bfloat16 or wider, within the bound.
No kernel may reach another device: no remote copies, remote signals or barrier semaphores. Data moves between devices by JAX's collectives and lax.ppermute only.
A program may use at most 128 MiB of HBM per device.

v0:
```python
import math

import jax
import jax.numpy as jnp
from jax import lax
from jax.sharding import PartitionSpec as P

LAGS = 512
REACH = 3


def passed_along(value, axis, steps):
    count = lax.axis_size(axis)
    leading, last = (max(0, -steps), min(count, count - steps))
    return lax.ppermute(value, axis, [(source, source + steps) for source in range(leading, last)])


def lag_table(bins, lags, windows):
    freq_index = jnp.arange(bins, dtype=jnp.int32)
    lag_offset = jnp.arange(lags, dtype=jnp.int32) - lags // 2
    phase_index = freq_index[:, None] * lag_offset[None, :] % (2 * bins)
    angles = phase_index.astype(jnp.float32) * (math.pi / bins)
    weights = jnp.where(freq_index == 0, 1.0, 2.0).astype(jnp.float32)[:, None] / math.sqrt(
        bins * windows
    )
    return jnp.concatenate([weights * jnp.cos(angles), -weights * jnp.sin(angles)], 0).astype(
        jnp.bfloat16
    )


def whiten(spectra):
    values = spectra.astype(jnp.float32)
    power = jnp.mean(values * values, axis=(2, 3), keepdims=True)
    return (values * lax.rsqrt(power + 1e-06)).astype(jnp.bfloat16)


def route(stacked, owners, blocks_total, capacity):
    onehot = (owners[:, None] == jnp.arange(blocks_total, dtype=jnp.int32)[None, :]).astype(
        jnp.int32
    )
    before = jnp.cumsum(onehot, axis=0, dtype=jnp.int32) - onehot
    position = jnp.sum(before * onehot, axis=1)
    buffer = jnp.zeros((blocks_total, capacity, stacked.shape[1]), jnp.float32)
    return buffer.at[owners, position].set(stacked)


def on_device(spectra, pair_first, pair_second, pair_count, pair_owner):
    whitened = whiten(spectra)
    pieces = [whitened] + [
        passed_along(whitened, "chan", -offset) for offset in range(1, REACH + 1)
    ]
    window = jnp.concatenate(pieces, 1)
    windows_all = spectra.shape[0] * lax.axis_size("win")
    inverse = lag_table(spectra.shape[3], LAGS, windows_all)
    slots = pair_first.shape[1]
    live_count = pair_count[0]
    first_idx = pair_first[0]
    second_idx = pair_second[0]
    left_rows = jnp.take(window, first_idx, axis=1).astype(jnp.float32)
    right_rows = jnp.take(window, second_idx, axis=1).astype(jnp.float32)
    real_part = left_rows[:, :, 0] * right_rows[:, :, 0] + left_rows[:, :, 1] * right_rows[:, :, 1]
    imag_part = left_rows[:, :, 1] * right_rows[:, :, 0] - left_rows[:, :, 0] * right_rows[:, :, 1]
    cross_spec = jnp.concatenate([real_part, imag_part], -1).astype(jnp.bfloat16)
    result = jnp.einsum("wpf,fl->pl", cross_spec, inverse, preferred_element_type=jnp.float32)
    live = (jnp.arange(slots, dtype=jnp.int32) < live_count).astype(jnp.float32)
    stacked = result * live[:, None]
    blocks_total = lax.axis_size("chan")
    capacity = 2 * slots // blocks_total
    owners = pair_owner[0, :, 0]
    buffer = route(stacked, owners, blocks_total, capacity)
    routed = lax.all_to_all(
        buffer.astype(jnp.bfloat16), "chan", split_axis=0, concat_axis=0, tiled=True
    ).astype(buffer.dtype)
    result = lax.psum_scatter(
        routed.astype(jnp.bfloat16), "win", scatter_dimension=2, tiled=True
    ).astype(jnp.float32)
    return result[None]


def solution(mesh):
    in_specs = (
        P("win", "chan", None, None),
        P("chan", None),
        P("chan", None),
        P("chan"),
        P("chan", None, None),
    )
    out_specs = P("chan", None, None, "win")
    return jax.shard_map(
        on_device, mesh=mesh, in_specs=in_specs, out_specs=out_specs, check_vma=False
    )
```

profile of v0, /device:TPU:32, one launch (start us, length us, event | category | flops | bytes accessed | tf_op | source)
XLA Modules:
  0.0 483.6 jit_solution(248621444329841415)
XLA Ops:
  6.5 0.0 copy-start.5
  6.5 0.0 copy-start.4
  6.5 0.0 copy-start.3
  6.5 0.0 copy-start.2
  6.5 0.0 reduce-scatter.4.cloned.1.call-start
  6.6 2.7 fusion.15
  9.3 2.1 fusion.16
  11.4 1.3 collective-permute-start
  12.7 1.3 collective-permute-start.1
  14.0 1.5 collective-permute-start.2
  15.5 0.7 fusion.27
  16.2 0.7 compare_and_fusion.1
  16.9 0.7 fusion.28
  17.6 0.7 fusion.24
  18.3 9.0 %reduce-window.6 = s32[32,8,128]{2,1,0:T(8,128)S(1)} reduce-window(s32[32,8,128]{2,1,0:T(8,128)S(1)} %fusion.24, s32[]{:T(128)} %constant.22.clone.1), window={size=1x1x128 pad=0_0x0_0x127_0}, to_apply=%region_0.0 | reduce-window | flops 4161536 | bytes 262148 | tf_op jit(solution)/shard_map/reduce-window
  27.3 0.1 slice.32
  27.4 0.1 copy.14
  27.6 0.1 copy.15
  27.7 0.1 broadcast_add_fusion
  27.8 0.0 copy-done.2
  27.9 0.0 copy-done.5
  27.9 0.1 multiply_reduce_fusion
  28.0 0.0 copy-done.4
  28.0 0.1 and_reduce_fusion
  28.7 0.0 copy-done.3
  28.8 18.8 %multiply_convert_fusion.1 = (bf16[2048,512]{1,0:T(8,128)(2,1)S(1)}, bf16[2048,512]{1,0:T(8,128)(2,1)}) fusion(s32[512]{0:T(512)S(1)} %iota_add_fusion, f32[2048]{0:T(1024)S(1)} %get-tuple-element.14, f32[2048]{0:T(1024)S(1)} %get-tuple-element.15), kind=kLoop, calls=%fused_computation.26 | loop fusion | flops 18874368 | bytes 4212736 | tf_op jit(solution)/shard_map/convert.1
  47.5 3.5 collective-permute-done
  51.0 0.0 collective-permute-done.1
  51.0 13.2 %collective-permute-done.2 = bf16[1,128,2,2048]{3,2,1,0:T(2,128)(2,1)} collective-permute-done((bf16[1,128,2,2048]{3,2,1,0:T(2,128)(2,1)S(1)}, bf16[1,128,2,2048]{3,2,1,0:T(2,128)(2,1)}, u32[]{:S(2)}, u32[]{:S(2)}) %collective-permute-start.2) | collective-permute-done | bytes 1048608 | tf_op jit(solution)/shard_map/ppermute | solution.py:15
  64.3 8.3 %maximum_bitcast_fusion = bf16[512,2,2048]{2,1,0:T(2,128)(2,1)} fusion(bf16[1,128,2,2048]{3,2,1,0:T(2,128)(2,1)} %collective-permute-done.2, bf16[1,128,2,2048]{3,2,1,0:T(2,128)(2,1)} %collective-permute-done.1, bf16[1,128,2,2048]{3,2,1,0:T(2,128)(2,1)} %collective-permute-done, bf16[1,128,2,2048]{3,2,1,0:T(2,128)(2,1)S(1)} %fusion.16), kind=kLoop, calls=%fused_computation.19 | loop fusion | flops 6291456 | bytes 8388608 | tf_op jit(solution)/shard_map/jit(_take)/Arg_0.9 | solution.py:59
  72.5 27.4 %gather_fusion = bf16[1024,2,2048]{2,1,0:T(2,128)(2,1)} fusion(bf16[512,2,2048]{2,1,0:T(2,128)(2,1)} %maximum_bitcast_fusion, s32[1024]{0:T(1024)S(1)} %fusion.27), kind=kCustom, calls=%fused_computation.clone | custom fusion | bytes 16781312 | tf_op jit(solution)/shard_map/jit(_take)/gather | solution.py:59
  99.9 27.4 %gather_fusion.1 = bf16[1024,2,2048]{2,1,0:T(2,128)(2,1)} fusion(bf16[512,2,2048]{2,1,0:T(2,128)(2,1)} %maximum_bitcast_fusion, s32[1024]{0:T(1024)S(1)} %fusion.28), kind=kCustom, calls=%fused_computation.1.clone | custom fusion | bytes 16781312 | tf_op jit(solution)/shard_map/jit(_take)/gather | solution.py:60
  127.3 0.0 copy-start
  127.3 12.8 %fusion = f32[1,1024,2,2048]{3,2,1,0:T(2,128)} fusion(pred[1024]{0:T(1024)(128)(4,1)S(1)} %compare_and_fusion.1, bf16[1024,2,2048]{2,1,0:T(2,128)(2,1)} %gather_fusion), kind=kLoop, calls=%fused_computation.5 | loop fusion | flops 8388608 | bytes 25166848 | tf_op jit(solution)/shard_map/convert_element_type | solution.py:59
  140.1 0.0 copy-done
  140.1 11.9 %fusion.1 = f32[1,1024,2,2048]{3,2,1,0:T(2,128)} fusion(pred[1024]{0:T(1024)(128)(4,1)S(1)} %compare_and_fusion, bf16[1024,2,2048]{2,1,0:T(2,128)(2,1)S(1)} %copy-done), kind=kLoop, calls=%fused_computation.6 | loop fusion | flops 8388608 | bytes 25166848 | tf_op jit(solution)/shard_map/convert_element_type | solution.py:60
  152.0 40.9 %add_convert_fusion = (bf16[1,1024,1,2048]{3,2,1,0:T(2,128)(2,1)}, bf16[1,1024,1,2048]{3,2,1,0:T(2,128)(2,1)}) fusion(f32[1,1024,2,2048]{3,2,1,0:T(2,128)} %fusion.1, f32[1,1024,2,2048]{3,2,1,0:T(2,128)} %fusion), kind=kLoop, calls=%fused_computation.12 | loop fusion | flops 16777216 | bytes 41943040 | tf_op jit(solution)/shard_map/convert.6
  192.9 0.0 copy-start.1
  192.9 13.2 %copy_bitcast_fusion = (bf16[1024,2048]{1,0:T(8,128)(2,1)S(1)}, bf16[1024,2048]{1,0:T(8,128)(2,1)S(1)}) fusion(bf16[1,1024,1,2048]{3,2,1,0:T(2,128)(2,1)} %get-tuple-element.7, bf16[1,1024,1,2048]{3,2,1,0:T(2,128)(2,1)} %get-tuple-element.6), kind=kLoop, calls=%fused_computation.23 | loop fusion | bytes 16777216
  206.1 0.0 copy-done.1
  206.1 5.8 %fusion.2 = f32[1024,512]{1,0:T(8,128)} fusion(bf16[1024,2048]{1,0:T(8,128)(2,1)S(1)} %get-tuple-element.12, bf16[1024,2048]{1,0:T(8,128)(2,1)S(1)} %get-tuple-element.13, bf16[2048,512]{1,0:T(8,128)(2,1)S(1)} %copy-done.1, bf16[2048,512]{1,0:T(8,128)(2,1)S(1)} %get-tuple-element.8), kind=kOutput, calls=%fused_computation.7 | convolution fusion | flops 4320133120 | bytes 14680064 | tf_op jit(solution)/shard_map/wpf,fl->pl/dot_general | solution.py:64
  211.9 8.1 %scatter_custom_fusion = f32[2048,512]{1,0:T(8,128)} fusion(s32[1024]{0:T(1024)S(1)} %broadcast_select_fusion.2, f32[]{:T(128)} %constant.21.clone.1, f32[1024,512]{1,0:T(8,128)} %fusion.2, f32[1024]{0:T(1024)S(1)} %fusion.25), kind=kCustom, calls=%fused_computation.34 | custom fusion | flops 524288 | bytes 6295556
  220.1 2.5 convert_element_type.52
  222.5 178.8 %all_to_all.5 = bf16[32,64,512]{2,1,0:T(8,128)(2,1)S(1)} all-to-all(bf16[32,64,512]{2,1,0:T(8,128)(2,1)S(1)} %bitcast.45), channel_id=1, replica_groups=mesh['chan'=32,'win'=8] {'chan'}, dimensions={0} | all-to-all | bytes 4194304 | tf_op jit(solution)/shard_map/all_to_all | solution.py:71
  401.3 6.6 %copy.16 = bf16[32,64,512]{1,0,2:T(8,128)(2,1)} copy(bf16[32,64,512]{2,1,0:T(8,128)(2,1)S(1)} %all_to_all.5) | data formatting | bytes 4194304
  408.0 6.8 %reshape.195 = bf16[512,2048]{1,0:T(8,128)(2,1)} reshape(bf16[512,32,64]{2,1,0:T(8,128)(2,1)} %bitcast.44) | data formatting | bytes 4194304
  414.7 0.0 reduce-scatter.4.cloned.1.call-update
  414.7 58.8 %reduce-scatter.4.cloned.1.call-done = bf16[64,2048]{1,0:T(8,128)(2,1)} async-done(((bf16[512,2048]{1,0:T(8,128)(2,1)}), bf16[64,2048]{1,0:T(8,128)(2,1)}) %reduce-scatter.4.cloned.1.call-update) | async-done | bytes 262160
  473.5 1.5 reshape.196
  475.0 0.6 copy.17
  475.6 1.1 bitcast_convert_fusion
  (10 shorter events, 0.1 us)
Async XLA Ops:
  6.5 21.3 %copy-start.5 = (s32[2]{0:T(128)S(1)}, s32[2]{0:T(128)}, u32[]{:S(2)}) copy-start(s32[2]{0:T(128)} %constant.61) | copy-start | bytes 28
  6.5 21.4 %copy-start.4 = (s32[2]{0:T(128)S(1)}, s32[2]{0:T(128)}, u32[]{:S(2)}) copy-start(s32[2]{0:T(128)} %constant.64) | copy-start | bytes 28
  6.5 22.2 %copy-start.3 = (s32[1,1024]{1,0:T(1,128)S(1)}, s32[1,1024]{1,0:T(1,128)}, u32[]{:S(2)}) copy-start(s32[1,1024]{1,0:T(1,128)} %param.9) | copy-start | bytes 12292
  6.5 21.2 %copy-start.2 = (s32[1,1024,1]{1,2,0:T(1,128)S(1)}, s32[1,1024,1]{1,2,0:T(1,128)}, u32[]{:S(2)}) copy-start(s32[1,1024,1]{1,2,0:T(1,128)} %param.11) | copy-start | bytes 12292
  6.5 467.0 %reduce-scatter.4.cloned.1.call-start = ((), (), s32[]{:S(2)}) async-start(), calls=%async_computation.2 | async-start | bytes 2359296
  11.4 39.6 %collective-permute-start = (bf16[1,128,2,2048]{3,2,1,0:T(2,128)(2,1)S(1)}, bf16[1,128,2,2048]{3,2,1,0:T(2,128)(2,1)}, u32[]{:S(2)}, u32[]{:S(2)}) collective-permute-start(bf16[1,128,2,2048]{3,2,1,0:T(2,128)(2,1)S(1)} %fusion.16), channel_id=1, source_target_pairs={{8,0},{16,8},{24,16},{32,24},{40,32},{48,40},{56,48},{64,56},{72,6... | collective-permute-start | bytes 3145736 | tf_op jit(solution)/shard_map/ppermute | solution.py:15
  12.7 38.3 %collective-permute-start.1 = (bf16[1,128,2,2048]{3,2,1,0:T(2,128)(2,1)S(1)}, bf16[1,128,2,2048]{3,2,1,0:T(2,128)(2,1)}, u32[]{:S(2)}, u32[]{:S(2)}) collective-permute-start(bf16[1,128,2,2048]{3,2,1,0:T(2,128)(2,1)S(1)} %fusion.16), channel_id=1, source_target_pairs={{16,0},{24,8},{32,16},{40,24},{48,32},{56,40},{64,48},{72,56},{80,... | collective-permute-start | bytes 3145736 | tf_op jit(solution)/shard_map/ppermute | solution.py:15
  14.0 50.2 %collective-permute-start.2 = (bf16[1,128,2,2048]{3,2,1,0:T(2,128)(2,1)S(1)}, bf16[1,128,2,2048]{3,2,1,0:T(2,128)(2,1)}, u32[]{:S(2)}, u32[]{:S(2)}) collective-permute-start(bf16[1,128,2,2048]{3,2,1,0:T(2,128)(2,1)S(1)} %fusion.16), channel_id=1, source_target_pairs={{24,0},{32,8},{40,16},{48,24},{56,32},{64,40},{72,48},{80,56},{88,... | collective-permute-start | bytes 3145736 | tf_op jit(solution)/shard_map/ppermute | solution.py:15
  127.3 12.8 %copy-start = (bf16[1024,2,2048]{2,1,0:T(2,128)(2,1)S(1)}, bf16[1024,2,2048]{2,1,0:T(2,128)(2,1)}, u32[]{:S(2)}) copy-start(bf16[1024,2,2048]{2,1,0:T(2,128)(2,1)} %gather_fusion.1) | copy-start | bytes 25165828
  192.9 13.2 %copy-start.1 = (bf16[2048,512]{1,0:T(8,128)(2,1)S(1)}, bf16[2048,512]{1,0:T(8,128)(2,1)}, u32[]{:S(2)}) copy-start(bf16[2048,512]{1,0:T(8,128)(2,1)} %get-tuple-element.9) | copy-start | bytes 6291460
Sparse Core Ops, SparseCore 0:
  414.9 58.6 reduce-scatter.3
where the time goes:
time: 488 us; the launch traced here: 484 us
  blocking collectives  179 us (37%)
  other arithmetic  121 us (25%)
  local copies, waits for them, and re-layouts  83.8 us (17%)
  waiting for transfers between devices  75.5 us (15%)
  between operations  14.2 us (3%)
  matrix products  5.82 us (1%)
    all_to_all x1, blocking collectives, on_device(): lax.all_to_all(buffer.astype(jnp.bfloat16), 'chan', split_axis=0, concat_...  179 us
    another operation x5, other arithmetic  68.8 us
    unnamed x2, waiting for transfers between devices  58.8 us
    unnamed x17, local copies, waits for them, and re-layouts  28.7 us
    gather x1, local copies, waits for them, and re-layouts, on_device(): left_rows = jnp.take(window, first_idx, axis=1).astype(jnp.float32)  27.4 us
    gather x1, local copies, waits for them, and re-layouts, on_device(): right_rows = jnp.take(window, second_idx, axis=1).astype(jnp.float32)  27.4 us
    ppermute x3, waiting for transfers between devices, passed_along(): lax.ppermute(value, axis, [(source, source + steps) for source in range(l...  16.7 us
    convert_element_type x1, other arithmetic, on_device(): left_rows = jnp.take(window, first_idx, axis=1).astype(jnp.float32)  12.8 us
  transfers between devices with their start and end apart: 4, of which 3 were waited for; matrix products, arithmetic and copies ran while one was open for 6% of the time, Pallas kernels for 0%

commit v1 on v0

v1 whole, which is shorter than its diff:
```python
import functools
import math

import jax
import jax.numpy as jnp
from jax import lax
from jax.experimental import pallas as pl
from jax.experimental.pallas import tpu as pltpu
from jax.sharding import PartitionSpec as P

LAGS = 512
REACH = 3
CHUNKS = 4
ROWS = 256
AXES = ("chan", "win")
N_X = 4
N_CORE = 2


def pairs_of(move):
    pairs = []
    for chan in range(32):
        for win in range(8):
            row, x, z, core = chan // N_X, chan % N_X, win // N_CORE, win % N_CORE
            row, x, z, core = move(row, x, z, core)
            pairs.append((chan * 8 + win, (row * N_X + x) * 8 + z * N_CORE + core))
    return pairs


def to_previous_row(row, x, z, core):
    return ((row - 1) % 8 if x < REACH else row), x, z, core


CROSS = pairs_of(to_previous_row)
AROUND = {d: pairs_of(lambda row, x, z, core, d=d: (row, (x - d) % N_X, z, core)) for d in (1, 2, 3)}
OTHER_CORE = pairs_of(lambda row, x, z, core: (row, x, z, 1 - core))
OTHER_CHIP = {k: pairs_of(lambda row, x, z, core, k=k: (row, x, z ^ k, core)) for k in (1, 2, 3)}


def lag_table(bins, windows):
    win = lax.axis_index("win")
    z, core = win // N_CORE, win % N_CORE
    column = jnp.arange(LAGS, dtype=jnp.int32)
    half, block, inner = column // 256, column // 64 % 4, column % 64
    lag = ((z ^ block) * N_CORE + (core ^ half)) * 64 + inner - LAGS // 2
    freq_index = jnp.arange(bins, dtype=jnp.int32)
    phase_index = freq_index[:, None] * lag[None, :] % (2 * bins)
    angles = phase_index.astype(jnp.float32) * (math.pi / bins)
    weights = jnp.where(freq_index == 0, 1.0, 2.0).astype(jnp.float32)[:, None] / math.sqrt(
        bins * windows
    )
    return jnp.stack([weights * jnp.cos(angles), -weights * jnp.sin(angles)], 0).astype(jnp.bfloat16)


def whiten(spectra):
    values = spectra.astype(jnp.float32)
    power = jnp.mean(values * values, axis=(1, 2), keepdims=True)
    return (values * lax.rsqrt(power + 1e-06)).astype(jnp.bfloat16)


def dot(a, b):
    return lax.dot_general(a, b, (((1,), (0,)), ((), ())), preferred_element_type=jnp.float32)


def correlate(bins, first_ref, second_ref, own_ref, one_ref, two_ref, three_ref, table_ref, acc):
    left_hot = first_ref[...]
    right_hot = second_ref[...]
    step = min(512, bins)
    for start in range(0, bins, step):
        at = pl.ds(start, step)
        left = [dot(left_hot, own_ref[part, :, at]) for part in range(2)]
        right = [
            dot(
                right_hot,
                jnp.concatenate(
                    [ref[part, :, at] for ref in (own_ref, one_ref, two_ref, three_ref)], 0
                ),
            )
            for part in range(2)
        ]
        real = (left[0] * right[0] + left[1] * right[1]).astype(jnp.bfloat16)
        imag = (left[1] * right[0] - left[0] * right[1]).astype(jnp.bfloat16)
        part = dot(real, table_ref[0, at, :]) + dot(imag, table_ref[1, at, :])
        acc = part if acc is None else acc + part
    return acc


def first_kernel(bins, first, second, own, one, two, three, table, out):
    out[...] = correlate(bins, first, second, own, one, two, three, table, None)


def next_kernel(bins, first, second, own, one, two, three, table, acc, out):
    out[...] = correlate(bins, first, second, own, one, two, three, table, acc[...])


def last_kernel(bins, first, second, own, one, two, three, table, acc, keep, send):
    total = correlate(bins, first, second, own, one, two, three, table, acc[...])
    keep[...] = total[:, :256]
    send[...] = total[:, 256:].astype(jnp.bfloat16)


def run_chunk(kernel, first_hot, second_hot, blocks, table, acc, outs):
    slots = first_hot.shape[0]
    bins = blocks[0].shape[2]

    def rows(width):
        return pl.BlockSpec((ROWS, width), lambda i: (i, 0))

    def whole(shape):
        return pl.BlockSpec(shape, lambda i: (0,) * len(shape))

    operands = [first_hot, second_hot, *blocks, table] + ([] if acc is None else [acc])
    in_specs = [rows(128), rows(512)] + [whole(b.shape) for b in blocks] + [whole(table.shape)]
    in_specs += [] if acc is None else [rows(512)]
    return pl.pallas_call(
        functools.partial(kernel, bins),
        grid=(slots // ROWS,),
        in_specs=in_specs,
        out_specs=[rows(o.shape[1]) for o in outs],
        out_shape=outs,
        compiler_params=pltpu.CompilerParams(vmem_limit_bytes=56 << 20),
        cost_estimate=pl.CostEstimate(
            flops=2 * slots * 2 * bins * (640 + 512), bytes_accessed=8 << 20, transcendentals=0
        ),
        name="correlate",
    )(*operands)


def split_kernel(keep, received, *outs):
    total = keep[...] + received[...].astype(jnp.float32)
    half = total.shape[0] // 2
    for k, out in enumerate(outs):
        piece = total[:, 64 * k : 64 * k + 64]
        out[...] = jnp.concatenate([piece[:half], piece[half:]], 1).astype(out.dtype)


def route_kernel(hot, keep, one, two, three, out):
    total = keep[...]
    for ref in (one, two, three):
        total = total + ref[...].astype(jnp.float32)
    rows = jnp.concatenate([total[:, :64], total[:, 64:]], 0).astype(jnp.bfloat16)
    for owner in range(32):
        placed = dot(hot[64 * owner : 64 * owner + 64, :], rows)
        out[owner] = jnp.concatenate([placed[:32], placed[32:]], 1).astype(jnp.bfloat16)


def unpack_kernel(routed, out):
    for block in range(32):
        values = routed[block].astype(jnp.float32)
        out[0, block, :32] = values[:, :64]
        out[0, block, 32:] = values[:, 64:]


def call(kernel, out_shape, *operands):
    return pl.pallas_call(
        kernel,
        out_shape=out_shape,
        compiler_params=pltpu.CompilerParams(vmem_limit_bytes=40 << 20),
        name=kernel.__name__,
    )(*operands)


def on_device(spectra, pair_first, pair_second, pair_count, pair_owner):
    windows_all = spectra.shape[0] * lax.axis_size("win")
    bins = spectra.shape[3]
    slots = pair_first.shape[1]
    x_place = lax.axis_index("chan") % N_X
    whitened = jnp.swapaxes(whiten(spectra[0]), 0, 1)
    size = bins // CHUNKS
    own = [whitened[:, :, q * size : (q + 1) * size] for q in range(CHUNKS)]
    crossed = [lax.ppermute(chunk, AXES, CROSS) for chunk in own]

    first_hot = (pair_first[0][:, None] == jnp.arange(128, dtype=jnp.int32)).astype(jnp.bfloat16)
    second_hot = (pair_second[0][:, None] == jnp.arange(512, dtype=jnp.int32)).astype(jnp.bfloat16)
    owners = pair_owner[0, :, 0]
    onehot = (owners[:, None] == jnp.arange(32, dtype=jnp.int32)[None, :]).astype(jnp.int32)
    before = jnp.cumsum(onehot, axis=0, dtype=jnp.int32) - onehot
    place = owners * 64 + jnp.sum(before * onehot, axis=1)
    place = jnp.where(jnp.arange(slots, dtype=jnp.int32) < pair_count[0], place, -1)
    place_hot = (place[None, :] == jnp.arange(2048, dtype=jnp.int32)[:, None]).astype(jnp.bfloat16)
    table = lag_table(bins, windows_all)

    acc = None
    f32 = jnp.float32
    for q in range(CHUNKS):
        ahead = {}
        for d in (2, 1, 3):
            source = jnp.where(x_place < d, crossed[q], own[q])
            ahead[d] = lax.ppermute(source, AXES, AROUND[d])
        blocks = [own[q], ahead[1], ahead[2], ahead[3]]
        part = table[:, q * size : (q + 1) * size]
        whole = jax.ShapeDtypeStruct((slots, LAGS), f32)
        if q == CHUNKS - 1:
            outs = [
                jax.ShapeDtypeStruct((slots, 256), f32),
                jax.ShapeDtypeStruct((slots, 256), jnp.bfloat16),
            ]
            keep, send = run_chunk(last_kernel, first_hot, second_hot, blocks, part, acc, outs)
        else:
            kernel = first_kernel if q == 0 else next_kernel
            (acc,) = run_chunk(kernel, first_hot, second_hot, blocks, part, acc, [whole])
    received = lax.ppermute(send, AXES, OTHER_CORE)
    packed = (slots // 2, 128)
    pieces = call(
        split_kernel,
        [jax.ShapeDtypeStruct(packed, f32)] + [jax.ShapeDtypeStruct(packed, jnp.bfloat16)] * 3,
        keep,
        received,
    )
    arrived = [lax.ppermute(pieces[k], AXES, OTHER_CHIP[k]) for k in (1, 2, 3)]
    buffer = call(
        route_kernel, jax.ShapeDtypeStruct((32, 32, 128), jnp.bfloat16), place_hot, pieces[0], *arrived
    )
    routed = lax.all_to_all(buffer, "chan", split_axis=0, concat_axis=0, tiled=True)
    return call(unpack_kernel, jax.ShapeDtypeStruct((1, 32, 64, 64), f32), routed)


def solution(mesh):
    in_specs = (
        P("win", "chan", None, None),
        P("chan", None),
        P("chan", None),
        P("chan"),
        P("chan", None, None),
    )
    out_specs = P("chan", None, None, "win")
    return jax.shard_map(
        on_device, mesh=mesh, in_specs=in_specs, out_specs=out_specs, check_vma=False
    )
```

time: 488 us -> 173 us (0.35)
  blocking collectives: 179 us -> 20.1 us
  other arithmetic: 121 us -> 40 us
  local copies, waits for them, and re-layouts: 83.8 us -> 3.85 us
  waiting for transfers between devices: 75.5 us -> 32.6 us
  starting transfers between devices: 4.09 us -> 44.7 us
  Pallas kernels: 0 us -> 30.2 us
  between operations: 14.2 us -> 0.98 us
  matrix products: 5.82 us -> 0 us
    all_to_all x1, blocking collectives: 179 us -> 20.1 us  [on_device(): lax.all_to_all(buffer, 'chan', split_axis=0, concat_axis=0, tiled=True)]
    unnamed x2 -> x0, waiting for transfers between devices: 58.8 us -> none
    gather x2 -> x0, local copies, waits for them, and re-layouts: 54.8 us -> none  [the longest x1 27.4 us: on_device(): left_rows = jnp.take(window, first_idx, axis=1).astype(jnp.float32)]
    another operation x6 -> x5, other arithmetic: 77.1 us -> 30.2 us
    ppermute x3 -> x20, starting transfers between devices: 4.06 us -> 44.7 us  [the longest x4 22.5 us: on_device(): crossed = [lax.ppermute(chunk, AXES, CROSS) for chunk in own]]
    pallas_call x0 -> x7, Pallas kernels: none -> 30.2 us  [the longest x4 27.4 us: run_chunk(): pl.pallas_call(functools.partial(kernel, bins), grid=(slots // ROWS,), in...]
    convert_element_type x6 -> x4, other arithmetic: 29.9 us -> 4.23 us  [the longest x1 2.09 us: on_device(): (place[None, :] == jnp.arange(2048, dtype=jnp.int32)[:, None]).astype(jnp...]
    unnamed x17 -> x36, local copies, waits for them, and re-layouts: 28.7 us -> 3.54 us
  transfers between devices with their start and end apart: 4 -> 20, of which waited for: 3 -> 7; matrix products, arithmetic and copies ran while one was open for 6% -> 20% of each run, Pallas kernels for 0% -> 12%
where the time goes in v1:
time: 173 us; the launch traced here: 172 us
  starting transfers between devices  44.7 us (26%)
  other arithmetic  40 us (23%)
  waiting for transfers between devices  32.6 us (19%)
  Pallas kernels  30.2 us (17%)
  blocking collectives  20.1 us (12%)
  local copies, waits for them, and re-layouts  3.85 us (2%)
    another operation x4, other arithmetic  27.9 us
    pallas_call x4, Pallas kernels, run_chunk(): pl.pallas_call(functools.partial(kernel, bins), grid=(slots // ROWS,), in...  27.4 us
    ppermute x4, starting transfers between devices, on_device(): crossed = [lax.ppermute(chunk, AXES, CROSS) for chunk in own]  22.5 us
    ppermute x4, waiting for transfers between devices, on_device(): crossed = [lax.ppermute(chunk, AXES, CROSS) for chunk in own]  21.1 us
    all_to_all x1, blocking collectives, on_device(): lax.all_to_all(buffer, 'chan', split_axis=0, concat_axis=0, tiled=True)  20.1 us
    ppermute x12, starting transfers between devices, on_device(): ahead[d] = lax.ppermute(source, AXES, AROUND[d])  18.6 us
    ppermute x3, waiting for transfers between devices, on_device(): arrived = [lax.ppermute(pieces[k], AXES, OTHER_CHIP[k]) for k in (1, 2, 3)]  9.61 us
    ppermute x3, starting transfers between devices, on_device(): arrived = [lax.ppermute(pieces[k], AXES, OTHER_CHIP[k]) for k in (1, 2, 3)]  3.58 us
  transfers between devices with their start and end apart: 20, of which 7 were waited for; matrix products, arithmetic and copies ran while one was open for 20% of the time, Pallas kernels for 12%

profile of v1, /device:TPU:32, one launch (start us, length us, event | category | flops | bytes accessed | tf_op | source)
XLA Modules:
  0.0 172.4 jit_solution(7491323894302940275)
XLA Ops:
  0.0 1.7 fusion.7
  1.7 1.7 fusion.10
  3.4 0.0 copy-start.7
  3.4 10.7 %collective-permute-start.12 = (bf16[2,128,512]{2,1,0:T(8,128)(2,1)S(1)}, bf16[2,128,512]{2,1,0:T(8,128)(2,1)}, u32[]{:S(2)}, u32[]{:S(2)}) collective-permute-start(bf16[2,128,512]{2,1,0:T(8,128)(2,1)S(1)} %slice.51.own), channel_id=1, source_target_pairs={{0,224},{1,225},{2,226},{3,227},{4,228},{5,229},{6,230},{7,231},{8... | collective-permute-start | bytes 786440 | tf_op jit(solution)/shard_map/ppermute | solution.py:171
  14.2 18.7 %multiply_convert_fusion = (bf16[1,2048,512]{2,1,0:T(8,128)(2,1)S(1)}, bf16[1,2048,512]{2,1,0:T(8,128)(2,1)}) fusion(f32[2048]{0:T(1024)S(1)} %get-tuple-element.45, s32[512]{0:T(512)S(1)} %fusion.30, f32[2048]{0:T(1024)S(1)} %get-tuple-element.44), kind=kLoop, calls=%fused_computation.14 | loop fusion | flops 18874368 | bytes 4212736 | tf_op jit(solution)/shard_map/convert.2
  32.9 0.0 collective-permute-done.12
  32.9 1.9 %broadcast_select_fusion = (bf16[2,128,512]{2,1,0:T(8,128)(2,1)}, bf16[2,128,512]{2,1,0:T(8,128)(2,1)S(1)}, bf16[2,128,512]{2,1,0:T(8,128)(2,1)S(1)}, bf16[2,128...) fusion(bf16[2,128,512]{2,1,0:T(8,128)(2,1)} %collective-permute-done.12, ...), kind=kLoop, calls=%fused_computation.32 | loop fusion | flops 393216 | bytes 2883587 | tf_op jit(solution)/shard_map/jit(_where)/select_n | solution.py:188
  34.8 2.7 %collective-permute-start = (bf16[2,128,512]{2,1,0:T(8,128)(2,1)S(1)}, bf16[2,128,512]{2,1,0:T(8,128)(2,1)S(1)}, u32[]{:S(2)}, u32[]{:S(2)}) collective-permute-start(bf16[2,128,512]{2,1,0:T(8,128)(2,1)S(1)} %get-tuple-element.35.own), channel_id=1, source_target_pairs={{0,224},{1,225},{2,226},{3,227},{4,228},{5,229},{6,230},{7,231},{8... | collective-permute-start | bytes 786440 | tf_op jit(solution)/shard_map/ppermute | solution.py:171
  37.5 7.2 %collective-permute-start.4 = (bf16[2,128,512]{2,1,0:T(8,128)(2,1)S(1)}, bf16[2,128,512]{2,1,0:T(8,128)(2,1)S(1)}, u32[]{:S(2)}, u32[]{:S(2)}) collective-permute-start(bf16[2,128,512]{2,1,0:T(8,128)(2,1)S(1)} %get-tuple-element.34.own), channel_id=1, source_target_pairs={{0,224},{1,225},{2,226},{3,227},{4,228},{5,229},{6,230},{7,231},{8... | collective-permute-start | bytes 786440 | tf_op jit(solution)/shard_map/ppermute | solution.py:171
  44.7 1.9 %collective-permute-start.8 = (bf16[2,128,512]{2,1,0:T(8,128)(2,1)S(1)}, bf16[2,128,512]{2,1,0:T(8,128)(2,1)S(1)}, u32[]{:S(2)}, u32[]{:S(2)}) collective-permute-start(bf16[2,128,512]{2,1,0:T(8,128)(2,1)S(1)} %get-tuple-element.33.own), channel_id=1, source_target_pairs={{0,224},{1,225},{2,226},{3,227},{4,228},{5,229},{6,230},{7,231},{8... | collective-permute-start | bytes 786440 | tf_op jit(solution)/shard_map/ppermute | solution.py:171
  46.7 1.2 fusion.9.second
  47.9 2.3 %pad_maximum_fusion = (bf16[2,512,512]{2,1,0:T(8,128)(2,1)}, bf16[2,512,512]{2,1,0:T(8,128)(2,1)}, bf16[2,512,512]{2,1,0:T(8,128)(2,1)}, bf16[2,512,512]{2,1,0:T(8,128)(2,1)}) fusion(bf16[1,2048,512]{2,1,0:T(8,128)(2,1)S(1)} %get-tuple-element.42, bf16[1,2048,512]{2,1,0:T(8,128)(2,1)S(1)} %copy-done.1), kind=kLoop, calls=%fused_computation.29 | loop fusion | flops 8388608 | bytes 8388608 | tf_op jit(solution)/shard_map/stack | solution.py:52
  50.2 0.0 copy-start.6
  50.2 0.1 collective-permute-start.13
  50.3 3.5 %collective-permute-start.14 = (bf16[2,128,512]{2,1,0:T(8,128)(2,1)S(1)}, bf16[2,128,512]{2,1,0:T(8,128)(2,1)S(1)}, u32[]{:S(2)}, u32[]{:S(2)}) collective-permute-start(bf16[2,128,512]{2,1,0:T(8,128)(2,1)S(1)} %get-tuple-element.22), channel_id=1, source_target_pairs={{0,16},{1,17},{2,18},{3,19},{4,20},{5,21},{6,22},{7,23},{8,24},{9,... | collective-permute-start | bytes 786440 | tf_op jit(solution)/shard_map/ppermute | solution.py:189
  53.9 5.4 %collective-permute-done = bf16[2,128,512]{2,1,0:T(8,128)(2,1)S(1)} collective-permute-done((bf16[2,128,512]{2,1,0:T(8,128)(2,1)S(1)}, bf16[2,128,512]{2,1,0:T(8,128)(2,1)S(1)}, u32[]{:S(2)}, u32[]{:S(2)}) %collective-permute-start) | collective-permute-done | bytes 262176 | tf_op jit(solution)/shard_map/ppermute | solution.py:171
  59.3 1.5 collective-permute-start.15
  60.8 11.4 %collective-permute-done.4 = bf16[2,128,512]{2,1,0:T(8,128)(2,1)S(1)} collective-permute-done((bf16[2,128,512]{2,1,0:T(8,128)(2,1)S(1)}, bf16[2,128,512]{2,1,0:T(8,128)(2,1)S(1)}, u32[]{:S(2)}, u32[]{:S(2)}) %collective-permute-start.4) | collective-permute-done | bytes 262176 | tf_op jit(solution)/shard_map/ppermute | solution.py:171
  72.2 4.2 %collective-permute-done.8 = bf16[2,128,512]{2,1,0:T(8,128)(2,1)S(1)} collective-permute-done((bf16[2,128,512]{2,1,0:T(8,128)(2,1)S(1)}, bf16[2,128,512]{2,1,0:T(8,128)(2,1)S(1)}, u32[]{:S(2)}, u32[]{:S(2)}) %collective-permute-start.8) | collective-permute-done | bytes 262176 | tf_op jit(solution)/shard_map/ppermute | solution.py:171
  76.4 0.2 broadcast_select_fusion.1
  76.6 3.1 %collective-permute-start.10 = (bf16[2,128,512]{2,1,0:T(8,128)(2,1)S(1)}, bf16[2,128,512]{2,1,0:T(8,128)(2,1)S(1)}, u32[]{:S(2)}, u32[]{:S(2)}) collective-permute-start(bf16[2,128,512]{2,1,0:T(8,128)(2,1)S(1)} %get-tuple-element.25), channel_id=1, source_target_pairs={{0,16},{1,17},{2,18},{3,19},{4,20},{5,21},{6,22},{7,23},{8,24},{9,... | collective-permute-start | bytes 786440 | tf_op jit(solution)/shard_map/ppermute | solution.py:189
  79.7 0.9 fusion.14.first
  80.7 0.0 collective-permute-start.11
  80.7 3.2 %collective-permute-start.9 = (bf16[2,128,512]{2,1,0:T(8,128)(2,1)S(1)}, bf16[2,128,512]{2,1,0:T(8,128)(2,1)}, u32[]{:S(2)}, u32[]{:S(2)}) collective-permute-start(bf16[2,128,512]{2,1,0:T(8,128)(2,1)S(1)} %get-tuple-element.26), channel_id=1, source_target_pairs={{0,24},{1,25},{2,26},{3,27},{4,28},{5,29},{6,30},{7,31},{8,0},{9,1... | collective-permute-start | bytes 786440 | tf_op jit(solution)/shard_map/ppermute | solution.py:189
  83.9 0.1 collective-permute-start.5
  84.0 0.6 copy-done.10
  84.6 9.0 %reduce-window.6 = s32[32,8,128]{2,1,0:T(8,128)S(1)} reduce-window(s32[32,8,128]{2,1,0:T(8,128)S(1)} %fusion.18, s32[]{:T(128)} %constant.111.clone.1), window={size=1x1x128 pad=0_0x0_0x127_0}, to_apply=%region_0.1 | reduce-window | flops 4161536 | bytes 262148 | tf_op jit(solution)/shard_map/reduce-window
  93.6 0.1 slice.40
  93.7 0.1 copy.7
  93.9 0.1 copy.8
  94.6 0.0 collective-permute-done.15.three
  94.7 0.3 collective-permute-start.6
  95.0 0.0 collective-permute-done.10.two
  95.0 1.2 collective-permute-start.7
  96.2 6.6 %correlate.4.acc = f32[1024,512]{1,0:T(8,128)} custom-call(bf16[1024,128]{1,0:T(8,128)(2,1)} %fusion.14.first, bf16[1024,512]{1,0:T(8,128)(2,1)} %fusion.9.second, bf16[2,128,512]{2,1,0:T(8,128)(2,1)} %copy-done.5, bf16[2,128,512]{2,1,0:T(8,128)(2,1)} %copy-done.9, bf16[2,128,512]{2,1,0:T(8,128)(2,1)} %copy-done.10, ...), custom_call_target="tpu_custom_call" | custom-call | flops 2415919104 | bytes 8388608 | tf_op jit(solution)/shard_map/correlate/pallas_call | solution.py:115
  102.7 0.0 collective-permute-done.11.three
  102.8 2.8 %collective-permute-start.1 = (bf16[2,128,512]{2,1,0:T(8,128)(2,1)S(1)}, bf16[2,128,512]{2,1,0:T(8,128)(2,1)S(1)}, u32[]{:S(2)}, u32[]{:S(2)}) collective-permute-start(bf16[2,128,512]{2,1,0:T(8,128)(2,1)S(1)} %get-tuple-element.39), channel_id=1, source_target_pairs={{0,24},{1,25},{2,26},{3,27},{4,28},{5,29},{6,30},{7,31},{8,0},{9,1... | collective-permute-start | bytes 786440 | tf_op jit(solution)/shard_map/ppermute | solution.py:189
  105.5 1.6 collective-permute-start.2
  107.2 1.1 collective-permute-start.3
  108.3 7.0 %correlate.5.acc = f32[1024,512]{1,0:T(8,128)} custom-call(bf16[1024,128]{1,0:T(8,128)(2,1)} %fusion.14.first, bf16[1024,512]{1,0:T(8,128)(2,1)} %fusion.9.second, bf16[2,128,512]{2,1,0:T(8,128)(2,1)} %copy-done.4, bf16[2,128,512]{2,1,0:T(8,128)(2,1)} %collective-permute-done.9.one, bf16[2,128,512]{2,1,0:T(8,128)(2,1)} %copy-done.11, ...), custom_call_target="tpu_custom_call" | custom-call | flops 2415919104 | bytes 8388608 | tf_op jit(solution)/shard_map/correlate/pallas_call | solution.py:115
  115.3 0.0 collective-permute-done.6.two
  115.3 0.0 collective-permute-done.7.three
  115.3 0.7 copy-done.14
  116.0 0.1 copy-done.16
  116.1 7.0 %correlate.6.acc = f32[1024,512]{1,0:T(8,128)} custom-call(bf16[1024,128]{1,0:T(8,128)(2,1)} %fusion.14.first, bf16[1024,512]{1,0:T(8,128)(2,1)} %fusion.9.second, bf16[2,128,512]{2,1,0:T(8,128)(2,1)} %copy-done.3, bf16[2,128,512]{2,1,0:T(8,128)(2,1)} %collective-permute-done.5.one, bf16[2,128,512]{2,1,0:T(8,128)(2,1)} %copy-done.14, ...), custom_call_target="tpu_custom_call" | custom-call | flops 2415919104 | bytes 8388608 | tf_op jit(solution)/shard_map/correlate/pallas_call | solution.py:115
  123.1 0.0 collective-permute-done.3.three
  123.1 0.6 copy-done.13
  123.8 0.1 copy-done.15
  123.9 0.1 copy-done.17
  124.0 6.9 %correlate.7 = (f32[1024,256]{1,0:T(8,128)}, bf16[1024,256]{1,0:T(8,128)(2,1)}) custom-call(bf16[1024,128]{1,0:T(8,128)(2,1)} %fusion.14.first, bf16[1024,512]{1,0:T(8,128)(2,1)} %fusion.9.second, bf16[2,128,512]{2,1,0:T(8,128)(2,1)} %copy-done.2, bf16[2,128,512]{2,1,0:T(8,128)(2,1)} %copy-done.13, bf16[2,128,512]{2,1,0:T(8,128)(2,1)} %copy-done.15, ...), custom_call_target="tpu_custom_call" | custom-call | flops 2415919104 | bytes 8388608 | tf_op jit(solution)/shard_map/correlate/pallas_call | solution.py:115
  130.9 0.1 broadcast_add_fusion
  131.1 2.0 %collective-permute-done.16.received = bf16[1024,256]{1,0:T(8,128)(2,1)S(1)} collective-permute-done((bf16[1024,256]{1,0:T(8,128)(2,1)}, bf16[1024,256]{1,0:T(8,128)(2,1)S(1)}, u32[]{:S(2)}, u32[]{:S(2)}) %collective-permute-start.16) | collective-permute-done | bytes 524320 | tf_op jit(solution)/shard_map/ppermute | solution.py:202
  133.0 1.2 copy-done
  134.2 0.2 split_kernel.1
  134.5 0.7 collective-permute-start.17
  135.2 1.8 %collective-permute-start.18 = (bf16[512,128]{1,0:T(8,128)(2,1)S(1)}, bf16[512,128]{1,0:T(8,128)(2,1)S(1)}, u32[]{:S(2)}, u32[]{:S(2)}) collective-permute-start(bf16[512,128]{1,0:T(8,128)(2,1)S(1)} %get-tuple-element.15), channel_id=1, source_target_pairs={{0,4},{1,5},{2,6},{3,7},{4,0},{5,1},{6,2},{7,3},{8,12},{9,13},{10,... | collective-permute-start | bytes 393224 | tf_op jit(solution)/shard_map/ppermute | solution.py:210
  137.0 1.1 collective-permute-start.19
  138.1 2.1 %fusion.hot = bf16[2048,1024]{1,0:T(8,128)(2,1)S(1)} fusion(s32[1024]{0:T(1024)S(1)} %add_select_fusion.1), kind=kLoop, calls=%fused_computation.1 | loop fusion | flops 4194304 | bytes 4198400 | tf_op jit(solution)/shard_map/convert_element_type | solution.py:180
  140.2 0.8 collective-permute-done.17.one
  140.9 5.6 %collective-permute-done.18.two = bf16[512,128]{1,0:T(8,128)(2,1)S(1)} collective-permute-done((bf16[512,128]{1,0:T(8,128)(2,1)S(1)}, bf16[512,128]{1,0:T(8,128)(2,1)S(1)}, u32[]{:S(2)}, u32[]{:S(2)}) %collective-permute-start.18) | collective-permute-done | bytes 131104 | tf_op jit(solution)/shard_map/ppermute | solution.py:210
  146.5 3.3 %collective-permute-done.19.three = bf16[512,128]{1,0:T(8,128)(2,1)S(1)} collective-permute-done((bf16[512,128]{1,0:T(8,128)(2,1)S(1)}, bf16[512,128]{1,0:T(8,128)(2,1)S(1)}, u32[]{:S(2)}, u32[]{:S(2)}) %collective-permute-start.19) | collective-permute-done | bytes 131104 | tf_op jit(solution)/shard_map/ppermute | solution.py:210
  149.8 1.4 route_kernel.1
  151.2 20.1 %all_to_all.5.routed = bf16[32,32,128]{2,1,0:T(8,128)(2,1)S(1)} all-to-all(bf16[32,32,128]{2,1,0:T(8,128)(2,1)S(1)} %route_kernel.1), channel_id=1, replica_groups=mesh['chan'=32,'win'=8] {'chan'}, dimensions={0} | all-to-all | bytes 524288 | tf_op jit(solution)/shard_map/all_to_all | solution.py:214
  171.3 1.1 unpack_kernel.1
  (43 shorter events, 0.2 us)
Async XLA Ops:
  3.4 43.3 %copy-start.7 = (s32[1,1024]{1,0:T(1,128)S(1)}, s32[1,1024]{1,0:T(1,128)}, u32[]{:S(2)}) copy-start(s32[1,1024]{1,0:T(1,128)} %param.7) | copy-start | bytes 12292
  3.4 29.4 %copy-start.5 = (bf16[2,128,512]{2,1,0:T(8,128)(2,1)}, bf16[2,128,512]{2,1,0:T(8,128)(2,1)S(1)}, u32[]{:S(2)}) copy-start(bf16[2,128,512]{2,1,0:T(8,128)(2,1)S(1)} %slice.51.own) | copy-start | bytes 786436
  3.4 29.4 %collective-permute-start.12 = (bf16[2,128,512]{2,1,0:T(8,128)(2,1)S(1)}, bf16[2,128,512]{2,1,0:T(8,128)(2,1)}, u32[]{:S(2)}, u32[]{:S(2)}) collective-permute-start(bf16[2,128,512]{2,1,0:T(8,128)(2,1)S(1)} %slice.51.own), channel_id=1, source_target_pairs={{0,224},{1,225},{2,226},{3,227},{4,228},{5,229},{6,230},{7,231},{8... | collective-permute-start | bytes 786440 | tf_op jit(solution)/shard_map/ppermute | solution.py:171
  32.9 15.0 %copy-start.1 = (bf16[1,2048,512]{2,1,0:T(8,128)(2,1)S(1)}, bf16[1,2048,512]{2,1,0:T(8,128)(2,1)}, u32[]{:S(2)}) copy-start(bf16[1,2048,512]{2,1,0:T(8,128)(2,1)} %get-tuple-element.43) | copy-start | bytes 6291460
  34.8 15.4 %copy-start.2 = (bf16[2,128,512]{2,1,0:T(8,128)(2,1)}, bf16[2,128,512]{2,1,0:T(8,128)(2,1)S(1)}, u32[]{:S(2)}) copy-start(bf16[2,128,512]{2,1,0:T(8,128)(2,1)S(1)} %get-tuple-element.35.own) | copy-start | bytes 786436
  34.8 15.4 %copy-start.3 = (bf16[2,128,512]{2,1,0:T(8,128)(2,1)}, bf16[2,128,512]{2,1,0:T(8,128)(2,1)S(1)}, u32[]{:S(2)}) copy-start(bf16[2,128,512]{2,1,0:T(8,128)(2,1)S(1)} %get-tuple-element.34.own) | copy-start | bytes 786436
  34.8 15.4 %copy-start.4 = (bf16[2,128,512]{2,1,0:T(8,128)(2,1)}, bf16[2,128,512]{2,1,0:T(8,128)(2,1)S(1)}, u32[]{:S(2)}) copy-start(bf16[2,128,512]{2,1,0:T(8,128)(2,1)S(1)} %get-tuple-element.33.own) | copy-start | bytes 786436
  34.8 24.5 %collective-permute-start = (bf16[2,128,512]{2,1,0:T(8,128)(2,1)S(1)}, bf16[2,128,512]{2,1,0:T(8,128)(2,1)S(1)}, u32[]{:S(2)}, u32[]{:S(2)}) collective-permute-start(bf16[2,128,512]{2,1,0:T(8,128)(2,1)S(1)} %get-tuple-element.35.own), channel_id=1, source_target_pairs={{0,224},{1,225},{2,226},{3,227},{4,228},{5,229},{6,230},{7,231},{8... | collective-permute-start | bytes 786440 | tf_op jit(solution)/shard_map/ppermute | solution.py:171
  37.5 34.7 %collective-permute-start.4 = (bf16[2,128,512]{2,1,0:T(8,128)(2,1)S(1)}, bf16[2,128,512]{2,1,0:T(8,128)(2,1)S(1)}, u32[]{:S(2)}, u32[]{:S(2)}) collective-permute-start(bf16[2,128,512]{2,1,0:T(8,128)(2,1)S(1)} %get-tuple-element.34.own), channel_id=1, source_target_pairs={{0,224},{1,225},{2,226},{3,227},{4,228},{5,229},{6,230},{7,231},{8... | collective-permute-start | bytes 786440 | tf_op jit(solution)/shard_map/ppermute | solution.py:171
  44.7 31.7 %collective-permute-start.8 = (bf16[2,128,512]{2,1,0:T(8,128)(2,1)S(1)}, bf16[2,128,512]{2,1,0:T(8,128)(2,1)S(1)}, u32[]{:S(2)}, u32[]{:S(2)}) collective-permute-start(bf16[2,128,512]{2,1,0:T(8,128)(2,1)S(1)} %get-tuple-element.33.own), channel_id=1, source_target_pairs={{0,224},{1,225},{2,226},{3,227},{4,228},{5,229},{6,230},{7,231},{8... | collective-permute-start | bytes 786440 | tf_op jit(solution)/shard_map/ppermute | solution.py:171
  47.9 31.9 %copy-start.8 = (s32[1,1024]{1,0:T(1,128)S(1)}, s32[1,1024]{1,0:T(1,128)}, u32[]{:S(2)}) copy-start(s32[1,1024]{1,0:T(1,128)} %param.6) | copy-start | bytes 12292
  50.2 34.4 %copy-start.6 = (s32[1,1024,1]{1,2,0:T(1,128)S(1)}, s32[1,1024,1]{1,2,0:T(1,128)}, u32[]{:S(2)}) copy-start(s32[1,1024,1]{1,2,0:T(1,128)} %param.9) | copy-start | bytes 12292
  50.2 30.4 %collective-permute-start.13 = (bf16[2,128,512]{2,1,0:T(8,128)(2,1)S(1)}, bf16[2,128,512]{2,1,0:T(8,128)(2,1)S(1)}, u32[]{:S(2)}, u32[]{:S(2)}) collective-permute-start(bf16[2,128,512]{2,1,0:T(8,128)(2,1)S(1)} %get-tuple-element.23), channel_id=1, source_target_pairs={{0,24},{1,25},{2,26},{3,27},{4,28},{5,29},{6,30},{7,31},{8,0},{9,1... | collective-permute-start | bytes 786440 | tf_op jit(solution)/shard_map/ppermute | solution.py:189
  50.3 33.6 %collective-permute-start.14 = (bf16[2,128,512]{2,1,0:T(8,128)(2,1)S(1)}, bf16[2,128,512]{2,1,0:T(8,128)(2,1)S(1)}, u32[]{:S(2)}, u32[]{:S(2)}) collective-permute-start(bf16[2,128,512]{2,1,0:T(8,128)(2,1)S(1)} %get-tuple-element.22), channel_id=1, source_target_pairs={{0,16},{1,17},{2,18},{3,19},{4,20},{5,21},{6,22},{7,23},{8,24},{9,... | collective-permute-start | bytes 786440 | tf_op jit(solution)/shard_map/ppermute | solution.py:189
  59.3 35.4 %collective-permute-start.15 = (bf16[2,128,512]{2,1,0:T(8,128)(2,1)}, bf16[2,128,512]{2,1,0:T(8,128)(2,1)}, u32[]{:S(2)}, u32[]{:S(2)}) collective-permute-start(bf16[2,128,512]{2,1,0:T(8,128)(2,1)} %get-tuple-element.21), channel_id=1, source_target_pairs={{0,8},{1,9},{2,10},{3,11},{4,12},{5,13},{6,14},{7,15},{8,16},{9,17... | collective-permute-start | bytes 786440 | tf_op jit(solution)/shard_map/ppermute | solution.py:189
  76.6 18.4 %collective-permute-start.10 = (bf16[2,128,512]{2,1,0:T(8,128)(2,1)S(1)}, bf16[2,128,512]{2,1,0:T(8,128)(2,1)S(1)}, u32[]{:S(2)}, u32[]{:S(2)}) collective-permute-start(bf16[2,128,512]{2,1,0:T(8,128)(2,1)S(1)} %get-tuple-element.25), channel_id=1, source_target_pairs={{0,16},{1,17},{2,18},{3,19},{4,20},{5,21},{6,22},{7,23},{8,24},{9,... | collective-permute-start | bytes 786440 | tf_op jit(solution)/shard_map/ppermute | solution.py:189
  80.7 22.1 %collective-permute-start.11 = (bf16[2,128,512]{2,1,0:T(8,128)(2,1)S(1)}, bf16[2,128,512]{2,1,0:T(8,128)(2,1)S(1)}, u32[]{:S(2)}, u32[]{:S(2)}) collective-permute-start(bf16[2,128,512]{2,1,0:T(8,128)(2,1)S(1)} %get-tuple-element.24), channel_id=1, source_target_pairs={{0,8},{1,9},{2,10},{3,11},{4,12},{5,13},{6,14},{7,15},{8,16},{9,17... | collective-permute-start | bytes 786440 | tf_op jit(solution)/shard_map/ppermute | solution.py:189
  80.7 3.3 %copy-start.9 = (bf16[2,128,512]{2,1,0:T(8,128)(2,1)}, bf16[2,128,512]{2,1,0:T(8,128)(2,1)S(1)}, u32[]{:S(2)}) copy-start(bf16[2,128,512]{2,1,0:T(8,128)(2,1)S(1)} %collective-permute-done.13.one) | copy-start | bytes 786436
  80.7 24.8 %collective-permute-start.9 = (bf16[2,128,512]{2,1,0:T(8,128)(2,1)S(1)}, bf16[2,128,512]{2,1,0:T(8,128)(2,1)}, u32[]{:S(2)}, u32[]{:S(2)}) collective-permute-start(bf16[2,128,512]{2,1,0:T(8,128)(2,1)S(1)} %get-tuple-element.26), channel_id=1, source_target_pairs={{0,24},{1,25},{2,26},{3,27},{4,28},{5,29},{6,30},{7,31},{8,0},{9,1... | collective-permute-start | bytes 786440 | tf_op jit(solution)/shard_map/ppermute | solution.py:189
  83.9 0.7 copy-start.10
  83.9 23.3 %collective-permute-start.5 = (bf16[2,128,512]{2,1,0:T(8,128)(2,1)S(1)}, bf16[2,128,512]{2,1,0:T(8,128)(2,1)}, u32[]{:S(2)}, u32[]{:S(2)}) collective-permute-start(bf16[2,128,512]{2,1,0:T(8,128)(2,1)S(1)} %get-tuple-element.36), channel_id=1, source_target_pairs={{0,24},{1,25},{2,26},{3,27},{4,28},{5,29},{6,30},{7,31},{8,0},{9,1... | collective-permute-start | bytes 786440 | tf_op jit(solution)/shard_map/ppermute | solution.py:189
  94.7 20.6 %collective-permute-start.6 = (bf16[2,128,512]{2,1,0:T(8,128)(2,1)S(1)}, bf16[2,128,512]{2,1,0:T(8,128)(2,1)S(1)}, u32[]{:S(2)}, u32[]{:S(2)}) collective-permute-start(bf16[2,128,512]{2,1,0:T(8,128)(2,1)S(1)} %get-tuple-element.37), channel_id=1, source_target_pairs={{0,16},{1,17},{2,18},{3,19},{4,20},{5,21},{6,22},{7,23},{8,24},{9,... | collective-permute-start | bytes 786440 | tf_op jit(solution)/shard_map/ppermute | solution.py:189
  95.0 7.8 %copy-start.11 = (bf16[2,128,512]{2,1,0:T(8,128)(2,1)}, bf16[2,128,512]{2,1,0:T(8,128)(2,1)S(1)}, u32[]{:S(2)}) copy-start(bf16[2,128,512]{2,1,0:T(8,128)(2,1)S(1)} %collective-permute-done.10.two) | copy-start | bytes 786436
  95.0 20.3 %collective-permute-start.7 = (bf16[2,128,512]{2,1,0:T(8,128)(2,1)S(1)}, bf16[2,128,512]{2,1,0:T(8,128)(2,1)S(1)}, u32[]{:S(2)}, u32[]{:S(2)}) collective-permute-start(bf16[2,128,512]{2,1,0:T(8,128)(2,1)S(1)} %get-tuple-element.38), channel_id=1, source_target_pairs={{0,8},{1,9},{2,10},{3,11},{4,12},{5,13},{6,14},{7,15},{8,16},{9,17... | collective-permute-start | bytes 786440 | tf_op jit(solution)/shard_map/ppermute | solution.py:189
  102.7 5.5 %copy-start.12 = (bf16[2,128,512]{2,1,0:T(8,128)(2,1)}, bf16[2,128,512]{2,1,0:T(8,128)(2,1)S(1)}, u32[]{:S(2)}) copy-start(bf16[2,128,512]{2,1,0:T(8,128)(2,1)S(1)} %collective-permute-done.11.three) | copy-start | bytes 786436
  102.8 20.3 %collective-permute-start.1 = (bf16[2,128,512]{2,1,0:T(8,128)(2,1)S(1)}, bf16[2,128,512]{2,1,0:T(8,128)(2,1)S(1)}, u32[]{:S(2)}, u32[]{:S(2)}) collective-permute-start(bf16[2,128,512]{2,1,0:T(8,128)(2,1)S(1)} %get-tuple-element.39), channel_id=1, source_target_pairs={{0,24},{1,25},{2,26},{3,27},{4,28},{5,29},{6,30},{7,31},{8,0},{9,1... | collective-permute-start | bytes 786440 | tf_op jit(solution)/shard_map/ppermute | solution.py:189
  105.5 17.6 %collective-permute-start.2 = (bf16[2,128,512]{2,1,0:T(8,128)(2,1)S(1)}, bf16[2,128,512]{2,1,0:T(8,128)(2,1)S(1)}, u32[]{:S(2)}, u32[]{:S(2)}) collective-permute-start(bf16[2,128,512]{2,1,0:T(8,128)(2,1)S(1)} %get-tuple-element.40), channel_id=1, source_target_pairs={{0,16},{1,17},{2,18},{3,19},{4,20},{5,21},{6,22},{7,23},{8,24},{9,... | collective-permute-start | bytes 786440 | tf_op jit(solution)/shard_map/ppermute | solution.py:189
  107.2 15.9 %collective-permute-start.3 = (bf16[2,128,512]{2,1,0:T(8,128)(2,1)S(1)}, bf16[2,128,512]{2,1,0:T(8,128)(2,1)S(1)}, u32[]{:S(2)}, u32[]{:S(2)}) collective-permute-start(bf16[2,128,512]{2,1,0:T(8,128)(2,1)S(1)} %get-tuple-element.41), channel_id=1, source_target_pairs={{0,8},{1,9},{2,10},{3,11},{4,12},{5,13},{6,14},{7,15},{8,16},{9,17... | collective-permute-start | bytes 786440 | tf_op jit(solution)/shard_map/ppermute | solution.py:189
  115.3 0.7 copy-start.14
  115.3 0.8 copy-start.16
  123.1 0.7 copy-start.13
  123.1 0.8 copy-start.15
  123.1 0.9 copy-start.17
  130.9 2.1 %collective-permute-start.16 = (bf16[1024,256]{1,0:T(8,128)(2,1)}, bf16[1024,256]{1,0:T(8,128)(2,1)S(1)}, u32[]{:S(2)}, u32[]{:S(2)}) collective-permute-start(bf16[1024,256]{1,0:T(8,128)(2,1)} %get-tuple-element.12), channel_id=1, source_target_pairs={{0,1},{1,0},{2,3},{3,2},{4,5},{5,4},{6,7},{7,6},{8,9},{9,8},{10,11... | collective-permute-start | bytes 1572872 | tf_op jit(solution)/shard_map/ppermute | solution.py:202
  133.0 1.2 copy-start
  134.5 6.4 %collective-permute-start.17 = (bf16[512,128]{1,0:T(8,128)(2,1)S(1)}, bf16[512,128]{1,0:T(8,128)(2,1)S(1)}, u32[]{:S(2)}, u32[]{:S(2)}) collective-permute-start(bf16[512,128]{1,0:T(8,128)(2,1)S(1)} %get-tuple-element.14), channel_id=1, source_target_pairs={{0,2},{1,3},{2,0},{3,1},{4,6},{5,7},{6,4},{7,5},{8,10},{9,11},{10,... | collective-permute-start | bytes 393224 | tf_op jit(solution)/shard_map/ppermute | solution.py:210
  135.2 11.3 %collective-permute-start.18 = (bf16[512,128]{1,0:T(8,128)(2,1)S(1)}, bf16[512,128]{1,0:T(8,128)(2,1)S(1)}, u32[]{:S(2)}, u32[]{:S(2)}) collective-permute-start(bf16[512,128]{1,0:T(8,128)(2,1)S(1)} %get-tuple-element.15), channel_id=1, source_target_pairs={{0,4},{1,5},{2,6},{3,7},{4,0},{5,1},{6,2},{7,3},{8,12},{9,13},{10,... | collective-permute-start | bytes 393224 | tf_op jit(solution)/shard_map/ppermute | solution.py:210
  137.0 12.8 %collective-permute-start.19 = (bf16[512,128]{1,0:T(8,128)(2,1)S(1)}, bf16[512,128]{1,0:T(8,128)(2,1)S(1)}, u32[]{:S(2)}, u32[]{:S(2)}) collective-permute-start(bf16[512,128]{1,0:T(8,128)(2,1)S(1)} %get-tuple-element.16), channel_id=1, source_target_pairs={{0,6},{1,7},{2,4},{3,5},{4,2},{5,3},{6,0},{7,1},{8,14},{9,15},{10,... | collective-permute-start | bytes 393224 | tf_op jit(solution)/shard_map/ppermute | solution.py:210

commit v2 on v1

--- a/solution.py
+++ b/solution.py
@@ -11,6 +11,8 @@
 LAGS = 512
 REACH = 3
 CHUNKS = 4
+FIRST_DONE = False
+CHOOSE_COST = (5_000_000_000,) * 4
 ROWS = 256
 AXES = ("chan", "win")
 N_X = 4
@@ -43,13 +45,22 @@
     column = jnp.arange(LAGS, dtype=jnp.int32)
     half, block, inner = column // 256, column // 64 % 4, column % 64
     lag = ((z ^ block) * N_CORE + (core ^ half)) * 64 + inner - LAGS // 2
-    freq_index = jnp.arange(bins, dtype=jnp.int32)
-    phase_index = freq_index[:, None] * lag[None, :] % (2 * bins)
-    angles = phase_index.astype(jnp.float32) * (math.pi / bins)
-    weights = jnp.where(freq_index == 0, 1.0, 2.0).astype(jnp.float32)[:, None] / math.sqrt(
-        bins * windows
-    )
-    return jnp.stack([weights * jnp.cos(angles), -weights * jnp.sin(angles)], 0).astype(jnp.bfloat16)
+
+    def turns(freq_index):
+        phase_index = freq_index[:, None] * lag[None, :] % (2 * bins)
+        angles = phase_index.astype(jnp.float32) * (math.pi / bins)
+        return jnp.cos(angles), jnp.sin(angles)
+
+    few = 32
+    low_cos, low_sin = turns(jnp.arange(few, dtype=jnp.int32))
+    high_cos, high_sin = turns(jnp.arange(0, bins, few, dtype=jnp.int32))
+    low_cos, low_sin = low_cos[None], low_sin[None]
+    high_cos, high_sin = high_cos[:, None], high_sin[:, None]
+    weights = jnp.where(jnp.arange(bins, dtype=jnp.int32) == 0, 1.0, 2.0).astype(jnp.float32)
+    weights = weights.reshape(bins // few, few, 1) / math.sqrt(bins * windows)
+    cosine = weights * (high_cos * low_cos - high_sin * low_sin)
+    sine = -weights * (high_sin * low_cos + high_cos * low_sin)
+    return [part.astype(jnp.bfloat16).reshape(bins, LAGS) for part in (cosine, sine)]
 
 
 def whiten(spectra):
@@ -62,46 +73,47 @@
     return lax.dot_general(a, b, (((1,), (0,)), ((), ())), preferred_element_type=jnp.float32)
 
 
-def correlate(bins, first_ref, second_ref, own_ref, one_ref, two_ref, three_ref, table_ref, acc):
+def correlate(first_ref, second_ref, halo, cos_ref, sin_ref, acc, blocks):
+    @pl.when(pl.program_id(0) == 0)
+    def _():
+        for d, ref in enumerate(halo):
+            blocks[:, 128 * d : 128 * (d + 1)] = ref[...]
+
     left_hot = first_ref[...]
     right_hot = second_ref[...]
+    bins = blocks.shape[2]
     step = min(512, bins)
     for start in range(0, bins, step):
         at = pl.ds(start, step)
-        left = [dot(left_hot, own_ref[part, :, at]) for part in range(2)]
-        right = [
-            dot(
-                right_hot,
-                jnp.concatenate(
-                    [ref[part, :, at] for ref in (own_ref, one_ref, two_ref, three_ref)], 0
-                ),
-            )
-            for part in range(2)
-        ]
+        left = [dot(left_hot, blocks[part, :128, at]) for part in range(2)]
+        right = [dot(right_hot, blocks[part, :, at]) for part in range(2)]
         real = (left[0] * right[0] + left[1] * right[1]).astype(jnp.bfloat16)
         imag = (left[1] * right[0] - left[0] * right[1]).astype(jnp.bfloat16)
-        part = dot(real, table_ref[0, at, :]) + dot(imag, table_ref[1, at, :])
+        part = dot(real, cos_ref[at, :]) + dot(imag, sin_ref[at, :])
         acc = part if acc is None else acc + part
     return acc
 
 
-def first_kernel(bins, first, second, own, one, two, three, table, out):
-    out[...] = correlate(bins, first, second, own, one, two, three, table, None)
-
-
-def next_kernel(bins, first, second, own, one, two, three, table, acc, out):
-    out[...] = correlate(bins, first, second, own, one, two, three, table, acc[...])
-
-
-def last_kernel(bins, first, second, own, one, two, three, table, acc, keep, send):
-    total = correlate(bins, first, second, own, one, two, three, table, acc[...])
+def first_kernel(first, second, *rest):
+    *halo, cosine, sine, out, blocks = rest
+    out[...] = correlate(first, second, halo, cosine, sine, None, blocks)
+
+
+def next_kernel(first, second, *rest):
+    *halo, cosine, sine, acc, out, blocks = rest
+    out[...] = correlate(first, second, halo, cosine, sine, acc[...], blocks)
+
+
+def last_kernel(first, second, *rest):
+    *halo, cosine, sine, acc, keep, send, blocks = rest
+    total = correlate(first, second, halo, cosine, sine, acc[...], blocks)
     keep[...] = total[:, :256]
     send[...] = total[:, 256:].astype(jnp.bfloat16)
 
 
-def run_chunk(kernel, first_hot, second_hot, blocks, table, acc, outs):
+def run_chunk(kernel, q, first_hot, second_hot, halo, cosine, sine, acc, outs):
     slots = first_hot.shape[0]
-    bins = blocks[0].shape[2]
+    bins = halo[0].shape[2]
 
     def rows(width):
         return pl.BlockSpec((ROWS, width), lambda i: (i, 0))
@@ -109,21 +121,55 @@
     def whole(shape):
         return pl.BlockSpec(shape, lambda i: (0,) * len(shape))
 
-    operands = [first_hot, second_hot, *blocks, table] + ([] if acc is None else [acc])
-    in_specs = [rows(128), rows(512)] + [whole(b.shape) for b in blocks] + [whole(table.shape)]
+    operands = [first_hot, second_hot, *halo, cosine, sine] + ([] if acc is None else [acc])
+    in_specs = [rows(128), rows(512)]
+    in_specs += [whole(b.shape) for b in halo]
+    in_specs += [pl.BlockSpec((bins, LAGS), lambda i: (q, 0)) for _ in range(2)]
     in_specs += [] if acc is None else [rows(512)]
     return pl.pallas_call(
-        functools.partial(kernel, bins),
+        kernel,
         grid=(slots // ROWS,),
         in_specs=in_specs,
         out_specs=[rows(o.shape[1]) for o in outs],
         out_shape=outs,
-        compiler_params=pltpu.CompilerParams(vmem_limit_bytes=56 << 20),
-        cost_estimate=pl.CostEstimate(
-            flops=2 * slots * 2 * bins * (640 + 512), bytes_accessed=8 << 20, transcendentals=0
-        ),
+        scratch_shapes=[pltpu.VMEM((2, 512, bins), jnp.bfloat16)],
+        compiler_params=pltpu.CompilerParams(vmem_limit_bytes=24 << 20),
+        cost_estimate=pl.CostEstimate(flops=200_000_000, bytes_accessed=1 << 20, transcendentals=0),
         name="correlate",
     )(*operands)
+
+
+def choose_kernel(has_later, place, crossed, own, *rest):
+    outs = rest[-REACH:]
+    if has_later:
+        rest[-REACH - 1][...] = rest[0][...]
+    for d, out in enumerate(outs):
+
+        @pl.when(place[0] <= d)
+        def _():
+            out[...] = crossed[...]
+
+        @pl.when(place[0] > d)
+        def _():
+            out[...] = own[...]
+
+
+def choose(place, crossed, own, later, after, flops):
+    shape = jax.ShapeDtypeStruct(own.shape, own.dtype)
+    held = [crossed, own] + ([] if later is None else [later])
+    vmem = pl.BlockSpec(memory_space=pltpu.VMEM)
+    outs = pl.pallas_call(
+        functools.partial(choose_kernel, later is not None),
+        in_specs=[pl.BlockSpec(memory_space=pltpu.SMEM)]
+        + [vmem] * len(held)
+        + [pl.BlockSpec(memory_space=pl.ANY)] * len(after),
+        out_specs=[vmem] * (REACH + len(held) - 2),
+        out_shape=[shape] * (REACH + len(held) - 2),
+        compiler_params=pltpu.CompilerParams(vmem_limit_bytes=16 << 20),
+        cost_estimate=pl.CostEstimate(flops=flops, bytes_accessed=1 << 20, transcendentals=0),
+        name="choose",
+    )(place[None], *held, *after)
+    return outs[-REACH:], outs[0]
 
 
 def split_kernel(keep, received, *outs):
@@ -155,7 +201,7 @@
     return pl.pallas_call(
         kernel,
         out_shape=out_shape,
-        compiler_params=pltpu.CompilerParams(vmem_limit_bytes=40 << 20),
+        compiler_params=pltpu.CompilerParams(vmem_limit_bytes=24 << 20),
         name=kernel.__name__,
     )(*operands)
 
@@ -168,37 +214,47 @@
     whitened = jnp.swapaxes(whiten(spectra[0]), 0, 1)
     size = bins // CHUNKS
     own = [whitened[:, :, q * size : (q + 1) * size] for q in range(CHUNKS)]
-    crossed = [lax.ppermute(chunk, AXES, CROSS) for chunk in own]
+    crossed = [lax.ppermute(own[q], AXES, CROSS) for q in range(2)]
 
     first_hot = (pair_first[0][:, None] == jnp.arange(128, dtype=jnp.int32)).astype(jnp.bfloat16)
     second_hot = (pair_second[0][:, None] == jnp.arange(512, dtype=jnp.int32)).astype(jnp.bfloat16)
     owners = pair_owner[0, :, 0]
     onehot = (owners[:, None] == jnp.arange(32, dtype=jnp.int32)[None, :]).astype(jnp.int32)
-    before = jnp.cumsum(onehot, axis=0, dtype=jnp.int32) - onehot
+    order = jnp.arange(slots, dtype=jnp.int32)
+    below = (order[None, :] < order[:, None]).astype(jnp.bfloat16)
+    before = dot(below, onehot.astype(jnp.bfloat16)).astype(jnp.int32)
     place = owners * 64 + jnp.sum(before * onehot, axis=1)
-    place = jnp.where(jnp.arange(slots, dtype=jnp.int32) < pair_count[0], place, -1)
+    place = jnp.where(order < pair_count[0], place, -1)
     place_hot = (place[None, :] == jnp.arange(2048, dtype=jnp.int32)[:, None]).astype(jnp.bfloat16)
-    table = lag_table(bins, windows_all)
+    cosine, sine = lag_table(bins, windows_all)
 
     acc = None
+    history = []
     f32 = jnp.float32
     for q in range(CHUNKS):
-        ahead = {}
-        for d in (2, 1, 3):
-            source = jnp.where(x_place < d, crossed[q], own[q])
-            ahead[d] = lax.ppermute(source, AXES, AROUND[d])
-        blocks = [own[q], ahead[1], ahead[2], ahead[3]]
-        part = table[:, q * size : (q + 1) * size]
+        after = []
+        if q >= 2:
+            after += [history[q - 2][d] for d in (1, 2, 3)]
+        if q >= 1 and FIRST_DONE:
+            after += [history[q - 1][2]]
+        later = own[q + 2] if q + 2 < CHUNKS else None
+        sources, copied = choose(x_place, crossed[q], own[q], later, after, CHOOSE_COST[q])
+        if later is not None:
+            crossed.append(lax.ppermute(copied, AXES, CROSS))
+        ahead = {d: lax.ppermute(sources[d - 1], AXES, AROUND[d]) for d in (2, 1, 3)}
+        history.append(ahead)
+        halo = [own[q], ahead[1], ahead[2], ahead[3]]
+        operands = (q, first_hot, second_hot, halo, cosine, sine, acc)
         whole = jax.ShapeDtypeStruct((slots, LAGS), f32)
         if q == CHUNKS - 1:
             outs = [
                 jax.ShapeDtypeStruct((slots, 256), f32),
                 jax.ShapeDtypeStruct((slots, 256), jnp.bfloat16),
             ]
-            keep, send = run_chunk(last_kernel, first_hot, second_hot, blocks, part, acc, outs)
+            keep, send = run_chunk(last_kernel, *operands, outs)
         else:
             kernel = first_kernel if q == 0 else next_kernel
-            (acc,) = run_chunk(kernel, first_hot, second_hot, blocks, part, acc, [whole])
+            (acc,) = run_chunk(kernel, *operands, [whole])
     received = lax.ppermute(send, AXES, OTHER_CORE)
     packed = (slots // 2, 128)
     pieces = call(

time: 173 us -> 132 us (0.76)
  other arithmetic: 40 us -> 10.2 us
  waiting for transfers between devices: 32.6 us -> 21.5 us
  starting transfers between devices: 44.7 us -> 54.9 us
  Pallas kernels: 30.2 us -> 20.3 us
  local copies, waits for them, and re-layouts: 3.85 us -> 0.18 us
  blocking collectives: 20.1 us -> 22.9 us
    another operation x5 -> x0, other arithmetic: 30.2 us -> none
    ppermute x16, waiting for transfers between devices: 21.1 us -> 10.9 us  [the longest x2 6.34 us: on_device(): crossed = [lax.ppermute(own[q], AXES, CROSS) for q in range(2)]]
    pallas_call x4 -> x8, Pallas kernels: 27.4 us -> 17.5 us  [the longest x4 16.2 us: run_chunk(): pl.pallas_call(kernel, grid=(slots // ROWS,), in_specs=in_specs, out_spec...]
    ppermute x16, starting transfers between devices: 41.1 us -> 49.7 us  [the longest x2 22.6 us: on_device(): crossed.append(lax.ppermute(copied, AXES, CROSS))]
    unnamed x36 -> x8, local copies, waits for them, and re-layouts: 3.54 us -> 0.02 us
    all_to_all x1, blocking collectives: 20.1 us -> 22.9 us  [on_device(): lax.all_to_all(buffer, 'chan', split_axis=0, concat_axis=0, tiled=True)]
    convert_element_type x1, other arithmetic: 0.01 us -> 2.24 us  [lag_table(): part.astype(jnp.bfloat16).reshape(bins, LAGS)]
    select_n x3 -> x1, other arithmetic: 2.11 us -> 0.01 us  [on_device(): place = jnp.where(order < pair_count[0], place, -1)]
  transfers between devices with their start and end apart: 20 -> 20, of which waited for: 7 -> 7; matrix products, arithmetic and copies ran while one was open for 20% -> 6% of each run, Pallas kernels for 12% -> 10%
where the time goes in v2:
time: 132 us
  starting transfers between devices  54.9 us (42%)
  blocking collectives  22.9 us (17%)
  waiting for transfers between devices  21.5 us (16%)
  Pallas kernels  20.3 us (15%)
  other arithmetic  10.2 us (8%)
    all_to_all x1, blocking collectives, on_device(): lax.all_to_all(buffer, 'chan', split_axis=0, concat_axis=0, tiled=True)  22.9 us
    ppermute x2, starting transfers between devices, on_device(): crossed.append(lax.ppermute(copied, AXES, CROSS))  22.6 us
    pallas_call x4, Pallas kernels, run_chunk(): pl.pallas_call(kernel, grid=(slots // ROWS,), in_specs=in_specs, out_spec...  16.2 us
    ppermute x12, starting transfers between devices, on_device(): lax.ppermute(sources[d - 1], AXES, AROUND[d])  14.6 us
    ppermute x2, starting transfers between devices, on_device(): crossed = [lax.ppermute(own[q], AXES, CROSS) for q in range(2)]  12.6 us
    ppermute x3, waiting for transfers between devices, on_device(): arrived = [lax.ppermute(pieces[k], AXES, OTHER_CHIP[k]) for k in (1, 2, 3)]  9.89 us
    ppermute x2, waiting for transfers between devices, on_device(): crossed = [lax.ppermute(own[q], AXES, CROSS) for q in range(2)]  6.34 us
    ppermute x3, starting transfers between devices, on_device(): arrived = [lax.ppermute(pieces[k], AXES, OTHER_CHIP[k]) for k in (1, 2, 3)]  5.11 us
  transfers between devices with their start and end apart: 20, of which 7 were waited for; matrix products, arithmetic and copies ran while one was open for 6% of the time, Pallas kernels for 10%

profile of v2, /device:TPU:32, one launch (start us, length us, event | category | flops | bytes accessed | tf_op | source)
XLA Modules:
  0.0 131.6 jit_solution(6907317964122605103)
XLA Ops:
  0.0 1.7 %fusion.4 = f32[128]{0:T(128)S(1)} fusion(bf16[1,128,2,2048]{3,2,1,0:T(2,128)(2,1)} %param.5), kind=kLoop, calls=%fused_computation.12 | loop fusion | flops 1572736 | bytes 1049088 | tf_op jit(solution)/shard_map/reduce_sum | solution.py:68
  1.7 1.7 %fusion.10 = bf16[2,128,2048]{2,1,0:T(8,128)(2,1)S(1)} fusion(f32[128]{0:T(128)S(1)} %add_rsqrt_fusion, bf16[1,128,2,2048]{3,2,1,0:T(2,128)(2,1)} %param.5), kind=kLoop, calls=%fused_computation.19 | loop fusion | flops 1572864 | bytes 2097664 | tf_op jit(solution)/shard_map/transpose | solution.py:214
  3.4 0.1 fusion.42
  3.5 10.7 %collective-permute-start.8 = (bf16[2,128,512]{2,1,0:T(8,128)(2,1)S(1)}, bf16[2,128,512]{2,1,0:T(8,128)(2,1)}, u32[]{:S(2)}, u32[]{:S(2)}) collective-permute-start(bf16[2,128,512]{2,1,0:T(8,128)(2,1)S(1)} %get-tuple-element.45.own.rest_0_), channel_id=1, source_target_pairs={{0,224},{1,225},{2,226},{3,227},{4,228},{5,229},{6,230},{7,231},{8... | collective-permute-start | bytes 786440 | tf_op jit(solution)/shard_map/ppermute | solution.py:217
  14.1 1.9 %collective-permute-start = (bf16[2,128,512]{2,1,0:T(8,128)(2,1)S(1)}, bf16[2,128,512]{2,1,0:T(8,128)(2,1)S(1)}, u32[]{:S(2)}, u32[]{:S(2)}) collective-permute-start(bf16[2,128,512]{2,1,0:T(8,128)(2,1)S(1)} %get-tuple-element.47.own.rest_0_), channel_id=1, source_target_pairs={{0,224},{1,225},{2,226},{3,227},{4,228},{5,229},{6,230},{7,231},{8... | collective-permute-start | bytes 786440 | tf_op jit(solution)/shard_map/ppermute | solution.py:217
  16.2 0.3 fusion.25
  16.4 0.6 fusion.21
  17.0 0.1 reshape.238
  17.1 1.2 multiply_add_fusion
  18.3 0.0 copy-start.1
  18.3 2.2 %fusion.1 = (bf16[2048,512]{1,0:T(8,128)(2,1)S(1)}, bf16[2048,512]{1,0:T(8,128)(2,1)}) fusion(f32[64,32,512]{2,1,0:T(8,128)S(1)} %get-tuple-element.49, f32[2048]{0:T(1024)S(1)} %neg.8, f32[64,32,512]{2,1,0:T(8,128)S(1)} %get-tuple-element.50, f32[2048]{0:T(1024)S(1)} %reshape.238), kind=kLoop, calls=%fused_computation.3 | loop fusion | flops 4194304 | bytes 12599296 | tf_op jit(solution)/shard_map/convert_element_type | solution.py:63
  20.6 0.2 fusion.6.second
  20.8 6.3 %collective-permute-done.8.crossed = bf16[2,128,512]{2,1,0:T(8,128)(2,1)} collective-permute-done((bf16[2,128,512]{2,1,0:T(8,128)(2,1)S(1)}, bf16[2,128,512]{2,1,0:T(8,128)(2,1)}, u32[]{:S(2)}, u32[]{:S(2)}) %collective-permute-start.8) | collective-permute-done | bytes 262176 | tf_op jit(solution)/shard_map/ppermute | solution.py:217
  27.1 1.0 choose.6
  28.2 0.1 collective-permute-start.10
  28.3 3.5 %collective-permute-start.11 = (bf16[2,128,512]{2,1,0:T(8,128)(2,1)S(1)}, bf16[2,128,512]{2,1,0:T(8,128)(2,1)S(1)}, u32[]{:S(2)}, u32[]{:S(2)}) collective-permute-start(bf16[2,128,512]{2,1,0:T(8,128)(2,1)S(1)} %get-tuple-element.34), channel_id=1, source_target_pairs={{0,16},{1,17},{2,18},{3,19},{4,20},{5,21},{6,22},{7,23},{8,24},{9,... | collective-permute-start | bytes 786440 | tf_op jit(solution)/shard_map/ppermute | solution.py:244
  31.8 0.9 collective-permute-start.12
  32.7 10.7 %collective-permute-start.9 = (bf16[2,128,512]{2,1,0:T(8,128)(2,1)S(1)}, bf16[2,128,512]{2,1,0:T(8,128)(2,1)S(1)}, u32[]{:S(2)}, u32[]{:S(2)}) collective-permute-start(bf16[2,128,512]{2,1,0:T(8,128)(2,1)S(1)} %get-tuple-element.32), channel_id=1, source_target_pairs={{0,224},{1,225},{2,226},{3,227},{4,228},{5,229},{6,230},{7,231},{8... | collective-permute-start | bytes 786440 | tf_op jit(solution)/shard_map/ppermute | solution.py:243
  43.4 0.0 collective-permute-done.crossed
  43.4 0.1 choose.4
  43.5 0.1 collective-permute-start.2
  43.6 0.0 collective-permute-done.10.rest_0_.rest_1_
  43.6 2.0 %collective-permute-start.3 = (bf16[2,128,512]{2,1,0:T(8,128)(2,1)S(1)}, bf16[2,128,512]{2,1,0:T(8,128)(2,1)S(1)}, u32[]{:S(2)}, u32[]{:S(2)}) collective-permute-start(bf16[2,128,512]{2,1,0:T(8,128)(2,1)S(1)} %get-tuple-element.27), channel_id=1, source_target_pairs={{0,16},{1,17},{2,18},{3,19},{4,20},{5,21},{6,22},{7,23},{8,24},{9,... | collective-permute-start | bytes 786440 | tf_op jit(solution)/shard_map/ppermute | solution.py:244
  45.7 0.0 collective-permute-done.11.rest_1_.rest_2_
  45.7 1.1 collective-permute-start.4
  46.8 0.0 collective-permute-done.12.rest_2_.rest_3_
  46.8 11.9 %collective-permute-start.1 = (bf16[2,128,512]{2,1,0:T(8,128)(2,1)S(1)}, bf16[2,128,512]{2,1,0:T(8,128)(2,1)S(1)}, u32[]{:S(2)}, u32[]{:S(2)}) collective-permute-start(bf16[2,128,512]{2,1,0:T(8,128)(2,1)S(1)} %get-tuple-element.25), channel_id=1, source_target_pairs={{0,224},{1,225},{2,226},{3,227},{4,228},{5,229},{6,230},{7,231},{8... | collective-permute-start | bytes 786440 | tf_op jit(solution)/shard_map/ppermute | solution.py:243
  58.7 0.0 collective-permute-done.9.crossed
  58.7 0.1 choose.7
  58.8 0.1 collective-permute-start.13
  58.9 0.0 collective-permute-done.2.rest_0_.rest_1_
  58.9 0.8 collective-permute-start.14
  59.7 0.0 collective-permute-done.3.rest_1_.rest_2_
  59.7 1.3 collective-permute-start.15
  61.0 0.0 collective-permute-done.4.rest_2_.rest_3_
  61.0 2.9 %collective-permute-done.1.crossed = bf16[2,128,512]{2,1,0:T(8,128)(2,1)S(1)} collective-permute-done((bf16[2,128,512]{2,1,0:T(8,128)(2,1)S(1)}, bf16[2,128,512]{2,1,0:T(8,128)(2,1)S(1)}, u32[]{:S(2)}, u32[]{:S(2)}) %collective-permute-start.1) | collective-permute-done | bytes 262176 | tf_op jit(solution)/shard_map/ppermute | solution.py:243
  63.9 0.1 choose.5
  64.0 0.1 collective-permute-start.5
  64.1 2.0 %collective-permute-start.6 = (bf16[2,128,512]{2,1,0:T(8,128)(2,1)S(1)}, bf16[2,128,512]{2,1,0:T(8,128)(2,1)S(1)}, u32[]{:S(2)}, u32[]{:S(2)}) collective-permute-start(bf16[2,128,512]{2,1,0:T(8,128)(2,1)S(1)} %get-tuple-element.30), channel_id=1, source_target_pairs={{0,16},{1,17},{2,18},{3,19},{4,20},{5,21},{6,22},{7,23},{8,24},{9,... | collective-permute-start | bytes 786440 | tf_op jit(solution)/shard_map/ppermute | solution.py:244
  66.1 1.6 %collective-permute-done.13.rest_1_ = bf16[2,128,512]{2,1,0:T(8,128)(2,1)S(1)} collective-permute-done((bf16[2,128,512]{2,1,0:T(8,128)(2,1)S(1)}, bf16[2,128,512]{2,1,0:T(8,128)(2,1)S(1)}, u32[]{:S(2)}, u32[]{:S(2)}) %collective-permute-start.13) | collective-permute-done | bytes 262176 | tf_op jit(solution)/shard_map/ppermute | solution.py:244
  67.7 2.6 %collective-permute-start.7 = (bf16[2,128,512]{2,1,0:T(8,128)(2,1)S(1)}, bf16[2,128,512]{2,1,0:T(8,128)(2,1)S(1)}, u32[]{:S(2)}, u32[]{:S(2)}) collective-permute-start(bf16[2,128,512]{2,1,0:T(8,128)(2,1)S(1)} %get-tuple-element.31), channel_id=1, source_target_pairs={{0,8},{1,9},{2,10},{3,11},{4,12},{5,13},{6,14},{7,15},{8,16},{9,17... | collective-permute-start | bytes 786440 | tf_op jit(solution)/shard_map/ppermute | solution.py:244
  70.3 0.2 fusion.11.first
  70.5 3.9 %correlate.4.rest_6_ = f32[1024,512]{1,0:T(8,128)S(1)} custom-call(bf16[1024,128]{1,0:T(8,128)(2,1)S(1)} %fusion.11.first, bf16[1024,512]{1,0:T(8,128)(2,1)S(1)} %fusion.6.second, bf16[2,128,512]{2,1,0:T(8,128)(2,1)S(1)} %get-tuple-element.45.own.rest_0_, bf16[2,128,512]{2,1,0:T(8,128)(2,1)S(1)} %collective-permute-done.10.rest_0_.rest_1_, ...), custom_call_target="tpu_custom_call" | custom-call | flops 200000000 | bytes 1048576 | tf_op jit(solution)/shard_map/correlate/pallas_call | solution.py:129
  74.4 4.1 %correlate.5.rest_6_ = f32[1024,512]{1,0:T(8,128)S(1)} custom-call(bf16[1024,128]{1,0:T(8,128)(2,1)S(1)} %fusion.11.first, bf16[1024,512]{1,0:T(8,128)(2,1)S(1)} %fusion.6.second, bf16[2,128,512]{2,1,0:T(8,128)(2,1)S(1)} %get-tuple-element.47.own.rest_0_, bf16[2,128,512]{2,1,0:T(8,128)(2,1)S(1)} %collective-permute-done.2.rest_0_.rest_1_, ...), custom_call_target="tpu_custom_call" | custom-call | flops 200000000 | bytes 1048576 | tf_op jit(solution)/shard_map/correlate/pallas_call | solution.py:129
  78.5 0.0 collective-permute-done.14.rest_2_
  78.6 0.0 collective-permute-done.15.rest_3_
  78.6 4.1 %correlate.6.rest_6_ = f32[1024,512]{1,0:T(8,128)S(1)} custom-call(bf16[1024,128]{1,0:T(8,128)(2,1)S(1)} %fusion.11.first, bf16[1024,512]{1,0:T(8,128)(2,1)S(1)} %fusion.6.second, bf16[2,128,512]{2,1,0:T(8,128)(2,1)S(1)} %get-tuple-element.46.rest_0_.own, bf16[2,128,512]{2,1,0:T(8,128)(2,1)S(1)} %collective-permute-done.13.rest_1_, ...), custom_call_target="tpu_custom_call" | custom-call | flops 200000000 | bytes 1048576 | tf_op jit(solution)/shard_map/correlate/pallas_call | solution.py:129
  82.7 0.0 copy-start.3
  82.7 0.0 collective-permute-done.5.rest_1_
  82.7 0.0 collective-permute-done.7.rest_3_
  82.7 4.1 %correlate.7 = (f32[1024,256]{1,0:T(8,128)S(1)}, bf16[1024,256]{1,0:T(8,128)(2,1)S(1)}) custom-call(bf16[1024,128]{1,0:T(8,128)(2,1)S(1)} %fusion.11.first, bf16[1024,512]{1,0:T(8,128)(2,1)S(1)} %fusion.6.second, bf16[2,128,512]{2,1,0:T(8,128)(2,1)S(1)} %get-tuple-element.48.rest_0_.own, bf16[2,128,512]{2,1,0:T(8,128)(2,1)S(1)} %collective-permute-done.5.rest_1_, ...), custom_call_target="tpu_custom_call" | custom-call | flops 200000000 | bytes 1048576 | tf_op jit(solution)/shard_map/correlate/pallas_call | solution.py:129
  86.8 0.1 collective-permute-start.16
  87.5 0.5 fusion.9
  88.1 0.7 collective-permute-done.16.received
  88.8 0.2 split_kernel.1
  89.0 3.5 %collective-permute-start.17 = (bf16[512,128]{1,0:T(8,128)(2,1)S(1)}, bf16[512,128]{1,0:T(8,128)(2,1)S(1)}, u32[]{:S(2)}, u32[]{:S(2)}) collective-permute-start(bf16[512,128]{1,0:T(8,128)(2,1)S(1)} %get-tuple-element.42), channel_id=1, source_target_pairs={{0,2},{1,3},{2,0},{3,1},{4,6},{5,7},{6,4},{7,5},{8,10},{9,11},{10,... | collective-permute-start | bytes 393224 | tf_op jit(solution)/shard_map/ppermute | solution.py:266
  92.6 1.6 %collective-permute-start.19 = (bf16[512,128]{1,0:T(8,128)(2,1)S(1)}, bf16[512,128]{1,0:T(8,128)(2,1)S(1)}, u32[]{:S(2)}, u32[]{:S(2)}) collective-permute-start(bf16[512,128]{1,0:T(8,128)(2,1)S(1)} %get-tuple-element.44), channel_id=1, source_target_pairs={{0,6},{1,7},{2,4},{3,5},{4,2},{5,3},{6,0},{7,1},{8,14},{9,15},{10,... | collective-permute-start | bytes 393224 | tf_op jit(solution)/shard_map/ppermute | solution.py:266
  94.2 2.1 %fusion.hot = bf16[2048,1024]{1,0:T(8,128)(2,1)S(1)} fusion(s32[1024]{0:T(1024)S(1)} %add_select_fusion.2), kind=kLoop, calls=%fused_computation.1 | loop fusion | flops 4194304 | bytes 4198400 | tf_op jit(solution)/shard_map/convert_element_type | solution.py:228
  96.2 0.6 collective-permute-done.17.one
  96.9 5.2 %collective-permute-done.18.two = bf16[512,128]{1,0:T(8,128)(2,1)S(1)} collective-permute-done((bf16[512,128]{1,0:T(8,128)(2,1)S(1)}, bf16[512,128]{1,0:T(8,128)(2,1)S(1)}, u32[]{:S(2)}, u32[]{:S(2)}) %collective-permute-start.18) | collective-permute-done | bytes 131104 | tf_op jit(solution)/shard_map/ppermute | solution.py:266
  102.1 4.1 %collective-permute-done.19.three = bf16[512,128]{1,0:T(8,128)(2,1)S(1)} collective-permute-done((bf16[512,128]{1,0:T(8,128)(2,1)S(1)}, bf16[512,128]{1,0:T(8,128)(2,1)S(1)}, u32[]{:S(2)}, u32[]{:S(2)}) %collective-permute-start.19) | collective-permute-done | bytes 131104 | tf_op jit(solution)/shard_map/ppermute | solution.py:266
  106.1 1.4 %route_kernel.1 = bf16[32,32,128]{2,1,0:T(8,128)(2,1)S(1)} custom-call(bf16[2048,1024]{1,0:T(8,128)(2,1)S(1)} %fusion.hot, f32[512,128]{1,0:T(8,128)S(1)} %get-tuple-element.41.keep, bf16[512,128]{1,0:T(8,128)(2,1)S(1)} %collective-permute-done.17.one, bf16[512,128]{1,0:T(8,128)(2,1)S(1)} %collective-permute-done.18.two, ...), custom_call_target="tpu_custom_call" | custom-call | tf_op jit(solution)/shard_map/route_kernel/pallas_call | solution.py:201
  107.6 22.9 %all_to_all.5.routed = bf16[32,32,128]{2,1,0:T(8,128)(2,1)S(1)} all-to-all(bf16[32,32,128]{2,1,0:T(8,128)(2,1)S(1)} %route_kernel.1), channel_id=1, replica_groups=mesh['chan'=32,'win'=8] {'chan'}, dimensions={0} | all-to-all | bytes 524288 | tf_op jit(solution)/shard_map/all_to_all | solution.py:270
  130.4 1.1 unpack_kernel.1
  (14 shorter events, 0.1 us)
Async XLA Ops:
  3.5 23.6 %collective-permute-start.8 = (bf16[2,128,512]{2,1,0:T(8,128)(2,1)S(1)}, bf16[2,128,512]{2,1,0:T(8,128)(2,1)}, u32[]{:S(2)}, u32[]{:S(2)}) collective-permute-start(bf16[2,128,512]{2,1,0:T(8,128)(2,1)S(1)} %get-tuple-element.45.own.rest_0_), channel_id=1, source_target_pairs={{0,224},{1,225},{2,226},{3,227},{4,228},{5,229},{6,230},{7,231},{8... | collective-permute-start | bytes 786440 | tf_op jit(solution)/shard_map/ppermute | solution.py:217
  14.1 29.3 %collective-permute-start = (bf16[2,128,512]{2,1,0:T(8,128)(2,1)S(1)}, bf16[2,128,512]{2,1,0:T(8,128)(2,1)S(1)}, u32[]{:S(2)}, u32[]{:S(2)}) collective-permute-start(bf16[2,128,512]{2,1,0:T(8,128)(2,1)S(1)} %get-tuple-element.47.own.rest_0_), channel_id=1, source_target_pairs={{0,224},{1,225},{2,226},{3,227},{4,228},{5,229},{6,230},{7,231},{8... | collective-permute-start | bytes 786440 | tf_op jit(solution)/shard_map/ppermute | solution.py:217
  18.3 2.3 %copy-start.1 = (s32[1,1024]{1,0:T(1,128)S(1)}, s32[1,1024]{1,0:T(1,128)}, u32[]{:S(2)}) copy-start(s32[1,1024]{1,0:T(1,128)} %param.7) | copy-start | bytes 12292
  28.2 15.4 %collective-permute-start.10 = (bf16[2,128,512]{2,1,0:T(8,128)(2,1)S(1)}, bf16[2,128,512]{2,1,0:T(8,128)(2,1)S(1)}, u32[]{:S(2)}, u32[]{:S(2)}) collective-permute-start(bf16[2,128,512]{2,1,0:T(8,128)(2,1)S(1)} %get-tuple-element.33), channel_id=1, source_target_pairs={{0,24},{1,25},{2,26},{3,27},{4,28},{5,29},{6,30},{7,31},{8,0},{9,1... | collective-permute-start | bytes 786440 | tf_op jit(solution)/shard_map/ppermute | solution.py:244
  28.3 17.4 %collective-permute-start.11 = (bf16[2,128,512]{2,1,0:T(8,128)(2,1)S(1)}, bf16[2,128,512]{2,1,0:T(8,128)(2,1)S(1)}, u32[]{:S(2)}, u32[]{:S(2)}) collective-permute-start(bf16[2,128,512]{2,1,0:T(8,128)(2,1)S(1)} %get-tuple-element.34), channel_id=1, source_target_pairs={{0,16},{1,17},{2,18},{3,19},{4,20},{5,21},{6,22},{7,23},{8,24},{9,... | collective-permute-start | bytes 786440 | tf_op jit(solution)/shard_map/ppermute | solution.py:244
  31.8 14.9 %collective-permute-start.12 = (bf16[2,128,512]{2,1,0:T(8,128)(2,1)S(1)}, bf16[2,128,512]{2,1,0:T(8,128)(2,1)S(1)}, u32[]{:S(2)}, u32[]{:S(2)}) collective-permute-start(bf16[2,128,512]{2,1,0:T(8,128)(2,1)S(1)} %get-tuple-element.35), channel_id=1, source_target_pairs={{0,8},{1,9},{2,10},{3,11},{4,12},{5,13},{6,14},{7,15},{8,16},{9,17... | collective-permute-start | bytes 786440 | tf_op jit(solution)/shard_map/ppermute | solution.py:244
  32.7 26.0 %collective-permute-start.9 = (bf16[2,128,512]{2,1,0:T(8,128)(2,1)S(1)}, bf16[2,128,512]{2,1,0:T(8,128)(2,1)S(1)}, u32[]{:S(2)}, u32[]{:S(2)}) collective-permute-start(bf16[2,128,512]{2,1,0:T(8,128)(2,1)S(1)} %get-tuple-element.32), channel_id=1, source_target_pairs={{0,224},{1,225},{2,226},{3,227},{4,228},{5,229},{6,230},{7,231},{8... | collective-permute-start | bytes 786440 | tf_op jit(solution)/shard_map/ppermute | solution.py:243
  43.5 15.3 %collective-permute-start.2 = (bf16[2,128,512]{2,1,0:T(8,128)(2,1)S(1)}, bf16[2,128,512]{2,1,0:T(8,128)(2,1)S(1)}, u32[]{:S(2)}, u32[]{:S(2)}) collective-permute-start(bf16[2,128,512]{2,1,0:T(8,128)(2,1)S(1)} %get-tuple-element.26), channel_id=1, source_target_pairs={{0,24},{1,25},{2,26},{3,27},{4,28},{5,29},{6,30},{7,31},{8,0},{9,1... | collective-permute-start | bytes 786440 | tf_op jit(solution)/shard_map/ppermute | solution.py:244
  43.6 16.1 %collective-permute-start.3 = (bf16[2,128,512]{2,1,0:T(8,128)(2,1)S(1)}, bf16[2,128,512]{2,1,0:T(8,128)(2,1)S(1)}, u32[]{:S(2)}, u32[]{:S(2)}) collective-permute-start(bf16[2,128,512]{2,1,0:T(8,128)(2,1)S(1)} %get-tuple-element.27), channel_id=1, source_target_pairs={{0,16},{1,17},{2,18},{3,19},{4,20},{5,21},{6,22},{7,23},{8,24},{9,... | collective-permute-start | bytes 786440 | tf_op jit(solution)/shard_map/ppermute | solution.py:244
  45.7 15.3 %collective-permute-start.4 = (bf16[2,128,512]{2,1,0:T(8,128)(2,1)S(1)}, bf16[2,128,512]{2,1,0:T(8,128)(2,1)S(1)}, u32[]{:S(2)}, u32[]{:S(2)}) collective-permute-start(bf16[2,128,512]{2,1,0:T(8,128)(2,1)S(1)} %get-tuple-element.28), channel_id=1, source_target_pairs={{0,8},{1,9},{2,10},{3,11},{4,12},{5,13},{6,14},{7,15},{8,16},{9,17... | collective-permute-start | bytes 786440 | tf_op jit(solution)/shard_map/ppermute | solution.py:244
  46.8 17.1 %collective-permute-start.1 = (bf16[2,128,512]{2,1,0:T(8,128)(2,1)S(1)}, bf16[2,128,512]{2,1,0:T(8,128)(2,1)S(1)}, u32[]{:S(2)}, u32[]{:S(2)}) collective-permute-start(bf16[2,128,512]{2,1,0:T(8,128)(2,1)S(1)} %get-tuple-element.25), channel_id=1, source_target_pairs={{0,224},{1,225},{2,226},{3,227},{4,228},{5,229},{6,230},{7,231},{8... | collective-permute-start | bytes 786440 | tf_op jit(solution)/shard_map/ppermute | solution.py:243
  58.8 8.9 %collective-permute-start.13 = (bf16[2,128,512]{2,1,0:T(8,128)(2,1)S(1)}, bf16[2,128,512]{2,1,0:T(8,128)(2,1)S(1)}, u32[]{:S(2)}, u32[]{:S(2)}) collective-permute-start(bf16[2,128,512]{2,1,0:T(8,128)(2,1)S(1)} %get-tuple-element.36), channel_id=1, source_target_pairs={{0,24},{1,25},{2,26},{3,27},{4,28},{5,29},{6,30},{7,31},{8,0},{9,1... | collective-permute-start | bytes 786440 | tf_op jit(solution)/shard_map/ppermute | solution.py:244
  58.9 19.7 %collective-permute-start.14 = (bf16[2,128,512]{2,1,0:T(8,128)(2,1)S(1)}, bf16[2,128,512]{2,1,0:T(8,128)(2,1)S(1)}, u32[]{:S(2)}, u32[]{:S(2)}) collective-permute-start(bf16[2,128,512]{2,1,0:T(8,128)(2,1)S(1)} %get-tuple-element.37), channel_id=1, source_target_pairs={{0,16},{1,17},{2,18},{3,19},{4,20},{5,21},{6,22},{7,23},{8,24},{9,... | collective-permute-start | bytes 786440 | tf_op jit(solution)/shard_map/ppermute | solution.py:244
  59.7 10.6 %copy-start.2 = (s32[1,1024]{1,0:T(1,128)S(1)}, s32[1,1024]{1,0:T(1,128)}, u32[]{:S(2)}) copy-start(s32[1,1024]{1,0:T(1,128)} %param.6) | copy-start | bytes 12292
  59.7 10.8 %copy-start = (bf16[2048,512]{1,0:T(8,128)(2,1)S(1)}, bf16[2048,512]{1,0:T(8,128)(2,1)}, u32[]{:S(2)}) copy-start(bf16[2048,512]{1,0:T(8,128)(2,1)} %get-tuple-element.56.rest_4_) | copy-start | bytes 6291460
  59.7 18.9 %collective-permute-start.15 = (bf16[2,128,512]{2,1,0:T(8,128)(2,1)S(1)}, bf16[2,128,512]{2,1,0:T(8,128)(2,1)S(1)}, u32[]{:S(2)}, u32[]{:S(2)}) collective-permute-start(bf16[2,128,512]{2,1,0:T(8,128)(2,1)S(1)} %get-tuple-element.38), channel_id=1, source_target_pairs={{0,8},{1,9},{2,10},{3,11},{4,12},{5,13},{6,14},{7,15},{8,16},{9,17... | collective-permute-start | bytes 786440 | tf_op jit(solution)/shard_map/ppermute | solution.py:244
  64.0 18.7 %collective-permute-start.5 = (bf16[2,128,512]{2,1,0:T(8,128)(2,1)S(1)}, bf16[2,128,512]{2,1,0:T(8,128)(2,1)S(1)}, u32[]{:S(2)}, u32[]{:S(2)}) collective-permute-start(bf16[2,128,512]{2,1,0:T(8,128)(2,1)S(1)} %get-tuple-element.29), channel_id=1, source_target_pairs={{0,24},{1,25},{2,26},{3,27},{4,28},{5,29},{6,30},{7,31},{8,0},{9,1... | collective-permute-start | bytes 786440 | tf_op jit(solution)/shard_map/ppermute | solution.py:244
  64.1 18.6 %collective-permute-start.6 = (bf16[2,128,512]{2,1,0:T(8,128)(2,1)S(1)}, bf16[2,128,512]{2,1,0:T(8,128)(2,1)S(1)}, u32[]{:S(2)}, u32[]{:S(2)}) collective-permute-start(bf16[2,128,512]{2,1,0:T(8,128)(2,1)S(1)} %get-tuple-element.30), channel_id=1, source_target_pairs={{0,16},{1,17},{2,18},{3,19},{4,20},{5,21},{6,22},{7,23},{8,24},{9,... | collective-permute-start | bytes 786440 | tf_op jit(solution)/shard_map/ppermute | solution.py:244
  67.7 15.0 %collective-permute-start.7 = (bf16[2,128,512]{2,1,0:T(8,128)(2,1)S(1)}, bf16[2,128,512]{2,1,0:T(8,128)(2,1)S(1)}, u32[]{:S(2)}, u32[]{:S(2)}) collective-permute-start(bf16[2,128,512]{2,1,0:T(8,128)(2,1)S(1)} %get-tuple-element.31), channel_id=1, source_target_pairs={{0,8},{1,9},{2,10},{3,11},{4,12},{5,13},{6,14},{7,15},{8,16},{9,17... | collective-permute-start | bytes 786440 | tf_op jit(solution)/shard_map/ppermute | solution.py:244
  82.7 4.9 %copy-start.3 = (s32[1,1024,1]{1,2,0:T(1,128)S(1)}, s32[1,1024,1]{1,2,0:T(1,128)}, u32[]{:S(2)}) copy-start(s32[1,1024,1]{1,2,0:T(1,128)} %param.9) | copy-start | bytes 12292
  86.8 2.0 %collective-permute-start.16 = (bf16[1024,256]{1,0:T(8,128)(2,1)S(1)}, bf16[1024,256]{1,0:T(8,128)(2,1)S(1)}, u32[]{:S(2)}, u32[]{:S(2)}) collective-permute-start(bf16[1024,256]{1,0:T(8,128)(2,1)S(1)} %get-tuple-element.40), channel_id=1, source_target_pairs={{0,1},{1,0},{2,3},{3,2},{4,5},{5,4},{6,7},{7,6},{8,9},{9,8},{10,11... | collective-permute-start | bytes 1572872 | tf_op jit(solution)/shard_map/ppermute | solution.py:258
  89.0 7.8 %collective-permute-start.17 = (bf16[512,128]{1,0:T(8,128)(2,1)S(1)}, bf16[512,128]{1,0:T(8,128)(2,1)S(1)}, u32[]{:S(2)}, u32[]{:S(2)}) collective-permute-start(bf16[512,128]{1,0:T(8,128)(2,1)S(1)} %get-tuple-element.42), channel_id=1, source_target_pairs={{0,2},{1,3},{2,0},{3,1},{4,6},{5,7},{6,4},{7,5},{8,10},{9,11},{10,... | collective-permute-start | bytes 393224 | tf_op jit(solution)/shard_map/ppermute | solution.py:266
  92.6 9.5 %collective-permute-start.18 = (bf16[512,128]{1,0:T(8,128)(2,1)S(1)}, bf16[512,128]{1,0:T(8,128)(2,1)S(1)}, u32[]{:S(2)}, u32[]{:S(2)}) collective-permute-start(bf16[512,128]{1,0:T(8,128)(2,1)S(1)} %get-tuple-element.43), channel_id=1, source_target_pairs={{0,4},{1,5},{2,6},{3,7},{4,0},{5,1},{6,2},{7,3},{8,12},{9,13},{10,... | collective-permute-start | bytes 393224 | tf_op jit(solution)/shard_map/ppermute | solution.py:266
  92.6 13.5 %collective-permute-start.19 = (bf16[512,128]{1,0:T(8,128)(2,1)S(1)}, bf16[512,128]{1,0:T(8,128)(2,1)S(1)}, u32[]{:S(2)}, u32[]{:S(2)}) collective-permute-start(bf16[512,128]{1,0:T(8,128)(2,1)S(1)} %get-tuple-element.44), channel_id=1, source_target_pairs={{0,6},{1,7},{2,4},{3,5},{4,2},{5,3},{6,0},{7,1},{8,14},{9,15},{10,... | collective-permute-start | bytes 393224 | tf_op jit(solution)/shard_map/ppermute | solution.py:266

commit v3 on v2

--- a/solution.py
+++ b/solution.py
@@ -10,9 +10,11 @@
 
 LAGS = 512
 REACH = 3
-CHUNKS = 4
-FIRST_DONE = False
-CHOOSE_COST = (5_000_000_000,) * 4
+SIZES = (512, 512, 512, 512)
+CHUNKS = len(SIZES)
+FIRST_DONE = (0, 0, 0, 0)
+LAG = (0, 0, 0, 3)
+CHOOSE_COST = 5_000_000_000
 ROWS = 256
 AXES = ("chan", "win")
 N_X = 4
@@ -24,13 +26,15 @@
     for chan in range(32):
         for win in range(8):
             row, x, z, core = chan // N_X, chan % N_X, win // N_CORE, win % N_CORE
-            row, x, z, core = move(row, x, z, core)
-            pairs.append((chan * 8 + win, (row * N_X + x) * 8 + z * N_CORE + core))
+            target = move(row, x, z, core)
+            if target is not None:
+                row, x, z, core = target
+                pairs.append((chan * 8 + win, (row * N_X + x) * 8 + z * N_CORE + core))
     return pairs
 
 
 def to_previous_row(row, x, z, core):
-    return ((row - 1) % 8 if x < REACH else row), x, z, core
+    return (row - 1, x, z, core) if row > 0 and x < REACH else None
 
 
 CROSS = pairs_of(to_previous_row)
@@ -82,7 +86,7 @@
     left_hot = first_ref[...]
     right_hot = second_ref[...]
     bins = blocks.shape[2]
-    step = min(512, bins)
+    step = bins
     for start in range(0, bins, step):
         at = pl.ds(start, step)
         left = [dot(left_hot, blocks[part, :128, at]) for part in range(2)]
@@ -155,21 +159,38 @@
 
 
 def choose(place, crossed, own, later, after, flops):
-    shape = jax.ShapeDtypeStruct(own.shape, own.dtype)
     held = [crossed, own] + ([] if later is None else [later])
+    shapes = [jax.ShapeDtypeStruct(a.shape, a.dtype) for a in held[2:] + [own] * REACH]
     vmem = pl.BlockSpec(memory_space=pltpu.VMEM)
     outs = pl.pallas_call(
         functools.partial(choose_kernel, later is not None),
         in_specs=[pl.BlockSpec(memory_space=pltpu.SMEM)]
         + [vmem] * len(held)
         + [pl.BlockSpec(memory_space=pl.ANY)] * len(after),
-        out_specs=[vmem] * (REACH + len(held) - 2),
-        out_shape=[shape] * (REACH + len(held) - 2),
+        out_specs=[vmem] * len(shapes),
+        out_shape=shapes,
         compiler_params=pltpu.CompilerParams(vmem_limit_bytes=16 << 20),
         cost_estimate=pl.CostEstimate(flops=flops, bytes_accessed=1 << 20, transcendentals=0),
         name="choose",
     )(place[None], *held, *after)
     return outs[-REACH:], outs[0]
+
+
+def hold_kernel(own, after, out):
+    out[...] = own[...]
+
+
+def hold(own, after):
+    vmem = pl.BlockSpec(memory_space=pltpu.VMEM)
+    return pl.pallas_call(
+        hold_kernel,
+        in_specs=[vmem, pl.BlockSpec(memory_space=pl.ANY)],
+        out_specs=vmem,
+        out_shape=jax.ShapeDtypeStruct(own.shape, own.dtype),
+        compiler_params=pltpu.CompilerParams(vmem_limit_bytes=16 << 20),
+        cost_estimate=pl.CostEstimate(flops=1_000_000, bytes_accessed=1 << 20, transcendentals=0),
+        name="hold",
+    )(own, after)
 
 
 def split_kernel(keep, received, *outs):
@@ -212,9 +233,9 @@
     slots = pair_first.shape[1]
     x_place = lax.axis_index("chan") % N_X
     whitened = jnp.swapaxes(whiten(spectra[0]), 0, 1)
-    size = bins // CHUNKS
-    own = [whitened[:, :, q * size : (q + 1) * size] for q in range(CHUNKS)]
-    crossed = [lax.ppermute(own[q], AXES, CROSS) for q in range(2)]
+    starts = [sum(SIZES[:q]) for q in range(CHUNKS)]
+    own = [whitened[:, :, at : at + size] for at, size in zip(starts, SIZES)]
+    crossed = [lax.ppermute(own[0], AXES, CROSS)]
 
     first_hot = (pair_first[0][:, None] == jnp.arange(128, dtype=jnp.int32)).astype(jnp.bfloat16)
     second_hot = (pair_second[0][:, None] == jnp.arange(512, dtype=jnp.int32)).astype(jnp.bfloat16)
@@ -227,18 +248,21 @@
     place = jnp.where(order < pair_count[0], place, -1)
     place_hot = (place[None, :] == jnp.arange(2048, dtype=jnp.int32)[:, None]).astype(jnp.bfloat16)
     cosine, sine = lag_table(bins, windows_all)
+    crossed.append(lax.ppermute(hold(own[1], cosine), AXES, CROSS))
 
     acc = None
-    history = []
+    history, sums = [], []
     f32 = jnp.float32
     for q in range(CHUNKS):
         after = []
         if q >= 2:
             after += [history[q - 2][d] for d in (1, 2, 3)]
-        if q >= 1 and FIRST_DONE:
-            after += [history[q - 1][2]]
+        if LAG[q]:
+            after.append(sums[q - LAG[q]])
+        if q >= 1:
+            after += [history[q - 1][d] for d in (2, 1, 3)[: FIRST_DONE[q]]]
         later = own[q + 2] if q + 2 < CHUNKS else None
-        sources, copied = choose(x_place, crossed[q], own[q], later, after, CHOOSE_COST[q])
+        sources, copied = choose(x_place, crossed[q], own[q], later, after, CHOOSE_COST)
         if later is not None:
             crossed.append(lax.ppermute(copied, AXES, CROSS))
         ahead = {d: lax.ppermute(sources[d - 1], AXES, AROUND[d]) for d in (2, 1, 3)}
@@ -255,6 +279,7 @@
         else:
             kernel = first_kernel if q == 0 else next_kernel
             (acc,) = run_chunk(kernel, *operands, [whole])
+            sums.append(acc)
     received = lax.ppermute(send, AXES, OTHER_CORE)
     packed = (slots // 2, 128)
     pieces = call(
@@ -263,9 +288,9 @@
         keep,
         received,
     )
-    arrived = [lax.ppermute(pieces[k], AXES, OTHER_CHIP[k]) for k in (1, 2, 3)]
+    arrived = {k: lax.ppermute(pieces[k], AXES, OTHER_CHIP[k]) for k in (3, 2, 1)}
     buffer = call(
-        route_kernel, jax.ShapeDtypeStruct((32, 32, 128), jnp.bfloat16), place_hot, pieces[0], *arrived
+        route_kernel, jax.ShapeDtypeStruct((32, 32, 128), jnp.bfloat16), place_hot, pieces[0], *(arrived[k] for k in (1, 2, 3))
     )
     routed = lax.all_to_all(buffer, "chan", split_axis=0, concat_axis=0, tiled=True)
     return call(unpack_kernel, jax.ShapeDtypeStruct((1, 32, 64, 64), f32), routed)

time: 132 us -> 129 us (0.977)
  starting transfers between devices: 54.9 us -> 30.6 us
  waiting for transfers between devices: 21.5 us -> 38.8 us
  blocking collectives: 22.9 us -> 25.6 us
  Pallas kernels: 20.3 us -> 21.9 us
    ppermute x2, starting transfers between devices: 22.6 us -> 2.69 us  [on_device(): crossed.append(lax.ppermute(copied, AXES, CROSS))]
    ppermute x5, waiting for transfers between devices: 16.2 us -> 28.2 us  [the longest x1 18.6 us: on_device(): crossed = [lax.ppermute(own[0], AXES, CROSS)]]
    ppermute x5, starting transfers between devices: 17.7 us -> 6.14 us  [the longest x3 3.57 us: on_device(): lax.ppermute(pieces[k], AXES, OTHER_CHIP[k])]
    ppermute x12, starting transfers between devices: 14.6 us -> 21.6 us  [on_device(): lax.ppermute(sources[d - 1], AXES, AROUND[d])]
    ppermute x12, waiting for transfers between devices: 1.65 us -> 6.42 us  [on_device(): lax.ppermute(sources[d - 1], AXES, AROUND[d])]
    all_to_all x1, blocking collectives: 22.9 us -> 25.6 us  [on_device(): lax.all_to_all(buffer, 'chan', split_axis=0, concat_axis=0, tiled=True)]
  transfers between devices with their start and end apart: 20 -> 20, of which waited for: 7 -> 10; matrix products, arithmetic and copies ran while one was open for 6% -> 6% of each run, Pallas kernels for 10% -> 12%
where the time goes in v3:
time: 129 us
  waiting for transfers between devices  38.8 us (30%)
  starting transfers between devices  30.6 us (24%)
  blocking collectives  25.6 us (20%)
  Pallas kernels  21.9 us (17%)
  other arithmetic  10 us (8%)
    all_to_all x1, blocking collectives, on_device(): lax.all_to_all(buffer, 'chan', split_axis=0, concat_axis=0, tiled=True)  25.6 us
    ppermute x12, starting transfers between devices, on_device(): lax.ppermute(sources[d - 1], AXES, AROUND[d])  21.6 us
    ppermute x1, waiting for transfers between devices, on_device(): crossed = [lax.ppermute(own[0], AXES, CROSS)]  18.6 us
    pallas_call x4, Pallas kernels, run_chunk(): pl.pallas_call(kernel, grid=(slots // ROWS,), in_specs=in_specs, out_spec...  16.1 us
    ppermute x3, waiting for transfers between devices, on_device(): lax.ppermute(pieces[k], AXES, OTHER_CHIP[k])  9.61 us
    ppermute x12, waiting for transfers between devices, on_device(): lax.ppermute(sources[d - 1], AXES, AROUND[d])  6.42 us
    ppermute x3, starting transfers between devices, on_device(): lax.ppermute(pieces[k], AXES, OTHER_CHIP[k])  3.57 us
    ppermute x2, waiting for transfers between devices, on_device(): crossed.append(lax.ppermute(copied, AXES, CROSS))  3.46 us
  transfers between devices with their start and end apart: 20, of which 10 were waited for; matrix products, arithmetic and copies ran while one was open for 6% of the time, Pallas kernels for 12%

profile of v3, /device:TPU:32, one launch (start us, length us, event | category | flops | bytes accessed | tf_op | source)
XLA Modules:
  0.0 128.6 jit_solution(9278795552372067360)
XLA Ops:
  0.0 1.7 %fusion.4 = f32[128]{0:T(128)S(1)} fusion(bf16[1,128,2,2048]{3,2,1,0:T(2,128)(2,1)} %param.5), kind=kLoop, calls=%fused_computation.12 | loop fusion | flops 1572736 | bytes 1049088 | tf_op jit(solution)/shard_map/reduce_sum | solution.py:72
  1.7 1.7 %fusion.10 = bf16[2,128,2048]{2,1,0:T(8,128)(2,1)S(1)} fusion(f32[128]{0:T(128)S(1)} %add_rsqrt_fusion, bf16[1,128,2,2048]{3,2,1,0:T(2,128)(2,1)} %param.5), kind=kLoop, calls=%fused_computation.19 | loop fusion | flops 1572864 | bytes 2097664 | tf_op jit(solution)/shard_map/transpose | solution.py:235
  3.4 0.1 fusion.42
  3.5 1.3 %collective-permute-start.5 = (bf16[2,128,512]{2,1,0:T(8,128)(2,1)S(1)}, bf16[2,128,512]{2,1,0:T(8,128)(2,1)}, u32[]{:S(2)}, u32[]{:S(2)}) collective-permute-start(bf16[2,128,512]{2,1,0:T(8,128)(2,1)S(1)} %get-tuple-element.46.own.rest_0_), channel_id=1, source_target_pairs={{32,0},{33,1},{34,2},{35,3},{36,4},{37,5},{38,6},{39,7},{40,8},{41... | collective-permute-start | bytes 786440 | tf_op jit(solution)/shard_map/ppermute | solution.py:238
  4.9 0.3 fusion.25
  5.1 0.6 fusion.21
  5.7 0.1 reshape.238
  5.8 1.2 multiply_add_fusion
  7.0 0.3 fusion.2.after.rest_4_
  7.4 0.0 copy-start.1
  7.4 0.0 copy-start.2
  7.4 0.7 hold.1
  8.1 1.3 collective-permute-start
  9.4 1.7 %fusion.1.rest_5_ = bf16[2048,512]{1,0:T(8,128)(2,1)} fusion(f32[64,32,512]{2,1,0:T(8,128)S(1)} %get-tuple-element.49, f32[2048]{0:T(1024)S(1)} %neg.8), kind=kLoop, calls=%fused_computation.3 | loop fusion | flops 2097152 | bytes 6299648 | tf_op jit(solution)/shard_map/convert_element_type | solution.py:67
  11.1 0.2 fusion.11.first
  11.3 0.2 fusion.6.second
  11.6 18.6 %collective-permute-done.5.crossed = bf16[2,128,512]{2,1,0:T(8,128)(2,1)} collective-permute-done((bf16[2,128,512]{2,1,0:T(8,128)(2,1)S(1)}, bf16[2,128,512]{2,1,0:T(8,128)(2,1)}, u32[]{:S(2)}, u32[]{:S(2)}) %collective-permute-start.5) | collective-permute-done | bytes 262176 | tf_op jit(solution)/shard_map/ppermute | solution.py:238
  30.2 1.0 choose.5
  31.2 0.1 collective-permute-start.6
  31.3 3.5 %collective-permute-start.7 = (bf16[2,128,512]{2,1,0:T(8,128)(2,1)S(1)}, bf16[2,128,512]{2,1,0:T(8,128)(2,1)S(1)}, u32[]{:S(2)}, u32[]{:S(2)}) collective-permute-start(bf16[2,128,512]{2,1,0:T(8,128)(2,1)S(1)} %get-tuple-element.30), channel_id=1, source_target_pairs={{0,16},{1,17},{2,18},{3,19},{4,20},{5,21},{6,22},{7,23},{8,24},{9,... | collective-permute-start | bytes 786440 | tf_op jit(solution)/shard_map/ppermute | solution.py:268
  34.8 0.9 collective-permute-start.8
  35.7 1.3 collective-permute-start.12
  37.0 0.0 collective-permute-done.crossed
  37.0 1.1 choose.4
  38.1 1.8 %collective-permute-start.2 = (bf16[2,128,512]{2,1,0:T(8,128)(2,1)S(1)}, bf16[2,128,512]{2,1,0:T(8,128)(2,1)S(1)}, u32[]{:S(2)}, u32[]{:S(2)}) collective-permute-start(bf16[2,128,512]{2,1,0:T(8,128)(2,1)S(1)} %get-tuple-element.26), channel_id=1, source_target_pairs={{0,24},{1,25},{2,26},{3,27},{4,28},{5,29},{6,30},{7,31},{8,0},{9,1... | collective-permute-start | bytes 786440 | tf_op jit(solution)/shard_map/ppermute | solution.py:268
  39.9 0.6 collective-permute-done.6.rest_1_.rest_0_
  40.5 3.0 %collective-permute-start.3 = (bf16[2,128,512]{2,1,0:T(8,128)(2,1)S(1)}, bf16[2,128,512]{2,1,0:T(8,128)(2,1)S(1)}, u32[]{:S(2)}, u32[]{:S(2)}) collective-permute-start(bf16[2,128,512]{2,1,0:T(8,128)(2,1)S(1)} %get-tuple-element.27), channel_id=1, source_target_pairs={{0,16},{1,17},{2,18},{3,19},{4,20},{5,21},{6,22},{7,23},{8,24},{9,... | collective-permute-start | bytes 786440 | tf_op jit(solution)/shard_map/ppermute | solution.py:268
  43.5 0.0 collective-permute-done.7.rest_2_.rest_1_
  43.5 5.0 %collective-permute-start.4 = (bf16[2,128,512]{2,1,0:T(8,128)(2,1)S(1)}, bf16[2,128,512]{2,1,0:T(8,128)(2,1)S(1)}, u32[]{:S(2)}, u32[]{:S(2)}) collective-permute-start(bf16[2,128,512]{2,1,0:T(8,128)(2,1)S(1)} %get-tuple-element.28), channel_id=1, source_target_pairs={{0,8},{1,9},{2,10},{3,11},{4,12},{5,13},{6,14},{7,15},{8,16},{9,17... | collective-permute-start | bytes 786440 | tf_op jit(solution)/shard_map/ppermute | solution.py:268
  48.6 2.4 %collective-permute-done.8.rest_3_.rest_2_ = bf16[2,128,512]{2,1,0:T(8,128)(2,1)S(1)} collective-permute-done((bf16[2,128,512]{2,1,0:T(8,128)(2,1)S(1)}, bf16[2,128,512]{2,1,0:T(8,128)(2,1)S(1)}, u32[]{:S(2)}, u32[]{:S(2)}) %collective-permute-start.8) | collective-permute-done | bytes 262176 | tf_op jit(solution)/shard_map/ppermute | solution.py:268
  51.0 1.4 %collective-permute-start.1 = (bf16[2,128,512]{2,1,0:T(8,128)(2,1)S(1)}, bf16[2,128,512]{2,1,0:T(8,128)(2,1)S(1)}, u32[]{:S(2)}, u32[]{:S(2)}) collective-permute-start(bf16[2,128,512]{2,1,0:T(8,128)(2,1)S(1)} %get-tuple-element.25), channel_id=1, source_target_pairs={{32,0},{33,1},{34,2},{35,3},{36,4},{37,5},{38,6},{39,7},{40,8},{41... | collective-permute-start | bytes 786440 | tf_op jit(solution)/shard_map/ppermute | solution.py:267
  52.4 0.1 choose.7
  52.5 0.1 collective-permute-start.13
  52.6 3.9 %correlate.4.rest_3_.rest_6_ = f32[1024,512]{1,0:T(8,128)S(1)} custom-call(bf16[1024,128]{1,0:T(8,128)(2,1)S(1)} %fusion.11.first, bf16[1024,512]{1,0:T(8,128)(2,1)S(1)} %fusion.6.second, bf16[2,128,512]{2,1,0:T(8,128)(2,1)S(1)} %get-tuple-element.46.own.rest_0_, bf16[2,128,512]{2,1,0:T(8,128)(2,1)S(1)} %collective-permute-done.6.rest_1_.rest_0_, ...), custom_call_target="tpu_custom_call" | custom-call | flops 200000000 | bytes 1048576 | tf_op jit(solution)/shard_map/correlate/pallas_call | solution.py:133
  56.5 0.0 collective-permute-done.2.rest_0_.rest_1_
  56.5 0.8 collective-permute-start.14
  57.4 0.0 collective-permute-done.3.rest_1_.rest_2_
  57.4 2.4 %collective-permute-start.15 = (bf16[2,128,512]{2,1,0:T(8,128)(2,1)S(1)}, bf16[2,128,512]{2,1,0:T(8,128)(2,1)S(1)}, u32[]{:S(2)}, u32[]{:S(2)}) collective-permute-start(bf16[2,128,512]{2,1,0:T(8,128)(2,1)S(1)} %get-tuple-element.38), channel_id=1, source_target_pairs={{0,8},{1,9},{2,10},{3,11},{4,12},{5,13},{6,14},{7,15},{8,16},{9,17... | collective-permute-start | bytes 786440 | tf_op jit(solution)/shard_map/ppermute | solution.py:268
  59.8 0.0 collective-permute-done.4.rest_2_.rest_3_
  59.8 3.5 %collective-permute-done.1.crossed = bf16[2,128,512]{2,1,0:T(8,128)(2,1)S(1)} collective-permute-done((bf16[2,128,512]{2,1,0:T(8,128)(2,1)S(1)}, bf16[2,128,512]{2,1,0:T(8,128)(2,1)S(1)}, u32[]{:S(2)}, u32[]{:S(2)}) %collective-permute-start.1) | collective-permute-done | bytes 262176 | tf_op jit(solution)/shard_map/ppermute | solution.py:267
  63.3 0.1 choose.6
  63.4 0.7 collective-permute-start.10
  64.1 0.0 collective-permute-start.11
  64.1 3.2 %collective-permute-start.9 = (bf16[2,128,512]{2,1,0:T(8,128)(2,1)S(1)}, bf16[2,128,512]{2,1,0:T(8,128)(2,1)S(1)}, u32[]{:S(2)}, u32[]{:S(2)}) collective-permute-start(bf16[2,128,512]{2,1,0:T(8,128)(2,1)S(1)} %get-tuple-element.32), channel_id=1, source_target_pairs={{0,24},{1,25},{2,26},{3,27},{4,28},{5,29},{6,30},{7,31},{8,0},{9,1... | collective-permute-start | bytes 786440 | tf_op jit(solution)/shard_map/ppermute | solution.py:268
  67.3 4.1 %correlate.5.rest_6_ = f32[1024,512]{1,0:T(8,128)S(1)} custom-call(bf16[1024,128]{1,0:T(8,128)(2,1)S(1)} %fusion.11.first, bf16[1024,512]{1,0:T(8,128)(2,1)S(1)} %fusion.6.second, bf16[2,128,512]{2,1,0:T(8,128)(2,1)S(1)} %get-tuple-element.47.own.rest_0_, bf16[2,128,512]{2,1,0:T(8,128)(2,1)S(1)} %collective-permute-done.2.rest_0_.rest_1_, ...), custom_call_target="tpu_custom_call" | custom-call | flops 200000000 | bytes 1048576 | tf_op jit(solution)/shard_map/correlate/pallas_call | solution.py:133
  71.4 1.9 %collective-permute-done.15.rest_3_ = bf16[2,128,512]{2,1,0:T(8,128)(2,1)S(1)} collective-permute-done((bf16[2,128,512]{2,1,0:T(8,128)(2,1)S(1)}, bf16[2,128,512]{2,1,0:T(8,128)(2,1)S(1)}, u32[]{:S(2)}, u32[]{:S(2)}) %collective-permute-start.15) | collective-permute-done | bytes 262176 | tf_op jit(solution)/shard_map/ppermute | solution.py:268
  73.3 4.1 %correlate.6.rest_6_ = f32[1024,512]{1,0:T(8,128)S(1)} custom-call(bf16[1024,128]{1,0:T(8,128)(2,1)S(1)} %fusion.11.first, bf16[1024,512]{1,0:T(8,128)(2,1)S(1)} %fusion.6.second, bf16[2,128,512]{2,1,0:T(8,128)(2,1)S(1)} %get-tuple-element.45.rest_0_.own, bf16[2,128,512]{2,1,0:T(8,128)(2,1)S(1)} %collective-permute-done.13.rest_1_, ...), custom_call_target="tpu_custom_call" | custom-call | flops 200000000 | bytes 1048576 | tf_op jit(solution)/shard_map/correlate/pallas_call | solution.py:133
  77.4 0.0 copy-start.3
  77.4 1.5 %collective-permute-done.11.rest_3_ = bf16[2,128,512]{2,1,0:T(8,128)(2,1)S(1)} collective-permute-done((bf16[2,128,512]{2,1,0:T(8,128)(2,1)S(1)}, bf16[2,128,512]{2,1,0:T(8,128)(2,1)S(1)}, u32[]{:S(2)}, u32[]{:S(2)}) %collective-permute-start.11) | collective-permute-done | bytes 262176 | tf_op jit(solution)/shard_map/ppermute | solution.py:268
  78.9 4.0 %correlate.7 = (f32[1024,256]{1,0:T(8,128)S(1)}, bf16[1024,256]{1,0:T(8,128)(2,1)S(1)}) custom-call(bf16[1024,128]{1,0:T(8,128)(2,1)S(1)} %fusion.11.first, bf16[1024,512]{1,0:T(8,128)(2,1)S(1)} %fusion.6.second, bf16[2,128,512]{2,1,0:T(8,128)(2,1)S(1)} %get-tuple-element.48.rest_0_.own, bf16[2,128,512]{2,1,0:T(8,128)(2,1)S(1)} %collective-permute-done.9.rest_1_, ...), custom_call_target="tpu_custom_call" | custom-call | flops 200000000 | bytes 1048576 | tf_op jit(solution)/shard_map/correlate/pallas_call | solution.py:133
  82.9 0.1 collective-permute-start.16
  83.7 0.5 fusion.9
  84.3 0.7 collective-permute-done.16.received
  84.9 0.2 split_kernel.1
  85.2 0.1 collective-permute-start.17
  85.3 2.8 %collective-permute-start.18 = (bf16[512,128]{1,0:T(8,128)(2,1)S(1)}, bf16[512,128]{1,0:T(8,128)(2,1)S(1)}, u32[]{:S(2)}, u32[]{:S(2)}) collective-permute-start(bf16[512,128]{1,0:T(8,128)(2,1)S(1)} %get-tuple-element.43), channel_id=1, source_target_pairs={{0,4},{1,5},{2,6},{3,7},{4,0},{5,1},{6,2},{7,3},{8,12},{9,13},{10,... | collective-permute-start | bytes 393224 | tf_op jit(solution)/shard_map/ppermute | solution.py:291
  88.1 0.7 collective-permute-start.19
  88.8 2.1 %fusion.hot = bf16[2048,1024]{1,0:T(8,128)(2,1)S(1)} fusion(s32[1024]{0:T(1024)S(1)} %add_select_fusion.2), kind=kLoop, calls=%fused_computation.1 | loop fusion | flops 4194304 | bytes 4198400 | tf_op jit(solution)/shard_map/convert_element_type | solution.py:249
  90.9 0.8 collective-permute-done.17.one
  91.6 6.0 %collective-permute-done.18.two = bf16[512,128]{1,0:T(8,128)(2,1)S(1)} collective-permute-done((bf16[512,128]{1,0:T(8,128)(2,1)S(1)}, bf16[512,128]{1,0:T(8,128)(2,1)S(1)}, u32[]{:S(2)}, u32[]{:S(2)}) %collective-permute-start.18) | collective-permute-done | bytes 131104 | tf_op jit(solution)/shard_map/ppermute | solution.py:291
  97.6 2.9 %collective-permute-done.19.three = bf16[512,128]{1,0:T(8,128)(2,1)S(1)} collective-permute-done((bf16[512,128]{1,0:T(8,128)(2,1)S(1)}, bf16[512,128]{1,0:T(8,128)(2,1)S(1)}, u32[]{:S(2)}, u32[]{:S(2)}) %collective-permute-start.19) | collective-permute-done | bytes 131104 | tf_op jit(solution)/shard_map/ppermute | solution.py:291
  100.5 1.4 %route_kernel.1 = bf16[32,32,128]{2,1,0:T(8,128)(2,1)S(1)} custom-call(bf16[2048,1024]{1,0:T(8,128)(2,1)S(1)} %fusion.hot, f32[512,128]{1,0:T(8,128)S(1)} %get-tuple-element.41.keep, bf16[512,128]{1,0:T(8,128)(2,1)S(1)} %collective-permute-done.17.one, bf16[512,128]{1,0:T(8,128)(2,1)S(1)} %collective-permute-done.18.two, ...), custom_call_target="tpu_custom_call" | custom-call | tf_op jit(solution)/shard_map/route_kernel/pallas_call | solution.py:222
  101.9 25.6 %all_to_all.5.routed = bf16[32,32,128]{2,1,0:T(8,128)(2,1)S(1)} all-to-all(bf16[32,32,128]{2,1,0:T(8,128)(2,1)S(1)} %route_kernel.1), channel_id=1, replica_groups=mesh['chan'=32,'win'=8] {'chan'}, dimensions={0} | all-to-all | bytes 524288 | tf_op jit(solution)/shard_map/all_to_all | solution.py:295
  127.5 1.1 unpack_kernel.1
  (16 shorter events, 0.1 us)
Async XLA Ops:
  3.5 26.7 %collective-permute-start.5 = (bf16[2,128,512]{2,1,0:T(8,128)(2,1)S(1)}, bf16[2,128,512]{2,1,0:T(8,128)(2,1)}, u32[]{:S(2)}, u32[]{:S(2)}) collective-permute-start(bf16[2,128,512]{2,1,0:T(8,128)(2,1)S(1)} %get-tuple-element.46.own.rest_0_), channel_id=1, source_target_pairs={{32,0},{33,1},{34,2},{35,3},{36,4},{37,5},{38,6},{39,7},{40,8},{41... | collective-permute-start | bytes 786440 | tf_op jit(solution)/shard_map/ppermute | solution.py:238
  7.4 3.7 %copy-start.1 = (s32[1,1024]{1,0:T(1,128)S(1)}, s32[1,1024]{1,0:T(1,128)}, u32[]{:S(2)}) copy-start(s32[1,1024]{1,0:T(1,128)} %param.6) | copy-start | bytes 12292
  7.4 3.9 %copy-start.2 = (s32[1,1024]{1,0:T(1,128)S(1)}, s32[1,1024]{1,0:T(1,128)}, u32[]{:S(2)}) copy-start(s32[1,1024]{1,0:T(1,128)} %param.7) | copy-start | bytes 12292
  8.1 28.9 %collective-permute-start = (bf16[2,128,512]{2,1,0:T(8,128)(2,1)}, bf16[2,128,512]{2,1,0:T(8,128)(2,1)}, u32[]{:S(2)}, u32[]{:S(2)}) collective-permute-start(bf16[2,128,512]{2,1,0:T(8,128)(2,1)} %hold.1), channel_id=1, source_target_pairs={{32,0},{33,1},{34,2},{35,3},{36,4},{37,5},{38,6},{39,7},{40,8},{41... | collective-permute-start | bytes 786440 | tf_op jit(solution)/shard_map/ppermute | solution.py:251
  31.2 9.3 %collective-permute-start.6 = (bf16[2,128,512]{2,1,0:T(8,128)(2,1)S(1)}, bf16[2,128,512]{2,1,0:T(8,128)(2,1)S(1)}, u32[]{:S(2)}, u32[]{:S(2)}) collective-permute-start(bf16[2,128,512]{2,1,0:T(8,128)(2,1)S(1)} %get-tuple-element.29), channel_id=1, source_target_pairs={{0,24},{1,25},{2,26},{3,27},{4,28},{5,29},{6,30},{7,31},{8,0},{9,1... | collective-permute-start | bytes 786440 | tf_op jit(solution)/shard_map/ppermute | solution.py:268
  31.3 12.3 %collective-permute-start.7 = (bf16[2,128,512]{2,1,0:T(8,128)(2,1)S(1)}, bf16[2,128,512]{2,1,0:T(8,128)(2,1)S(1)}, u32[]{:S(2)}, u32[]{:S(2)}) collective-permute-start(bf16[2,128,512]{2,1,0:T(8,128)(2,1)S(1)} %get-tuple-element.30), channel_id=1, source_target_pairs={{0,16},{1,17},{2,18},{3,19},{4,20},{5,21},{6,22},{7,23},{8,24},{9,... | collective-permute-start | bytes 786440 | tf_op jit(solution)/shard_map/ppermute | solution.py:268
  34.8 16.1 %collective-permute-start.8 = (bf16[2,128,512]{2,1,0:T(8,128)(2,1)S(1)}, bf16[2,128,512]{2,1,0:T(8,128)(2,1)S(1)}, u32[]{:S(2)}, u32[]{:S(2)}) collective-permute-start(bf16[2,128,512]{2,1,0:T(8,128)(2,1)S(1)} %get-tuple-element.31), channel_id=1, source_target_pairs={{0,8},{1,9},{2,10},{3,11},{4,12},{5,13},{6,14},{7,15},{8,16},{9,17... | collective-permute-start | bytes 786440 | tf_op jit(solution)/shard_map/ppermute | solution.py:268
  35.7 16.7 %collective-permute-start.12 = (bf16[2,128,512]{2,1,0:T(8,128)(2,1)S(1)}, bf16[2,128,512]{2,1,0:T(8,128)(2,1)S(1)}, u32[]{:S(2)}, u32[]{:S(2)}) collective-permute-start(bf16[2,128,512]{2,1,0:T(8,128)(2,1)S(1)} %get-tuple-element.35), channel_id=1, source_target_pairs={{32,0},{33,1},{34,2},{35,3},{36,4},{37,5},{38,6},{39,7},{40,8},{41... | collective-permute-start | bytes 786440 | tf_op jit(solution)/shard_map/ppermute | solution.py:267
  38.1 18.5 %collective-permute-start.2 = (bf16[2,128,512]{2,1,0:T(8,128)(2,1)S(1)}, bf16[2,128,512]{2,1,0:T(8,128)(2,1)S(1)}, u32[]{:S(2)}, u32[]{:S(2)}) collective-permute-start(bf16[2,128,512]{2,1,0:T(8,128)(2,1)S(1)} %get-tuple-element.26), channel_id=1, source_target_pairs={{0,24},{1,25},{2,26},{3,27},{4,28},{5,29},{6,30},{7,31},{8,0},{9,1... | collective-permute-start | bytes 786440 | tf_op jit(solution)/shard_map/ppermute | solution.py:268
  40.5 16.9 %collective-permute-start.3 = (bf16[2,128,512]{2,1,0:T(8,128)(2,1)S(1)}, bf16[2,128,512]{2,1,0:T(8,128)(2,1)S(1)}, u32[]{:S(2)}, u32[]{:S(2)}) collective-permute-start(bf16[2,128,512]{2,1,0:T(8,128)(2,1)S(1)} %get-tuple-element.27), channel_id=1, source_target_pairs={{0,16},{1,17},{2,18},{3,19},{4,20},{5,21},{6,22},{7,23},{8,24},{9,... | collective-permute-start | bytes 786440 | tf_op jit(solution)/shard_map/ppermute | solution.py:268
  43.5 16.3 %collective-permute-start.4 = (bf16[2,128,512]{2,1,0:T(8,128)(2,1)S(1)}, bf16[2,128,512]{2,1,0:T(8,128)(2,1)S(1)}, u32[]{:S(2)}, u32[]{:S(2)}) collective-permute-start(bf16[2,128,512]{2,1,0:T(8,128)(2,1)S(1)} %get-tuple-element.28), channel_id=1, source_target_pairs={{0,8},{1,9},{2,10},{3,11},{4,12},{5,13},{6,14},{7,15},{8,16},{9,17... | collective-permute-start | bytes 786440 | tf_op jit(solution)/shard_map/ppermute | solution.py:268
  51.0 1.6 %copy-start = (bf16[2048,512]{1,0:T(8,128)(2,1)S(1)}, bf16[2048,512]{1,0:T(8,128)(2,1)}, u32[]{:S(2)}) copy-start(bf16[2048,512]{1,0:T(8,128)(2,1)} %fusion.1.rest_5_) | copy-start | bytes 6291460
  51.0 12.3 %collective-permute-start.1 = (bf16[2,128,512]{2,1,0:T(8,128)(2,1)S(1)}, bf16[2,128,512]{2,1,0:T(8,128)(2,1)S(1)}, u32[]{:S(2)}, u32[]{:S(2)}) collective-permute-start(bf16[2,128,512]{2,1,0:T(8,128)(2,1)S(1)} %get-tuple-element.25), channel_id=1, source_target_pairs={{32,0},{33,1},{34,2},{35,3},{36,4},{37,5},{38,6},{39,7},{40,8},{41... | collective-permute-start | bytes 786440 | tf_op jit(solution)/shard_map/ppermute | solution.py:267
  52.5 11.6 %collective-permute-start.13 = (bf16[2,128,512]{2,1,0:T(8,128)(2,1)S(1)}, bf16[2,128,512]{2,1,0:T(8,128)(2,1)S(1)}, u32[]{:S(2)}, u32[]{:S(2)}) collective-permute-start(bf16[2,128,512]{2,1,0:T(8,128)(2,1)S(1)} %get-tuple-element.36), channel_id=1, source_target_pairs={{0,24},{1,25},{2,26},{3,27},{4,28},{5,29},{6,30},{7,31},{8,0},{9,1... | collective-permute-start | bytes 786440 | tf_op jit(solution)/shard_map/ppermute | solution.py:268
  56.5 14.8 %collective-permute-start.14 = (bf16[2,128,512]{2,1,0:T(8,128)(2,1)S(1)}, bf16[2,128,512]{2,1,0:T(8,128)(2,1)S(1)}, u32[]{:S(2)}, u32[]{:S(2)}) collective-permute-start(bf16[2,128,512]{2,1,0:T(8,128)(2,1)S(1)} %get-tuple-element.37), channel_id=1, source_target_pairs={{0,16},{1,17},{2,18},{3,19},{4,20},{5,21},{6,22},{7,23},{8,24},{9,... | collective-permute-start | bytes 786440 | tf_op jit(solution)/shard_map/ppermute | solution.py:268
  57.4 15.9 %collective-permute-start.15 = (bf16[2,128,512]{2,1,0:T(8,128)(2,1)S(1)}, bf16[2,128,512]{2,1,0:T(8,128)(2,1)S(1)}, u32[]{:S(2)}, u32[]{:S(2)}) collective-permute-start(bf16[2,128,512]{2,1,0:T(8,128)(2,1)S(1)} %get-tuple-element.38), channel_id=1, source_target_pairs={{0,8},{1,9},{2,10},{3,11},{4,12},{5,13},{6,14},{7,15},{8,16},{9,17... | collective-permute-start | bytes 786440 | tf_op jit(solution)/shard_map/ppermute | solution.py:268
  63.4 14.1 %collective-permute-start.10 = (bf16[2,128,512]{2,1,0:T(8,128)(2,1)S(1)}, bf16[2,128,512]{2,1,0:T(8,128)(2,1)S(1)}, u32[]{:S(2)}, u32[]{:S(2)}) collective-permute-start(bf16[2,128,512]{2,1,0:T(8,128)(2,1)S(1)} %get-tuple-element.33), channel_id=1, source_target_pairs={{0,16},{1,17},{2,18},{3,19},{4,20},{5,21},{6,22},{7,23},{8,24},{9,... | collective-permute-start | bytes 786440 | tf_op jit(solution)/shard_map/ppermute | solution.py:268
  64.1 14.8 %collective-permute-start.11 = (bf16[2,128,512]{2,1,0:T(8,128)(2,1)S(1)}, bf16[2,128,512]{2,1,0:T(8,128)(2,1)S(1)}, u32[]{:S(2)}, u32[]{:S(2)}) collective-permute-start(bf16[2,128,512]{2,1,0:T(8,128)(2,1)S(1)} %get-tuple-element.34), channel_id=1, source_target_pairs={{0,8},{1,9},{2,10},{3,11},{4,12},{5,13},{6,14},{7,15},{8,16},{9,17... | collective-permute-start | bytes 786440 | tf_op jit(solution)/shard_map/ppermute | solution.py:268
  64.1 14.8 %collective-permute-start.9 = (bf16[2,128,512]{2,1,0:T(8,128)(2,1)S(1)}, bf16[2,128,512]{2,1,0:T(8,128)(2,1)S(1)}, u32[]{:S(2)}, u32[]{:S(2)}) collective-permute-start(bf16[2,128,512]{2,1,0:T(8,128)(2,1)S(1)} %get-tuple-element.32), channel_id=1, source_target_pairs={{0,24},{1,25},{2,26},{3,27},{4,28},{5,29},{6,30},{7,31},{8,0},{9,1... | collective-permute-start | bytes 786440 | tf_op jit(solution)/shard_map/ppermute | solution.py:268
  77.4 6.3 %copy-start.3 = (s32[1,1024,1]{1,2,0:T(1,128)S(1)}, s32[1,1024,1]{1,2,0:T(1,128)}, u32[]{:S(2)}) copy-start(s32[1,1024,1]{1,2,0:T(1,128)} %param.9) | copy-start | bytes 12292
  82.9 2.0 %collective-permute-start.16 = (bf16[1024,256]{1,0:T(8,128)(2,1)S(1)}, bf16[1024,256]{1,0:T(8,128)(2,1)S(1)}, u32[]{:S(2)}, u32[]{:S(2)}) collective-permute-start(bf16[1024,256]{1,0:T(8,128)(2,1)S(1)} %get-tuple-element.40), channel_id=1, source_target_pairs={{0,1},{1,0},{2,3},{3,2},{4,5},{5,4},{6,7},{7,6},{8,9},{9,8},{10,11... | collective-permute-start | bytes 1572872 | tf_op jit(solution)/shard_map/ppermute | solution.py:283
  85.2 6.4 %collective-permute-start.17 = (bf16[512,128]{1,0:T(8,128)(2,1)S(1)}, bf16[512,128]{1,0:T(8,128)(2,1)S(1)}, u32[]{:S(2)}, u32[]{:S(2)}) collective-permute-start(bf16[512,128]{1,0:T(8,128)(2,1)S(1)} %get-tuple-element.42), channel_id=1, source_target_pairs={{0,2},{1,3},{2,0},{3,1},{4,6},{5,7},{6,4},{7,5},{8,10},{9,11},{10,... | collective-permute-start | bytes 393224 | tf_op jit(solution)/shard_map/ppermute | solution.py:291
  85.3 12.3 %collective-permute-start.18 = (bf16[512,128]{1,0:T(8,128)(2,1)S(1)}, bf16[512,128]{1,0:T(8,128)(2,1)S(1)}, u32[]{:S(2)}, u32[]{:S(2)}) collective-permute-start(bf16[512,128]{1,0:T(8,128)(2,1)S(1)} %get-tuple-element.43), channel_id=1, source_target_pairs={{0,4},{1,5},{2,6},{3,7},{4,0},{5,1},{6,2},{7,3},{8,12},{9,13},{10,... | collective-permute-start | bytes 393224 | tf_op jit(solution)/shard_map/ppermute | solution.py:291
  88.1 12.4 %collective-permute-start.19 = (bf16[512,128]{1,0:T(8,128)(2,1)S(1)}, bf16[512,128]{1,0:T(8,128)(2,1)S(1)}, u32[]{:S(2)}, u32[]{:S(2)}) collective-permute-start(bf16[512,128]{1,0:T(8,128)(2,1)S(1)} %get-tuple-element.44), channel_id=1, source_target_pairs={{0,6},{1,7},{2,4},{3,5},{4,2},{5,3},{6,0},{7,1},{8,14},{9,15},{10,... | collective-permute-start | bytes 393224 | tf_op jit(solution)/shard_map/ppermute | solution.py:291

commit v4 on v3

--- a/solution.py
+++ b/solution.py
@@ -12,7 +12,6 @@
 REACH = 3
 SIZES = (512, 512, 512, 512)
 CHUNKS = len(SIZES)
-FIRST_DONE = (0, 0, 0, 0)
 LAG = (0, 0, 0, 3)
 CHOOSE_COST = 5_000_000_000
 ROWS = 256
@@ -67,10 +66,17 @@
     return [part.astype(jnp.bfloat16).reshape(bins, LAGS) for part in (cosine, sine)]
 
 
-def whiten(spectra):
+def whitening_scale(spectra):
     values = spectra.astype(jnp.float32)
-    power = jnp.mean(values * values, axis=(1, 2), keepdims=True)
-    return (values * lax.rsqrt(power + 1e-06)).astype(jnp.bfloat16)
+    return lax.rsqrt(jnp.mean(values * values, axis=(1, 2)) + 1e-06)
+
+
+def scale_rows(scale, bins):
+    pieces = []
+    for _ in range(3):
+        pieces.append(scale.astype(jnp.bfloat16))
+        scale = scale - pieces[-1].astype(jnp.float32)
+    return jnp.pad(jnp.stack(pieces), ((0, 13), (0, bins - scale.shape[0])))
 
 
 def dot(a, b):
@@ -81,7 +87,7 @@
     @pl.when(pl.program_id(0) == 0)
     def _():
         for d, ref in enumerate(halo):
-            blocks[:, 128 * d : 128 * (d + 1)] = ref[...]
+            blocks[:, 128 * d : 128 * (d + 1)] = ref[:, :128]
 
     left_hot = first_ref[...]
     right_hot = second_ref[...]
@@ -98,9 +104,19 @@
     return acc
 
 
+def slot_scale(hot, carriers):
+    total = jnp.zeros((hot.shape[0], 128), jnp.float32)
+    for d, ref in enumerate(carriers):
+        pieces = ref[0, 128:144, :128].astype(jnp.float32)
+        scale = pieces[0:1] + pieces[1:2] + pieces[2:3]
+        total = total + hot[:, 128 * d : 128 * (d + 1)].astype(jnp.float32) * scale
+    return jnp.sum(total, axis=1, keepdims=True)
+
+
 def first_kernel(first, second, *rest):
-    *halo, cosine, sine, out, blocks = rest
-    out[...] = correlate(first, second, halo, cosine, sine, None, blocks)
+    halo, (cosine, sine), carriers, (out, blocks) = rest[:4], rest[4:6], rest[6:10], rest[10:]
+    total = correlate(first, second, halo, cosine, sine, None, blocks)
+    out[...] = total * (slot_scale(first, carriers[:1]) * slot_scale(second, carriers))
 
 
 def next_kernel(first, second, *rest):
@@ -115,7 +131,7 @@
     send[...] = total[:, 256:].astype(jnp.bfloat16)
 
 
-def run_chunk(kernel, q, first_hot, second_hot, halo, cosine, sine, acc, outs):
+def run_chunk(kernel, q, first_hot, second_hot, halo, cosine, sine, acc, carriers, outs):
     slots = first_hot.shape[0]
     bins = halo[0].shape[2]
 
@@ -125,10 +141,11 @@
     def whole(shape):
         return pl.BlockSpec(shape, lambda i: (0,) * len(shape))
 
-    operands = [first_hot, second_hot, *halo, cosine, sine] + ([] if acc is None else [acc])
+    operands = [first_hot, second_hot, *halo, cosine, sine, *carriers] + ([] if acc is None else [acc])
     in_specs = [rows(128), rows(512)]
     in_specs += [whole(b.shape) for b in halo]
     in_specs += [pl.BlockSpec((bins, LAGS), lambda i: (q, 0)) for _ in range(2)]
+    in_specs += [whole(c.shape) for c in carriers]
     in_specs += [] if acc is None else [rows(512)]
     return pl.pallas_call(
         kernel,
@@ -193,6 +210,23 @@
     )(own, after)
 
 
+def part_kernel(apart, out):
+    out[...] = apart[...]
+
+
+def first_part(apart, bins):
+    shape = (2, 128, bins)
+    return pl.pallas_call(
+        part_kernel,
+        grid=(1,),
+        in_specs=[pl.BlockSpec(shape, lambda i: (0, 0, 0))],
+        out_specs=pl.BlockSpec(shape, lambda i: (0, 0, 0)),
+        out_shape=jax.ShapeDtypeStruct(shape, apart.dtype),
+        compiler_params=pltpu.CompilerParams(vmem_limit_bytes=16 << 20),
+        name="first_part",
+    )(apart)
+
+
 def split_kernel(keep, received, *outs):
     total = keep[...] + received[...].astype(jnp.float32)
     half = total.shape[0] // 2
@@ -232,11 +266,18 @@
     bins = spectra.shape[3]
     slots = pair_first.shape[1]
     x_place = lax.axis_index("chan") % N_X
-    whitened = jnp.swapaxes(whiten(spectra[0]), 0, 1)
+    apart = jnp.swapaxes(spectra[0], 0, 1)
     starts = [sum(SIZES[:q]) for q in range(CHUNKS)]
-    own = [whitened[:, :, at : at + size] for at, size in zip(starts, SIZES)]
+    own = [apart[:, :, at : at + size] for at, size in zip(starts, SIZES)]
+    own[0] = first_part(apart, SIZES[0])
     crossed = [lax.ppermute(own[0], AXES, CROSS)]
-
+    scale = whitening_scale(hold(spectra, own[0])[0])
+    for q in range(1, CHUNKS):
+        own[q] = (own[q].astype(jnp.float32) * scale[None, :, None]).astype(jnp.bfloat16)
+    extra = scale_rows(scale, SIZES[1])
+    own[1] = jnp.concatenate([own[1], jnp.stack([extra, jnp.zeros_like(extra)])], 1)
+
+    pair_first, pair_second = (hold(p, crossed[0]) for p in (pair_first, pair_second))
     first_hot = (pair_first[0][:, None] == jnp.arange(128, dtype=jnp.int32)).astype(jnp.bfloat16)
     second_hot = (pair_second[0][:, None] == jnp.arange(512, dtype=jnp.int32)).astype(jnp.bfloat16)
     owners = pair_owner[0, :, 0]
@@ -250,36 +291,35 @@
     cosine, sine = lag_table(bins, windows_all)
     crossed.append(lax.ppermute(hold(own[1], cosine), AXES, CROSS))
 
-    acc = None
-    history, sums = [], []
     f32 = jnp.float32
+    whole = jax.ShapeDtypeStruct((slots, LAGS), f32)
+    ends = [jax.ShapeDtypeStruct((slots, 256), t) for t in (f32, jnp.bfloat16)]
+    halos, sums = [], []
+
+    def add_up(q):
+        kernel = first_kernel if q == 0 else last_kernel if q == CHUNKS - 1 else next_kernel
+        acc = sums[-1] if q else None
+        carriers = [] if q else halos[1]
+        outs = ends if q == CHUNKS - 1 else [whole]
+        return run_chunk(
+            kernel, q, first_hot, second_hot, halos[q], cosine, sine, acc, carriers, outs
+        )
+
     for q in range(CHUNKS):
         after = []
         if q >= 2:
-            after += [history[q - 2][d] for d in (1, 2, 3)]
+            after += halos[q - 2][1:]
         if LAG[q]:
             after.append(sums[q - LAG[q]])
-        if q >= 1:
-            after += [history[q - 1][d] for d in (2, 1, 3)[: FIRST_DONE[q]]]
         later = own[q + 2] if q + 2 < CHUNKS else None
         sources, copied = choose(x_place, crossed[q], own[q], later, after, CHOOSE_COST)
         if later is not None:
             crossed.append(lax.ppermute(copied, AXES, CROSS))
         ahead = {d: lax.ppermute(sources[d - 1], AXES, AROUND[d]) for d in (2, 1, 3)}
-        history.append(ahead)
-        halo = [own[q], ahead[1], ahead[2], ahead[3]]
-        operands = (q, first_hot, second_hot, halo, cosine, sine, acc)
-        whole = jax.ShapeDtypeStruct((slots, LAGS), f32)
-        if q == CHUNKS - 1:
-            outs = [
-                jax.ShapeDtypeStruct((slots, 256), f32),
-                jax.ShapeDtypeStruct((slots, 256), jnp.bfloat16),
-            ]
-            keep, send = run_chunk(last_kernel, *operands, outs)
-        else:
-            kernel = first_kernel if q == 0 else next_kernel
-            (acc,) = run_chunk(kernel, *operands, [whole])
-            sums.append(acc)
+        halos.append([own[q], ahead[1], ahead[2], ahead[3]])
+        if q:
+            sums += add_up(q - 1)
+    keep, send = add_up(CHUNKS - 1)
     received = lax.ppermute(send, AXES, OTHER_CORE)
     packed = (slots // 2, 128)
     pieces = call(

time: 129 us -> 128 us (level)
  local copies, waits for them, and re-layouts: 0.18 us -> 2.88 us
  starting transfers between devices: 30.6 us -> 33.3 us
  waiting for transfers between devices: 38.8 us -> 36.5 us
  blocking collectives: 25.6 us -> 23.7 us
  other arithmetic: 10 us -> 8.47 us
    ppermute x1, waiting for transfers between devices: 0.01 us -> 5.49 us  [on_device(): crossed.append(lax.ppermute(hold(own[1], cosine), AXES, CROSS))]
    ppermute x2, waiting for transfers between devices: 3.46 us -> 0.01 us  [on_device(): crossed.append(lax.ppermute(copied, AXES, CROSS))]
    unnamed x8 -> x11, local copies, waits for them, and re-layouts: 0.02 us -> 2.81 us
    ppermute x12, starting transfers between devices: 21.6 us -> 24.4 us  [on_device(): lax.ppermute(sources[d - 1], AXES, AROUND[d])]
    ppermute x12, waiting for transfers between devices: 6.42 us -> 4.24 us  [on_device(): lax.ppermute(sources[d - 1], AXES, AROUND[d])]
    ppermute x1, waiting for transfers between devices: 18.6 us -> 16.5 us  [on_device(): crossed = [lax.ppermute(own[0], AXES, CROSS)]]
    all_to_all x1, blocking collectives: 25.6 us -> 23.7 us  [on_device(): lax.all_to_all(buffer, 'chan', split_axis=0, concat_axis=0, tiled=True)]
    transpose x1 -> x0, other arithmetic: 1.7 us -> none  [on_device(): whitened = jnp.swapaxes(whiten(spectra[0]), 0, 1)]
  transfers between devices with their start and end apart: 20 -> 20, of which waited for: 10 -> 9; matrix products, arithmetic and copies ran while one was open for 6% -> 7% of each run, Pallas kernels for 12% -> 11%
where the time goes in v4:
time: 128 us
  waiting for transfers between devices  36.5 us (29%)
  starting transfers between devices  33.3 us (26%)
  blocking collectives  23.7 us (19%)
  Pallas kernels  21.1 us (16%)
  other arithmetic  8.47 us (7%)
  local copies, waits for them, and re-layouts  2.88 us (2%)
    ppermute x12, starting transfers between devices, on_device(): lax.ppermute(sources[d - 1], AXES, AROUND[d])  24.4 us
    all_to_all x1, blocking collectives, on_device(): lax.all_to_all(buffer, 'chan', split_axis=0, concat_axis=0, tiled=True)  23.7 us
    ppermute x1, waiting for transfers between devices, on_device(): crossed = [lax.ppermute(own[0], AXES, CROSS)]  16.5 us
    pallas_call x4, Pallas kernels, run_chunk(): pl.pallas_call(kernel, grid=(slots // ROWS,), in_specs=in_specs, out_spec...  16.1 us
    ppermute x3, waiting for transfers between devices, on_device(): lax.ppermute(pieces[k], AXES, OTHER_CHIP[k])  9.61 us
    ppermute x1, waiting for transfers between devices, on_device(): crossed.append(lax.ppermute(hold(own[1], cosine), AXES, CROSS))  5.49 us
    ppermute x12, waiting for transfers between devices, on_device(): lax.ppermute(sources[d - 1], AXES, AROUND[d])  4.24 us
    ppermute x3, starting transfers between devices, on_device(): lax.ppermute(pieces[k], AXES, OTHER_CHIP[k])  3.57 us
  transfers between devices with their start and end apart: 20, of which 9 were waited for; matrix products, arithmetic and copies ran while one was open for 7% of the time, Pallas kernels for 11%

profile of v4, /device:TPU:32, one launch (start us, length us, event | category | flops | bytes accessed | tf_op | source)
XLA Modules:
  0.0 127.6 jit_solution(15116602066615661203)
XLA Ops:
  0.0 1.6 %copy.9 = bf16[1,128,2,2048]{3,1,2,0:T(8,128)(2,1)S(1)} copy(bf16[1,128,2,2048]{3,2,1,0:T(2,128)(2,1)} %own.5) | data formatting | bytes 2097152 | tf_op args[0]
  1.6 1.3 %collective-permute-start = (bf16[2,128,512]{2,1,0:T(8,128)(2,1)S(1)}, bf16[2,128,512]{2,1,0:T(8,128)(2,1)S(1)}, u32[]{:S(2)}, u32[]{:S(2)}) collective-permute-start(bf16[2,128,512]{2,1,0:T(8,128)(2,1)S(1)} %first_part.1.after.own.rest_0_), channel_id=1, source_target_pairs={{32,0},{33,1},{34,2},{35,3},{36,4},{37,5},{38,6},{39,7},{40,8},{41... | collective-permute-start | bytes 786440 | tf_op jit(solution)/shard_map/ppermute | solution.py:273
  2.9 0.0 copy-start.1
  3.0 1.2 copy-done.1
  4.2 0.1 hold.6
  4.2 1.5 %multiply_reduce_fusion = f32[128]{0:T(128)S(1)} fusion(bf16[1,128,2,2048]{3,2,1,0:T(2,128)(2,1)S(1)} %hold.6), kind=kLoop, calls=%fused_computation.10 | loop fusion | flops 1572736 | bytes 1049088 | tf_op jit(solution)/shard_map/reduce_sum | solution.py:71
  5.8 0.3 fusion.28
  6.1 0.6 fusion.20
  6.7 0.1 reshape.281
  6.8 0.3 multiply_convert_fusion
  7.0 1.2 multiply_add_fusion
  8.2 0.3 fusion.2.after.rest_4_
  8.6 0.7 hold.7
  9.4 1.3 %collective-permute-start.1 = (bf16[2,144,512]{2,1,0:T(8,128)(2,1)}, bf16[2,144,512]{2,1,0:T(8,128)(2,1)}, u32[]{:S(2)}, u32[]{:S(2)}) collective-permute-start(bf16[2,144,512]{2,1,0:T(8,128)(2,1)} %hold.7), channel_id=1, source_target_pairs={{32,0},{33,1},{34,2},{35,3},{36,4},{37,5},{38,6},{39,7},{40,8},{41... | collective-permute-start | bytes 884744 | tf_op jit(solution)/shard_map/ppermute | solution.py:292
  10.7 1.7 %fusion.1.rest_5_ = bf16[2048,512]{1,0:T(8,128)(2,1)} fusion(f32[64,32,512]{2,1,0:T(8,128)S(1)} %get-tuple-element.48, f32[2048]{0:T(1024)S(1)} %neg.8), kind=kLoop, calls=%fused_computation.3 | loop fusion | flops 2097152 | bytes 6299648 | tf_op jit(solution)/shard_map/convert_element_type | solution.py:66
  12.3 16.5 %collective-permute-done.after.crossed = bf16[2,128,512]{2,1,0:T(8,128)(2,1)S(1)} collective-permute-done((bf16[2,128,512]{2,1,0:T(8,128)(2,1)S(1)}, bf16[2,128,512]{2,1,0:T(8,128)(2,1)S(1)}, u32[]{:S(2)}, u32[]{:S(2)}) %collective-permute-start) | collective-permute-done | bytes 262176 | tf_op jit(solution)/shard_map/ppermute | solution.py:273
  28.9 0.1 choose.5
  29.0 0.1 collective-permute-start.6
  29.1 3.5 %collective-permute-start.7 = (bf16[2,128,512]{2,1,0:T(8,128)(2,1)S(1)}, bf16[2,128,512]{2,1,0:T(8,128)(2,1)S(1)}, u32[]{:S(2)}, u32[]{:S(2)}) collective-permute-start(bf16[2,128,512]{2,1,0:T(8,128)(2,1)S(1)} %get-tuple-element.30), channel_id=1, source_target_pairs={{0,16},{1,17},{2,18},{3,19},{4,20},{5,21},{6,22},{7,23},{8,24},{9,... | collective-permute-start | bytes 786440 | tf_op jit(solution)/shard_map/ppermute | solution.py:318
  32.6 0.9 collective-permute-start.8
  33.5 0.2 fusion.9.first
  33.7 1.3 %collective-permute-start.12 = (bf16[2,128,512]{2,1,0:T(8,128)(2,1)S(1)}, bf16[2,128,512]{2,1,0:T(8,128)(2,1)S(1)}, u32[]{:S(2)}, u32[]{:S(2)}) collective-permute-start(bf16[2,128,512]{2,1,0:T(8,128)(2,1)S(1)} %get-tuple-element.35), channel_id=1, source_target_pairs={{32,0},{33,1},{34,2},{35,3},{36,4},{37,5},{38,6},{39,7},{40,8},{41... | collective-permute-start | bytes 786440 | tf_op jit(solution)/shard_map/ppermute | solution.py:317
  35.0 0.2 fusion.4.second
  35.3 5.5 %collective-permute-done.1.crossed = bf16[2,144,512]{2,1,0:T(8,128)(2,1)} collective-permute-done((bf16[2,144,512]{2,1,0:T(8,128)(2,1)}, bf16[2,144,512]{2,1,0:T(8,128)(2,1)}, u32[]{:S(2)}, u32[]{:S(2)}) %collective-permute-start.1) | collective-permute-done | bytes 294944 | tf_op jit(solution)/shard_map/ppermute | solution.py:292
  40.8 1.1 choose.4
  41.8 0.1 collective-permute-start.3
  41.9 0.0 collective-permute-done.6.rest_1_.rest_0_
  41.9 3.7 %collective-permute-start.4 = (bf16[2,144,512]{2,1,0:T(8,128)(2,1)S(1)}, bf16[2,144,512]{2,1,0:T(8,128)(2,1)S(1)}, u32[]{:S(2)}, u32[]{:S(2)}) collective-permute-start(bf16[2,144,512]{2,1,0:T(8,128)(2,1)S(1)} %get-tuple-element.27), channel_id=1, source_target_pairs={{0,16},{1,17},{2,18},{3,19},{4,20},{5,21},{6,22},{7,23},{8,24},{9,... | collective-permute-start | bytes 884744 | tf_op jit(solution)/shard_map/ppermute | solution.py:318
  45.6 0.0 collective-permute-done.7.rest_2_.rest_1_
  45.6 0.9 collective-permute-start.5
  46.5 0.0 collective-permute-done.8.rest_3_.rest_2_
  46.5 1.4 %collective-permute-start.2 = (bf16[2,128,512]{2,1,0:T(8,128)(2,1)S(1)}, bf16[2,128,512]{2,1,0:T(8,128)(2,1)S(1)}, u32[]{:S(2)}, u32[]{:S(2)}) collective-permute-start(bf16[2,128,512]{2,1,0:T(8,128)(2,1)S(1)} %get-tuple-element.25), channel_id=1, source_target_pairs={{32,0},{33,1},{34,2},{35,3},{36,4},{37,5},{38,6},{39,7},{40,8},{41... | collective-permute-start | bytes 786440 | tf_op jit(solution)/shard_map/ppermute | solution.py:317
  47.9 0.1 choose.7
  48.0 1.8 %collective-permute-start.13 = (bf16[2,128,512]{2,1,0:T(8,128)(2,1)S(1)}, bf16[2,128,512]{2,1,0:T(8,128)(2,1)S(1)}, u32[]{:S(2)}, u32[]{:S(2)}) collective-permute-start(bf16[2,128,512]{2,1,0:T(8,128)(2,1)S(1)} %get-tuple-element.36), channel_id=1, source_target_pairs={{0,24},{1,25},{2,26},{3,27},{4,28},{5,29},{6,30},{7,31},{8,0},{9,1... | collective-permute-start | bytes 786440 | tf_op jit(solution)/shard_map/ppermute | solution.py:318
  49.9 2.0 %collective-permute-done.3.rest_7_.rest_0_.rest_1_ = bf16[2,144,512]{2,1,0:T(8,128)(2,1)S(1)} collective-permute-done((bf16[2,144,512]{2,1,0:T(8,128)(2,1)S(1)}, bf16[2,144,512]{2,1,0:T(8,128)(2,1)S(1)}, u32[]{:S(2)}, u32[]{:S(2)}) %collective-permute-start.3) | collective-permute-done | bytes 294944 | tf_op jit(solution)/shard_map/ppermute | solution.py:318
  51.9 5.3 %collective-permute-start.14 = (bf16[2,128,512]{2,1,0:T(8,128)(2,1)S(1)}, bf16[2,128,512]{2,1,0:T(8,128)(2,1)S(1)}, u32[]{:S(2)}, u32[]{:S(2)}) collective-permute-start(bf16[2,128,512]{2,1,0:T(8,128)(2,1)S(1)} %get-tuple-element.37), channel_id=1, source_target_pairs={{0,16},{1,17},{2,18},{3,19},{4,20},{5,21},{6,22},{7,23},{8,24},{9,... | collective-permute-start | bytes 786440 | tf_op jit(solution)/shard_map/ppermute | solution.py:318
  57.2 0.0 collective-permute-done.4.rest_8_.rest_1_.rest_2_
  57.2 3.6 %collective-permute-start.15 = (bf16[2,128,512]{2,1,0:T(8,128)(2,1)S(1)}, bf16[2,128,512]{2,1,0:T(8,128)(2,1)S(1)}, u32[]{:S(2)}, u32[]{:S(2)}) collective-permute-start(bf16[2,128,512]{2,1,0:T(8,128)(2,1)S(1)} %get-tuple-element.38), channel_id=1, source_target_pairs={{0,8},{1,9},{2,10},{3,11},{4,12},{5,13},{6,14},{7,15},{8,16},{9,17... | collective-permute-start | bytes 786440 | tf_op jit(solution)/shard_map/ppermute | solution.py:318
  60.8 1.7 %collective-permute-done.5.rest_9_.rest_2_.rest_3_ = bf16[2,144,512]{2,1,0:T(8,128)(2,1)S(1)} collective-permute-done((bf16[2,144,512]{2,1,0:T(8,128)(2,1)S(1)}, bf16[2,144,512]{2,1,0:T(8,128)(2,1)S(1)}, u32[]{:S(2)}, u32[]{:S(2)}) %collective-permute-start.5) | collective-permute-done | bytes 294944 | tf_op jit(solution)/shard_map/ppermute | solution.py:318
  62.5 3.9 %correlate.4.rest_3_.rest_6_ = f32[1024,512]{1,0:T(8,128)S(1)} custom-call(bf16[1024,128]{1,0:T(8,128)(2,1)S(1)} %fusion.9.first, bf16[1024,512]{1,0:T(8,128)(2,1)S(1)} %fusion.4.second, bf16[2,128,512]{2,1,0:T(8,128)(2,1)S(1)} %first_part.1.after.own.rest_0_, bf16[2,128,512]{2,1,0:T(8,128)(2,1)S(1)} %collective-permute-done.6.rest_1_.rest_0_, ...), custom_call_target="tpu_custom_call" | custom-call | flops 200000000 | bytes 1048576 | tf_op jit(solution)/shard_map/correlate/pallas_call | solution.py:150
  66.4 0.1 choose.6
  66.5 1.2 collective-permute-start.10
  67.7 0.0 collective-permute-start.11
  67.7 0.0 collective-permute-done.13.rest_1_
  67.7 3.2 %collective-permute-start.9 = (bf16[2,128,512]{2,1,0:T(8,128)(2,1)S(1)}, bf16[2,128,512]{2,1,0:T(8,128)(2,1)S(1)}, u32[]{:S(2)}, u32[]{:S(2)}) collective-permute-start(bf16[2,128,512]{2,1,0:T(8,128)(2,1)S(1)} %get-tuple-element.32), channel_id=1, source_target_pairs={{0,24},{1,25},{2,26},{3,27},{4,28},{5,29},{6,30},{7,31},{8,0},{9,1... | collective-permute-start | bytes 786440 | tf_op jit(solution)/shard_map/ppermute | solution.py:318
  71.0 4.1 %correlate.5.rest_6_ = f32[1024,512]{1,0:T(8,128)S(1)} custom-call(bf16[1024,128]{1,0:T(8,128)(2,1)S(1)} %fusion.9.first, bf16[1024,512]{1,0:T(8,128)(2,1)S(1)} %fusion.4.second, bf16[2,144,512]{2,1,0:T(8,128)(2,1)S(1)} %fusion.10.own.rest_6_.rest_0_, bf16[2,144,512]{2,1,0:T(8,128)(2,1)S(1)} %collective-permute-done.3.rest_7_.rest_0_.rest_1_, ...), custom_call_target="tpu_custom_call" | custom-call | flops 200000000 | bytes 1048576 | tf_op jit(solution)/shard_map/correlate/pallas_call | solution.py:150
  75.1 4.1 %correlate.6.rest_6_ = f32[1024,512]{1,0:T(8,128)S(1)} custom-call(bf16[1024,128]{1,0:T(8,128)(2,1)S(1)} %fusion.9.first, bf16[1024,512]{1,0:T(8,128)(2,1)S(1)} %fusion.4.second, bf16[2,128,512]{2,1,0:T(8,128)(2,1)S(1)} %get-tuple-element.45.rest_0_.own, bf16[2,128,512]{2,1,0:T(8,128)(2,1)S(1)} %collective-permute-done.13.rest_1_, ...), custom_call_target="tpu_custom_call" | custom-call | flops 200000000 | bytes 1048576 | tf_op jit(solution)/shard_map/correlate/pallas_call | solution.py:150
  79.2 0.0 copy-start.4
  79.2 0.5 collective-permute-done.11.rest_3_
  79.8 4.0 %correlate.7 = (f32[1024,256]{1,0:T(8,128)S(1)}, bf16[1024,256]{1,0:T(8,128)(2,1)S(1)}) custom-call(bf16[1024,128]{1,0:T(8,128)(2,1)S(1)} %fusion.9.first, bf16[1024,512]{1,0:T(8,128)(2,1)S(1)} %fusion.4.second, bf16[2,128,512]{2,1,0:T(8,128)(2,1)S(1)} %get-tuple-element.47.rest_0_.own, bf16[2,128,512]{2,1,0:T(8,128)(2,1)S(1)} %collective-permute-done.9.rest_1_, ...), custom_call_target="tpu_custom_call" | custom-call | flops 200000000 | bytes 1048576 | tf_op jit(solution)/shard_map/correlate/pallas_call | solution.py:150
  83.8 0.1 collective-permute-start.16
  84.6 0.5 fusion.7
  85.1 0.7 collective-permute-done.16.received
  85.8 0.2 split_kernel.1
  86.1 0.1 collective-permute-start.17
  86.2 2.9 %collective-permute-start.18 = (bf16[512,128]{1,0:T(8,128)(2,1)S(1)}, bf16[512,128]{1,0:T(8,128)(2,1)S(1)}, u32[]{:S(2)}, u32[]{:S(2)}) collective-permute-start(bf16[512,128]{1,0:T(8,128)(2,1)S(1)} %get-tuple-element.43), channel_id=1, source_target_pairs={{0,4},{1,5},{2,6},{3,7},{4,0},{5,1},{6,2},{7,3},{8,12},{9,13},{10,... | collective-permute-start | bytes 393224 | tf_op jit(solution)/shard_map/ppermute | solution.py:331
  89.0 0.6 collective-permute-start.19
  89.6 2.1 %fusion.hot = bf16[2048,1024]{1,0:T(8,128)(2,1)S(1)} fusion(s32[1024]{0:T(1024)S(1)} %add_select_fusion.2), kind=kLoop, calls=%fused_computation.1 | loop fusion | flops 4194304 | bytes 4198400 | tf_op jit(solution)/shard_map/convert_element_type | solution.py:290
  91.7 0.8 collective-permute-done.17.one
  92.5 5.9 %collective-permute-done.18.two = bf16[512,128]{1,0:T(8,128)(2,1)S(1)} collective-permute-done((bf16[512,128]{1,0:T(8,128)(2,1)S(1)}, bf16[512,128]{1,0:T(8,128)(2,1)S(1)}, u32[]{:S(2)}, u32[]{:S(2)}) %collective-permute-start.18) | collective-permute-done | bytes 131104 | tf_op jit(solution)/shard_map/ppermute | solution.py:331
  98.4 2.9 %collective-permute-done.19.three = bf16[512,128]{1,0:T(8,128)(2,1)S(1)} collective-permute-done((bf16[512,128]{1,0:T(8,128)(2,1)S(1)}, bf16[512,128]{1,0:T(8,128)(2,1)S(1)}, u32[]{:S(2)}, u32[]{:S(2)}) %collective-permute-start.19) | collective-permute-done | bytes 131104 | tf_op jit(solution)/shard_map/ppermute | solution.py:331
  101.3 1.4 %route_kernel.1 = bf16[32,32,128]{2,1,0:T(8,128)(2,1)S(1)} custom-call(bf16[2048,1024]{1,0:T(8,128)(2,1)S(1)} %fusion.hot, f32[512,128]{1,0:T(8,128)S(1)} %get-tuple-element.41.keep, bf16[512,128]{1,0:T(8,128)(2,1)S(1)} %collective-permute-done.17.one, bf16[512,128]{1,0:T(8,128)(2,1)S(1)} %collective-permute-done.18.two, ...), custom_call_target="tpu_custom_call" | custom-call | tf_op jit(solution)/shard_map/route_kernel/pallas_call | solution.py:256
  102.8 23.7 %all_to_all.5.routed = bf16[32,32,128]{2,1,0:T(8,128)(2,1)S(1)} all-to-all(bf16[32,32,128]{2,1,0:T(8,128)(2,1)S(1)} %route_kernel.1), channel_id=1, replica_groups=mesh['chan'=32,'win'=8] {'chan'}, dimensions={0} | all-to-all | bytes 524288 | tf_op jit(solution)/shard_map/all_to_all | solution.py:335
  126.5 1.1 unpack_kernel.1
  (25 shorter events, 0.1 us)
Async XLA Ops:
  1.6 27.3 %collective-permute-start = (bf16[2,128,512]{2,1,0:T(8,128)(2,1)S(1)}, bf16[2,128,512]{2,1,0:T(8,128)(2,1)S(1)}, u32[]{:S(2)}, u32[]{:S(2)}) collective-permute-start(bf16[2,128,512]{2,1,0:T(8,128)(2,1)S(1)} %first_part.1.after.own.rest_0_), channel_id=1, source_target_pairs={{32,0},{33,1},{34,2},{35,3},{36,4},{37,5},{38,6},{39,7},{40,8},{41... | collective-permute-start | bytes 786440 | tf_op jit(solution)/shard_map/ppermute | solution.py:273
  2.9 1.2 copy-start.1
  9.4 31.4 %collective-permute-start.1 = (bf16[2,144,512]{2,1,0:T(8,128)(2,1)}, bf16[2,144,512]{2,1,0:T(8,128)(2,1)}, u32[]{:S(2)}, u32[]{:S(2)}) collective-permute-start(bf16[2,144,512]{2,1,0:T(8,128)(2,1)} %hold.7), channel_id=1, source_target_pairs={{32,0},{33,1},{34,2},{35,3},{36,4},{37,5},{38,6},{39,7},{40,8},{41... | collective-permute-start | bytes 884744 | tf_op jit(solution)/shard_map/ppermute | solution.py:292
  28.9 4.6 %copy-start.2 = (s32[1,1024]{1,0:T(1,128)S(1)}, s32[1,1024]{1,0:T(1,128)}, u32[]{:S(2)}) copy-start(s32[1,1024]{1,0:T(1,128)} %own.3) | copy-start | bytes 12292
  28.9 6.1 %copy-start.3 = (s32[1,1024]{1,0:T(1,128)S(1)}, s32[1,1024]{1,0:T(1,128)}, u32[]{:S(2)}) copy-start(s32[1,1024]{1,0:T(1,128)} %own.4) | copy-start | bytes 12292
  29.0 13.0 %collective-permute-start.6 = (bf16[2,128,512]{2,1,0:T(8,128)(2,1)S(1)}, bf16[2,128,512]{2,1,0:T(8,128)(2,1)S(1)}, u32[]{:S(2)}, u32[]{:S(2)}) collective-permute-start(bf16[2,128,512]{2,1,0:T(8,128)(2,1)S(1)} %get-tuple-element.29), channel_id=1, source_target_pairs={{0,24},{1,25},{2,26},{3,27},{4,28},{5,29},{6,30},{7,31},{8,0},{9,1... | collective-permute-start | bytes 786440 | tf_op jit(solution)/shard_map/ppermute | solution.py:318
  29.1 16.6 %collective-permute-start.7 = (bf16[2,128,512]{2,1,0:T(8,128)(2,1)S(1)}, bf16[2,128,512]{2,1,0:T(8,128)(2,1)S(1)}, u32[]{:S(2)}, u32[]{:S(2)}) collective-permute-start(bf16[2,128,512]{2,1,0:T(8,128)(2,1)S(1)} %get-tuple-element.30), channel_id=1, source_target_pairs={{0,16},{1,17},{2,18},{3,19},{4,20},{5,21},{6,22},{7,23},{8,24},{9,... | collective-permute-start | bytes 786440 | tf_op jit(solution)/shard_map/ppermute | solution.py:318
  32.6 13.9 %collective-permute-start.8 = (bf16[2,128,512]{2,1,0:T(8,128)(2,1)S(1)}, bf16[2,128,512]{2,1,0:T(8,128)(2,1)S(1)}, u32[]{:S(2)}, u32[]{:S(2)}) collective-permute-start(bf16[2,128,512]{2,1,0:T(8,128)(2,1)S(1)} %get-tuple-element.31), channel_id=1, source_target_pairs={{0,8},{1,9},{2,10},{3,11},{4,12},{5,13},{6,14},{7,15},{8,16},{9,17... | collective-permute-start | bytes 786440 | tf_op jit(solution)/shard_map/ppermute | solution.py:318
  33.7 14.2 %collective-permute-start.12 = (bf16[2,128,512]{2,1,0:T(8,128)(2,1)S(1)}, bf16[2,128,512]{2,1,0:T(8,128)(2,1)S(1)}, u32[]{:S(2)}, u32[]{:S(2)}) collective-permute-start(bf16[2,128,512]{2,1,0:T(8,128)(2,1)S(1)} %get-tuple-element.35), channel_id=1, source_target_pairs={{32,0},{33,1},{34,2},{35,3},{36,4},{37,5},{38,6},{39,7},{40,8},{41... | collective-permute-start | bytes 786440 | tf_op jit(solution)/shard_map/ppermute | solution.py:317
  41.8 10.0 %collective-permute-start.3 = (bf16[2,144,512]{2,1,0:T(8,128)(2,1)S(1)}, bf16[2,144,512]{2,1,0:T(8,128)(2,1)S(1)}, u32[]{:S(2)}, u32[]{:S(2)}) collective-permute-start(bf16[2,144,512]{2,1,0:T(8,128)(2,1)S(1)} %get-tuple-element.26), channel_id=1, source_target_pairs={{0,24},{1,25},{2,26},{3,27},{4,28},{5,29},{6,30},{7,31},{8,0},{9,1... | collective-permute-start | bytes 884744 | tf_op jit(solution)/shard_map/ppermute | solution.py:318
  41.9 15.3 %collective-permute-start.4 = (bf16[2,144,512]{2,1,0:T(8,128)(2,1)S(1)}, bf16[2,144,512]{2,1,0:T(8,128)(2,1)S(1)}, u32[]{:S(2)}, u32[]{:S(2)}) collective-permute-start(bf16[2,144,512]{2,1,0:T(8,128)(2,1)S(1)} %get-tuple-element.27), channel_id=1, source_target_pairs={{0,16},{1,17},{2,18},{3,19},{4,20},{5,21},{6,22},{7,23},{8,24},{9,... | collective-permute-start | bytes 884744 | tf_op jit(solution)/shard_map/ppermute | solution.py:318
  45.6 16.8 %collective-permute-start.5 = (bf16[2,144,512]{2,1,0:T(8,128)(2,1)S(1)}, bf16[2,144,512]{2,1,0:T(8,128)(2,1)S(1)}, u32[]{:S(2)}, u32[]{:S(2)}) collective-permute-start(bf16[2,144,512]{2,1,0:T(8,128)(2,1)S(1)} %get-tuple-element.28), channel_id=1, source_target_pairs={{0,8},{1,9},{2,10},{3,11},{4,12},{5,13},{6,14},{7,15},{8,16},{9,17... | collective-permute-start | bytes 884744 | tf_op jit(solution)/shard_map/ppermute | solution.py:318
  46.5 15.9 %copy-start = (bf16[2048,512]{1,0:T(8,128)(2,1)S(1)}, bf16[2048,512]{1,0:T(8,128)(2,1)}, u32[]{:S(2)}) copy-start(bf16[2048,512]{1,0:T(8,128)(2,1)} %fusion.1.rest_5_) | copy-start | bytes 6291460
  46.5 19.9 %collective-permute-start.2 = (bf16[2,128,512]{2,1,0:T(8,128)(2,1)S(1)}, bf16[2,128,512]{2,1,0:T(8,128)(2,1)S(1)}, u32[]{:S(2)}, u32[]{:S(2)}) collective-permute-start(bf16[2,128,512]{2,1,0:T(8,128)(2,1)S(1)} %get-tuple-element.25), channel_id=1, source_target_pairs={{32,0},{33,1},{34,2},{35,3},{36,4},{37,5},{38,6},{39,7},{40,8},{41... | collective-permute-start | bytes 786440 | tf_op jit(solution)/shard_map/ppermute | solution.py:317
  48.0 19.7 %collective-permute-start.13 = (bf16[2,128,512]{2,1,0:T(8,128)(2,1)S(1)}, bf16[2,128,512]{2,1,0:T(8,128)(2,1)S(1)}, u32[]{:S(2)}, u32[]{:S(2)}) collective-permute-start(bf16[2,128,512]{2,1,0:T(8,128)(2,1)S(1)} %get-tuple-element.36), channel_id=1, source_target_pairs={{0,24},{1,25},{2,26},{3,27},{4,28},{5,29},{6,30},{7,31},{8,0},{9,1... | collective-permute-start | bytes 786440 | tf_op jit(solution)/shard_map/ppermute | solution.py:318
  51.9 23.2 %collective-permute-start.14 = (bf16[2,128,512]{2,1,0:T(8,128)(2,1)S(1)}, bf16[2,128,512]{2,1,0:T(8,128)(2,1)S(1)}, u32[]{:S(2)}, u32[]{:S(2)}) collective-permute-start(bf16[2,128,512]{2,1,0:T(8,128)(2,1)S(1)} %get-tuple-element.37), channel_id=1, source_target_pairs={{0,16},{1,17},{2,18},{3,19},{4,20},{5,21},{6,22},{7,23},{8,24},{9,... | collective-permute-start | bytes 786440 | tf_op jit(solution)/shard_map/ppermute | solution.py:318
  57.2 17.9 %collective-permute-start.15 = (bf16[2,128,512]{2,1,0:T(8,128)(2,1)S(1)}, bf16[2,128,512]{2,1,0:T(8,128)(2,1)S(1)}, u32[]{:S(2)}, u32[]{:S(2)}) collective-permute-start(bf16[2,128,512]{2,1,0:T(8,128)(2,1)S(1)} %get-tuple-element.38), channel_id=1, source_target_pairs={{0,8},{1,9},{2,10},{3,11},{4,12},{5,13},{6,14},{7,15},{8,16},{9,17... | collective-permute-start | bytes 786440 | tf_op jit(solution)/shard_map/ppermute | solution.py:318
  66.5 12.7 %collective-permute-start.10 = (bf16[2,128,512]{2,1,0:T(8,128)(2,1)S(1)}, bf16[2,128,512]{2,1,0:T(8,128)(2,1)S(1)}, u32[]{:S(2)}, u32[]{:S(2)}) collective-permute-start(bf16[2,128,512]{2,1,0:T(8,128)(2,1)S(1)} %get-tuple-element.33), channel_id=1, source_target_pairs={{0,16},{1,17},{2,18},{3,19},{4,20},{5,21},{6,22},{7,23},{8,24},{9,... | collective-permute-start | bytes 786440 | tf_op jit(solution)/shard_map/ppermute | solution.py:318
  67.7 12.0 %collective-permute-start.11 = (bf16[2,128,512]{2,1,0:T(8,128)(2,1)S(1)}, bf16[2,128,512]{2,1,0:T(8,128)(2,1)S(1)}, u32[]{:S(2)}, u32[]{:S(2)}) collective-permute-start(bf16[2,128,512]{2,1,0:T(8,128)(2,1)S(1)} %get-tuple-element.34), channel_id=1, source_target_pairs={{0,8},{1,9},{2,10},{3,11},{4,12},{5,13},{6,14},{7,15},{8,16},{9,17... | collective-permute-start | bytes 786440 | tf_op jit(solution)/shard_map/ppermute | solution.py:318
  67.7 12.0 %collective-permute-start.9 = (bf16[2,128,512]{2,1,0:T(8,128)(2,1)S(1)}, bf16[2,128,512]{2,1,0:T(8,128)(2,1)S(1)}, u32[]{:S(2)}, u32[]{:S(2)}) collective-permute-start(bf16[2,128,512]{2,1,0:T(8,128)(2,1)S(1)} %get-tuple-element.32), channel_id=1, source_target_pairs={{0,24},{1,25},{2,26},{3,27},{4,28},{5,29},{6,30},{7,31},{8,0},{9,1... | collective-permute-start | bytes 786440 | tf_op jit(solution)/shard_map/ppermute | solution.py:318
  79.2 5.4 %copy-start.4 = (s32[1,1024,1]{1,2,0:T(1,128)S(1)}, s32[1,1024,1]{1,2,0:T(1,128)}, u32[]{:S(2)}) copy-start(s32[1,1024,1]{1,2,0:T(1,128)} %param.9) | copy-start | bytes 12292
  83.8 2.0 %collective-permute-start.16 = (bf16[1024,256]{1,0:T(8,128)(2,1)S(1)}, bf16[1024,256]{1,0:T(8,128)(2,1)S(1)}, u32[]{:S(2)}, u32[]{:S(2)}) collective-permute-start(bf16[1024,256]{1,0:T(8,128)(2,1)S(1)} %get-tuple-element.40), channel_id=1, source_target_pairs={{0,1},{1,0},{2,3},{3,2},{4,5},{5,4},{6,7},{7,6},{8,9},{9,8},{10,11... | collective-permute-start | bytes 1572872 | tf_op jit(solution)/shard_map/ppermute | solution.py:323
  86.1 6.4 %collective-permute-start.17 = (bf16[512,128]{1,0:T(8,128)(2,1)S(1)}, bf16[512,128]{1,0:T(8,128)(2,1)S(1)}, u32[]{:S(2)}, u32[]{:S(2)}) collective-permute-start(bf16[512,128]{1,0:T(8,128)(2,1)S(1)} %get-tuple-element.42), channel_id=1, source_target_pairs={{0,2},{1,3},{2,0},{3,1},{4,6},{5,7},{6,4},{7,5},{8,10},{9,11},{10,... | collective-permute-start | bytes 393224 | tf_op jit(solution)/shard_map/ppermute | solution.py:331
  86.2 12.3 %collective-permute-start.18 = (bf16[512,128]{1,0:T(8,128)(2,1)S(1)}, bf16[512,128]{1,0:T(8,128)(2,1)S(1)}, u32[]{:S(2)}, u32[]{:S(2)}) collective-permute-start(bf16[512,128]{1,0:T(8,128)(2,1)S(1)} %get-tuple-element.43), channel_id=1, source_target_pairs={{0,4},{1,5},{2,6},{3,7},{4,0},{5,1},{6,2},{7,3},{8,12},{9,13},{10,... | collective-permute-start | bytes 393224 | tf_op jit(solution)/shard_map/ppermute | solution.py:331
  89.0 12.3 %collective-permute-start.19 = (bf16[512,128]{1,0:T(8,128)(2,1)S(1)}, bf16[512,128]{1,0:T(8,128)(2,1)S(1)}, u32[]{:S(2)}, u32[]{:S(2)}) collective-permute-start(bf16[512,128]{1,0:T(8,128)(2,1)S(1)} %get-tuple-element.44), channel_id=1, source_target_pairs={{0,6},{1,7},{2,4},{3,5},{4,2},{5,3},{6,0},{7,1},{8,14},{9,15},{10,... | collective-permute-start | bytes 393224 | tf_op jit(solution)/shard_map/ppermute | solution.py:331

commit v5 on v4

--- a/solution.py
+++ b/solution.py
@@ -14,7 +14,7 @@
 CHUNKS = len(SIZES)
 LAG = (0, 0, 0, 3)
 CHOOSE_COST = 5_000_000_000
-ROWS = 256
+ROWS = 1024
 AXES = ("chan", "win")
 N_X = 4
 N_CORE = 2
@@ -92,7 +92,7 @@
     left_hot = first_ref[...]
     right_hot = second_ref[...]
     bins = blocks.shape[2]
-    step = bins
+    step = 256
     for start in range(0, bins, step):
         at = pl.ds(start, step)
         left = [dot(left_hot, blocks[part, :128, at]) for part in range(2)]

time: 128 us -> 127 us (level)
  Pallas kernels: 21.1 us -> 16.4 us
  waiting for transfers between devices: 36.5 us -> 40.1 us
    pallas_call x4, Pallas kernels: 16.1 us -> 11.5 us  [run_chunk(): pl.pallas_call(kernel, grid=(slots // ROWS,), in_specs=in_specs, out_spec...]
    ppermute x12, waiting for transfers between devices: 4.24 us -> 7.75 us  [on_device(): lax.ppermute(sources[d - 1], AXES, AROUND[d])]
  transfers between devices with their start and end apart: 20 -> 20, of which waited for: 9 -> 11; matrix products, arithmetic and copies ran while one was open for 7% -> 7% of each run, Pallas kernels for 11% -> 8%
where the time goes in v5:
time: 127 us
  waiting for transfers between devices  40.1 us (32%)
  starting transfers between devices  33.5 us (26%)
  blocking collectives  23.6 us (19%)
  Pallas kernels  16.4 us (13%)
  other arithmetic  8.47 us (7%)
  local copies, waits for them, and re-layouts  2.88 us (2%)
    ppermute x12, starting transfers between devices, on_device(): lax.ppermute(sources[d - 1], AXES, AROUND[d])  24.4 us
    all_to_all x1, blocking collectives, on_device(): lax.all_to_all(buffer, 'chan', split_axis=0, concat_axis=0, tiled=True)  23.6 us
    ppermute x1, waiting for transfers between devices, on_device(): crossed = [lax.ppermute(own[0], AXES, CROSS)]  16.5 us
    pallas_call x4, Pallas kernels, run_chunk(): pl.pallas_call(kernel, grid=(slots // ROWS,), in_specs=in_specs, out_spec...  11.5 us
    ppermute x3, waiting for transfers between devices, on_device(): lax.ppermute(pieces[k], AXES, OTHER_CHIP[k])  9.61 us
    ppermute x12, waiting for transfers between devices, on_device(): lax.ppermute(sources[d - 1], AXES, AROUND[d])  7.75 us
    ppermute x1, waiting for transfers between devices, on_device(): crossed.append(lax.ppermute(hold(own[1], cosine), AXES, CROSS))  5.49 us
    ppermute x3, starting transfers between devices, on_device(): lax.ppermute(pieces[k], AXES, OTHER_CHIP[k])  3.57 us
  transfers between devices with their start and end apart: 20, of which 11 were waited for; matrix products, arithmetic and copies ran while one was open for 7% of the time, Pallas kernels for 8%

profile of v5, /device:TPU:32, one launch (start us, length us, event | category | flops | bytes accessed | tf_op | source)
XLA Modules:
  0.0 126.6 jit_solution(8352347142576515099)
XLA Ops:
  0.0 1.6 %copy.9 = bf16[1,128,2,2048]{3,1,2,0:T(8,128)(2,1)S(1)} copy(bf16[1,128,2,2048]{3,2,1,0:T(2,128)(2,1)} %own.5) | data formatting | bytes 2097152 | tf_op args[0]
  1.6 1.3 %collective-permute-start = (bf16[2,128,512]{2,1,0:T(8,128)(2,1)S(1)}, bf16[2,128,512]{2,1,0:T(8,128)(2,1)S(1)}, u32[]{:S(2)}, u32[]{:S(2)}) collective-permute-start(bf16[2,128,512]{2,1,0:T(8,128)(2,1)S(1)} %first_part.1.after.own.rest_0_), channel_id=1, source_target_pairs={{32,0},{33,1},{34,2},{35,3},{36,4},{37,5},{38,6},{39,7},{40,8},{41... | collective-permute-start | bytes 786440 | tf_op jit(solution)/shard_map/ppermute | solution.py:273
  2.9 0.0 copy-start.1
  3.0 1.2 copy-done.1
  4.2 0.1 hold.6
  4.2 1.5 %multiply_reduce_fusion = f32[128]{0:T(128)S(1)} fusion(bf16[1,128,2,2048]{3,2,1,0:T(2,128)(2,1)S(1)} %hold.6), kind=kLoop, calls=%fused_computation.10 | loop fusion | flops 1572736 | bytes 1049088 | tf_op jit(solution)/shard_map/reduce_sum | solution.py:71
  5.8 0.3 fusion.28
  6.1 0.6 fusion.20
  6.7 0.1 reshape.281
  6.8 0.3 multiply_convert_fusion
  7.0 1.2 multiply_add_fusion
  8.2 0.3 fusion.2.after.rest_4_
  8.6 0.7 hold.7
  9.4 1.3 %collective-permute-start.1 = (bf16[2,144,512]{2,1,0:T(8,128)(2,1)}, bf16[2,144,512]{2,1,0:T(8,128)(2,1)}, u32[]{:S(2)}, u32[]{:S(2)}) collective-permute-start(bf16[2,144,512]{2,1,0:T(8,128)(2,1)} %hold.7), channel_id=1, source_target_pairs={{32,0},{33,1},{34,2},{35,3},{36,4},{37,5},{38,6},{39,7},{40,8},{41... | collective-permute-start | bytes 884744 | tf_op jit(solution)/shard_map/ppermute | solution.py:292
  10.7 1.7 %fusion.1.rest_5_ = bf16[2048,512]{1,0:T(8,128)(2,1)} fusion(f32[64,32,512]{2,1,0:T(8,128)S(1)} %get-tuple-element.48, f32[2048]{0:T(1024)S(1)} %neg.8), kind=kLoop, calls=%fused_computation.3 | loop fusion | flops 2097152 | bytes 6299648 | tf_op jit(solution)/shard_map/convert_element_type | solution.py:66
  12.3 16.5 %collective-permute-done.after.crossed = bf16[2,128,512]{2,1,0:T(8,128)(2,1)S(1)} collective-permute-done((bf16[2,128,512]{2,1,0:T(8,128)(2,1)S(1)}, bf16[2,128,512]{2,1,0:T(8,128)(2,1)S(1)}, u32[]{:S(2)}, u32[]{:S(2)}) %collective-permute-start) | collective-permute-done | bytes 262176 | tf_op jit(solution)/shard_map/ppermute | solution.py:273
  28.9 0.1 choose.5
  29.0 0.1 collective-permute-start.6
  29.1 3.5 %collective-permute-start.7 = (bf16[2,128,512]{2,1,0:T(8,128)(2,1)S(1)}, bf16[2,128,512]{2,1,0:T(8,128)(2,1)S(1)}, u32[]{:S(2)}, u32[]{:S(2)}) collective-permute-start(bf16[2,128,512]{2,1,0:T(8,128)(2,1)S(1)} %get-tuple-element.30), channel_id=1, source_target_pairs={{0,16},{1,17},{2,18},{3,19},{4,20},{5,21},{6,22},{7,23},{8,24},{9,... | collective-permute-start | bytes 786440 | tf_op jit(solution)/shard_map/ppermute | solution.py:318
  32.6 0.9 collective-permute-start.8
  33.5 0.2 fusion.9.first
  33.7 1.3 %collective-permute-start.12 = (bf16[2,128,512]{2,1,0:T(8,128)(2,1)S(1)}, bf16[2,128,512]{2,1,0:T(8,128)(2,1)S(1)}, u32[]{:S(2)}, u32[]{:S(2)}) collective-permute-start(bf16[2,128,512]{2,1,0:T(8,128)(2,1)S(1)} %get-tuple-element.35), channel_id=1, source_target_pairs={{32,0},{33,1},{34,2},{35,3},{36,4},{37,5},{38,6},{39,7},{40,8},{41... | collective-permute-start | bytes 786440 | tf_op jit(solution)/shard_map/ppermute | solution.py:317
  35.0 0.2 fusion.4.second
  35.3 5.5 %collective-permute-done.1.crossed = bf16[2,144,512]{2,1,0:T(8,128)(2,1)} collective-permute-done((bf16[2,144,512]{2,1,0:T(8,128)(2,1)}, bf16[2,144,512]{2,1,0:T(8,128)(2,1)}, u32[]{:S(2)}, u32[]{:S(2)}) %collective-permute-start.1) | collective-permute-done | bytes 294944 | tf_op jit(solution)/shard_map/ppermute | solution.py:292
  40.8 1.1 choose.4
  41.8 0.1 collective-permute-start.3
  41.9 3.7 %collective-permute-start.4 = (bf16[2,144,512]{2,1,0:T(8,128)(2,1)S(1)}, bf16[2,144,512]{2,1,0:T(8,128)(2,1)S(1)}, u32[]{:S(2)}, u32[]{:S(2)}) collective-permute-start(bf16[2,144,512]{2,1,0:T(8,128)(2,1)S(1)} %get-tuple-element.27), channel_id=1, source_target_pairs={{0,16},{1,17},{2,18},{3,19},{4,20},{5,21},{6,22},{7,23},{8,24},{9,... | collective-permute-start | bytes 884744 | tf_op jit(solution)/shard_map/ppermute | solution.py:318
  45.6 0.9 collective-permute-start.5
  46.5 1.4 %collective-permute-start.2 = (bf16[2,128,512]{2,1,0:T(8,128)(2,1)S(1)}, bf16[2,128,512]{2,1,0:T(8,128)(2,1)S(1)}, u32[]{:S(2)}, u32[]{:S(2)}) collective-permute-start(bf16[2,128,512]{2,1,0:T(8,128)(2,1)S(1)} %get-tuple-element.25), channel_id=1, source_target_pairs={{32,0},{33,1},{34,2},{35,3},{36,4},{37,5},{38,6},{39,7},{40,8},{41... | collective-permute-start | bytes 786440 | tf_op jit(solution)/shard_map/ppermute | solution.py:317
  47.9 0.0 collective-permute-done.12.crossed
  47.9 0.1 choose.7
  48.0 1.8 %collective-permute-start.13 = (bf16[2,128,512]{2,1,0:T(8,128)(2,1)S(1)}, bf16[2,128,512]{2,1,0:T(8,128)(2,1)S(1)}, u32[]{:S(2)}, u32[]{:S(2)}) collective-permute-start(bf16[2,128,512]{2,1,0:T(8,128)(2,1)S(1)} %get-tuple-element.36), channel_id=1, source_target_pairs={{0,24},{1,25},{2,26},{3,27},{4,28},{5,29},{6,30},{7,31},{8,0},{9,1... | collective-permute-start | bytes 786440 | tf_op jit(solution)/shard_map/ppermute | solution.py:318
  49.9 2.0 %collective-permute-done.3.rest_7_.rest_0_.rest_1_ = bf16[2,144,512]{2,1,0:T(8,128)(2,1)S(1)} collective-permute-done((bf16[2,144,512]{2,1,0:T(8,128)(2,1)S(1)}, bf16[2,144,512]{2,1,0:T(8,128)(2,1)S(1)}, u32[]{:S(2)}, u32[]{:S(2)}) %collective-permute-start.3) | collective-permute-done | bytes 294944 | tf_op jit(solution)/shard_map/ppermute | solution.py:318
  51.9 5.3 %collective-permute-start.14 = (bf16[2,128,512]{2,1,0:T(8,128)(2,1)S(1)}, bf16[2,128,512]{2,1,0:T(8,128)(2,1)S(1)}, u32[]{:S(2)}, u32[]{:S(2)}) collective-permute-start(bf16[2,128,512]{2,1,0:T(8,128)(2,1)S(1)} %get-tuple-element.37), channel_id=1, source_target_pairs={{0,16},{1,17},{2,18},{3,19},{4,20},{5,21},{6,22},{7,23},{8,24},{9,... | collective-permute-start | bytes 786440 | tf_op jit(solution)/shard_map/ppermute | solution.py:318
  57.2 3.6 %collective-permute-start.15 = (bf16[2,128,512]{2,1,0:T(8,128)(2,1)S(1)}, bf16[2,128,512]{2,1,0:T(8,128)(2,1)S(1)}, u32[]{:S(2)}, u32[]{:S(2)}) collective-permute-start(bf16[2,128,512]{2,1,0:T(8,128)(2,1)S(1)} %get-tuple-element.38), channel_id=1, source_target_pairs={{0,8},{1,9},{2,10},{3,11},{4,12},{5,13},{6,14},{7,15},{8,16},{9,17... | collective-permute-start | bytes 786440 | tf_op jit(solution)/shard_map/ppermute | solution.py:318
  60.8 1.7 %collective-permute-done.5.rest_9_.rest_2_.rest_3_ = bf16[2,144,512]{2,1,0:T(8,128)(2,1)S(1)} collective-permute-done((bf16[2,144,512]{2,1,0:T(8,128)(2,1)S(1)}, bf16[2,144,512]{2,1,0:T(8,128)(2,1)S(1)}, u32[]{:S(2)}, u32[]{:S(2)}) %collective-permute-start.5) | collective-permute-done | bytes 294944 | tf_op jit(solution)/shard_map/ppermute | solution.py:318
  62.5 2.9 %correlate.4.rest_3_.rest_6_ = f32[1024,512]{1,0:T(8,128)S(1)} custom-call(bf16[1024,128]{1,0:T(8,128)(2,1)S(1)} %fusion.9.first, bf16[1024,512]{1,0:T(8,128)(2,1)S(1)} %fusion.4.second, bf16[2,128,512]{2,1,0:T(8,128)(2,1)S(1)} %first_part.1.after.own.rest_0_, bf16[2,128,512]{2,1,0:T(8,128)(2,1)S(1)} %collective-permute-done.6.rest_1_.rest_0_, ...), custom_call_target="tpu_custom_call" | custom-call | flops 200000000 | bytes 1048576 | tf_op jit(solution)/shard_map/correlate/pallas_call | solution.py:150
  65.3 0.0 collective-permute-done.2.crossed
  65.3 0.1 choose.6
  65.4 1.2 collective-permute-start.10
  66.7 0.0 collective-permute-start.11
  66.7 0.0 collective-permute-done.13.rest_1_
  66.7 3.2 %collective-permute-start.9 = (bf16[2,128,512]{2,1,0:T(8,128)(2,1)S(1)}, bf16[2,128,512]{2,1,0:T(8,128)(2,1)S(1)}, u32[]{:S(2)}, u32[]{:S(2)}) collective-permute-start(bf16[2,128,512]{2,1,0:T(8,128)(2,1)S(1)} %get-tuple-element.32), channel_id=1, source_target_pairs={{0,24},{1,25},{2,26},{3,27},{4,28},{5,29},{6,30},{7,31},{8,0},{9,1... | collective-permute-start | bytes 786440 | tf_op jit(solution)/shard_map/ppermute | solution.py:318
  69.9 2.9 %correlate.5.rest_6_ = f32[1024,512]{1,0:T(8,128)S(1)} custom-call(bf16[1024,128]{1,0:T(8,128)(2,1)S(1)} %fusion.9.first, bf16[1024,512]{1,0:T(8,128)(2,1)S(1)} %fusion.4.second, bf16[2,144,512]{2,1,0:T(8,128)(2,1)S(1)} %fusion.10.own.rest_6_.rest_0_, bf16[2,144,512]{2,1,0:T(8,128)(2,1)S(1)} %collective-permute-done.3.rest_7_.rest_0_.rest_1_, ...), custom_call_target="tpu_custom_call" | custom-call | flops 200000000 | bytes 1048576 | tf_op jit(solution)/shard_map/correlate/pallas_call | solution.py:150
  72.8 0.9 collective-permute-done.15.rest_3_
  73.7 2.9 %correlate.6.rest_6_ = f32[1024,512]{1,0:T(8,128)S(1)} custom-call(bf16[1024,128]{1,0:T(8,128)(2,1)S(1)} %fusion.9.first, bf16[1024,512]{1,0:T(8,128)(2,1)S(1)} %fusion.4.second, bf16[2,128,512]{2,1,0:T(8,128)(2,1)S(1)} %get-tuple-element.45.rest_0_.own, bf16[2,128,512]{2,1,0:T(8,128)(2,1)S(1)} %collective-permute-done.13.rest_1_, ...), custom_call_target="tpu_custom_call" | custom-call | flops 200000000 | bytes 1048576 | tf_op jit(solution)/shard_map/correlate/pallas_call | solution.py:150
  76.6 0.0 copy-start.4
  76.6 0.1 collective-permute-done.10.rest_2_
  76.7 3.0 %collective-permute-done.11.rest_3_ = bf16[2,128,512]{2,1,0:T(8,128)(2,1)S(1)} collective-permute-done((bf16[2,128,512]{2,1,0:T(8,128)(2,1)S(1)}, bf16[2,128,512]{2,1,0:T(8,128)(2,1)S(1)}, u32[]{:S(2)}, u32[]{:S(2)}) %collective-permute-start.11) | collective-permute-done | bytes 262176 | tf_op jit(solution)/shard_map/ppermute | solution.py:318
  79.8 2.9 %correlate.7 = (f32[1024,256]{1,0:T(8,128)S(1)}, bf16[1024,256]{1,0:T(8,128)(2,1)S(1)}) custom-call(bf16[1024,128]{1,0:T(8,128)(2,1)S(1)} %fusion.9.first, bf16[1024,512]{1,0:T(8,128)(2,1)S(1)} %fusion.4.second, bf16[2,128,512]{2,1,0:T(8,128)(2,1)S(1)} %get-tuple-element.47.rest_0_.own, bf16[2,128,512]{2,1,0:T(8,128)(2,1)S(1)} %collective-permute-done.9.rest_1_, ...), custom_call_target="tpu_custom_call" | custom-call | flops 200000000 | bytes 1048576 | tf_op jit(solution)/shard_map/correlate/pallas_call | solution.py:150
  82.6 0.3 collective-permute-start.16
  83.6 0.5 fusion.7
  84.2 0.7 collective-permute-done.16.received
  84.9 0.2 split_kernel.1
  85.1 0.1 collective-permute-start.17
  85.2 2.9 %collective-permute-start.18 = (bf16[512,128]{1,0:T(8,128)(2,1)S(1)}, bf16[512,128]{1,0:T(8,128)(2,1)S(1)}, u32[]{:S(2)}, u32[]{:S(2)}) collective-permute-start(bf16[512,128]{1,0:T(8,128)(2,1)S(1)} %get-tuple-element.43), channel_id=1, source_target_pairs={{0,4},{1,5},{2,6},{3,7},{4,0},{5,1},{6,2},{7,3},{8,12},{9,13},{10,... | collective-permute-start | bytes 393224 | tf_op jit(solution)/shard_map/ppermute | solution.py:331
  88.1 0.6 collective-permute-start.19
  88.7 2.1 %fusion.hot = bf16[2048,1024]{1,0:T(8,128)(2,1)S(1)} fusion(s32[1024]{0:T(1024)S(1)} %add_select_fusion.2), kind=kLoop, calls=%fused_computation.1 | loop fusion | flops 4194304 | bytes 4198400 | tf_op jit(solution)/shard_map/convert_element_type | solution.py:290
  90.8 0.8 collective-permute-done.17.one
  91.5 5.9 %collective-permute-done.18.two = bf16[512,128]{1,0:T(8,128)(2,1)S(1)} collective-permute-done((bf16[512,128]{1,0:T(8,128)(2,1)S(1)}, bf16[512,128]{1,0:T(8,128)(2,1)S(1)}, u32[]{:S(2)}, u32[]{:S(2)}) %collective-permute-start.18) | collective-permute-done | bytes 131104 | tf_op jit(solution)/shard_map/ppermute | solution.py:331
  97.5 2.9 %collective-permute-done.19.three = bf16[512,128]{1,0:T(8,128)(2,1)S(1)} collective-permute-done((bf16[512,128]{1,0:T(8,128)(2,1)S(1)}, bf16[512,128]{1,0:T(8,128)(2,1)S(1)}, u32[]{:S(2)}, u32[]{:S(2)}) %collective-permute-start.19) | collective-permute-done | bytes 131104 | tf_op jit(solution)/shard_map/ppermute | solution.py:331
  100.4 1.4 %route_kernel.1 = bf16[32,32,128]{2,1,0:T(8,128)(2,1)S(1)} custom-call(bf16[2048,1024]{1,0:T(8,128)(2,1)S(1)} %fusion.hot, f32[512,128]{1,0:T(8,128)S(1)} %get-tuple-element.41.keep, bf16[512,128]{1,0:T(8,128)(2,1)S(1)} %collective-permute-done.17.one, bf16[512,128]{1,0:T(8,128)(2,1)S(1)} %collective-permute-done.18.two, ...), custom_call_target="tpu_custom_call" | custom-call | tf_op jit(solution)/shard_map/route_kernel/pallas_call | solution.py:256
  101.8 23.6 %all_to_all.5.routed = bf16[32,32,128]{2,1,0:T(8,128)(2,1)S(1)} all-to-all(bf16[32,32,128]{2,1,0:T(8,128)(2,1)S(1)} %route_kernel.1), channel_id=1, replica_groups=mesh['chan'=32,'win'=8] {'chan'}, dimensions={0} | all-to-all | bytes 524288 | tf_op jit(solution)/shard_map/all_to_all | solution.py:335
  125.4 1.1 unpack_kernel.1
  (25 shorter events, 0.1 us)
Async XLA Ops:
  1.6 27.3 %collective-permute-start = (bf16[2,128,512]{2,1,0:T(8,128)(2,1)S(1)}, bf16[2,128,512]{2,1,0:T(8,128)(2,1)S(1)}, u32[]{:S(2)}, u32[]{:S(2)}) collective-permute-start(bf16[2,128,512]{2,1,0:T(8,128)(2,1)S(1)} %first_part.1.after.own.rest_0_), channel_id=1, source_target_pairs={{32,0},{33,1},{34,2},{35,3},{36,4},{37,5},{38,6},{39,7},{40,8},{41... | collective-permute-start | bytes 786440 | tf_op jit(solution)/shard_map/ppermute | solution.py:273
  2.9 1.2 copy-start.1
  9.4 31.4 %collective-permute-start.1 = (bf16[2,144,512]{2,1,0:T(8,128)(2,1)}, bf16[2,144,512]{2,1,0:T(8,128)(2,1)}, u32[]{:S(2)}, u32[]{:S(2)}) collective-permute-start(bf16[2,144,512]{2,1,0:T(8,128)(2,1)} %hold.7), channel_id=1, source_target_pairs={{32,0},{33,1},{34,2},{35,3},{36,4},{37,5},{38,6},{39,7},{40,8},{41... | collective-permute-start | bytes 884744 | tf_op jit(solution)/shard_map/ppermute | solution.py:292
  28.9 4.6 %copy-start.2 = (s32[1,1024]{1,0:T(1,128)S(1)}, s32[1,1024]{1,0:T(1,128)}, u32[]{:S(2)}) copy-start(s32[1,1024]{1,0:T(1,128)} %own.3) | copy-start | bytes 12292
  28.9 6.1 %copy-start.3 = (s32[1,1024]{1,0:T(1,128)S(1)}, s32[1,1024]{1,0:T(1,128)}, u32[]{:S(2)}) copy-start(s32[1,1024]{1,0:T(1,128)} %own.4) | copy-start | bytes 12292
  29.0 13.0 %collective-permute-start.6 = (bf16[2,128,512]{2,1,0:T(8,128)(2,1)S(1)}, bf16[2,128,512]{2,1,0:T(8,128)(2,1)S(1)}, u32[]{:S(2)}, u32[]{:S(2)}) collective-permute-start(bf16[2,128,512]{2,1,0:T(8,128)(2,1)S(1)} %get-tuple-element.29), channel_id=1, source_target_pairs={{0,24},{1,25},{2,26},{3,27},{4,28},{5,29},{6,30},{7,31},{8,0},{9,1... | collective-permute-start | bytes 786440 | tf_op jit(solution)/shard_map/ppermute | solution.py:318
  29.1 16.6 %collective-permute-start.7 = (bf16[2,128,512]{2,1,0:T(8,128)(2,1)S(1)}, bf16[2,128,512]{2,1,0:T(8,128)(2,1)S(1)}, u32[]{:S(2)}, u32[]{:S(2)}) collective-permute-start(bf16[2,128,512]{2,1,0:T(8,128)(2,1)S(1)} %get-tuple-element.30), channel_id=1, source_target_pairs={{0,16},{1,17},{2,18},{3,19},{4,20},{5,21},{6,22},{7,23},{8,24},{9,... | collective-permute-start | bytes 786440 | tf_op jit(solution)/shard_map/ppermute | solution.py:318
  32.6 13.9 %collective-permute-start.8 = (bf16[2,128,512]{2,1,0:T(8,128)(2,1)S(1)}, bf16[2,128,512]{2,1,0:T(8,128)(2,1)S(1)}, u32[]{:S(2)}, u32[]{:S(2)}) collective-permute-start(bf16[2,128,512]{2,1,0:T(8,128)(2,1)S(1)} %get-tuple-element.31), channel_id=1, source_target_pairs={{0,8},{1,9},{2,10},{3,11},{4,12},{5,13},{6,14},{7,15},{8,16},{9,17... | collective-permute-start | bytes 786440 | tf_op jit(solution)/shard_map/ppermute | solution.py:318
  33.7 14.2 %collective-permute-start.12 = (bf16[2,128,512]{2,1,0:T(8,128)(2,1)S(1)}, bf16[2,128,512]{2,1,0:T(8,128)(2,1)S(1)}, u32[]{:S(2)}, u32[]{:S(2)}) collective-permute-start(bf16[2,128,512]{2,1,0:T(8,128)(2,1)S(1)} %get-tuple-element.35), channel_id=1, source_target_pairs={{32,0},{33,1},{34,2},{35,3},{36,4},{37,5},{38,6},{39,7},{40,8},{41... | collective-permute-start | bytes 786440 | tf_op jit(solution)/shard_map/ppermute | solution.py:317
  41.8 10.0 %collective-permute-start.3 = (bf16[2,144,512]{2,1,0:T(8,128)(2,1)S(1)}, bf16[2,144,512]{2,1,0:T(8,128)(2,1)S(1)}, u32[]{:S(2)}, u32[]{:S(2)}) collective-permute-start(bf16[2,144,512]{2,1,0:T(8,128)(2,1)S(1)} %get-tuple-element.26), channel_id=1, source_target_pairs={{0,24},{1,25},{2,26},{3,27},{4,28},{5,29},{6,30},{7,31},{8,0},{9,1... | collective-permute-start | bytes 884744 | tf_op jit(solution)/shard_map/ppermute | solution.py:318
  41.9 15.3 %collective-permute-start.4 = (bf16[2,144,512]{2,1,0:T(8,128)(2,1)S(1)}, bf16[2,144,512]{2,1,0:T(8,128)(2,1)S(1)}, u32[]{:S(2)}, u32[]{:S(2)}) collective-permute-start(bf16[2,144,512]{2,1,0:T(8,128)(2,1)S(1)} %get-tuple-element.27), channel_id=1, source_target_pairs={{0,16},{1,17},{2,18},{3,19},{4,20},{5,21},{6,22},{7,23},{8,24},{9,... | collective-permute-start | bytes 884744 | tf_op jit(solution)/shard_map/ppermute | solution.py:318
  45.6 16.8 %collective-permute-start.5 = (bf16[2,144,512]{2,1,0:T(8,128)(2,1)S(1)}, bf16[2,144,512]{2,1,0:T(8,128)(2,1)S(1)}, u32[]{:S(2)}, u32[]{:S(2)}) collective-permute-start(bf16[2,144,512]{2,1,0:T(8,128)(2,1)S(1)} %get-tuple-element.28), channel_id=1, source_target_pairs={{0,8},{1,9},{2,10},{3,11},{4,12},{5,13},{6,14},{7,15},{8,16},{9,17... | collective-permute-start | bytes 884744 | tf_op jit(solution)/shard_map/ppermute | solution.py:318
  46.5 15.9 %copy-start = (bf16[2048,512]{1,0:T(8,128)(2,1)S(1)}, bf16[2048,512]{1,0:T(8,128)(2,1)}, u32[]{:S(2)}) copy-start(bf16[2048,512]{1,0:T(8,128)(2,1)} %fusion.1.rest_5_) | copy-start | bytes 6291460
  46.5 18.8 %collective-permute-start.2 = (bf16[2,128,512]{2,1,0:T(8,128)(2,1)S(1)}, bf16[2,128,512]{2,1,0:T(8,128)(2,1)S(1)}, u32[]{:S(2)}, u32[]{:S(2)}) collective-permute-start(bf16[2,128,512]{2,1,0:T(8,128)(2,1)S(1)} %get-tuple-element.25), channel_id=1, source_target_pairs={{32,0},{33,1},{34,2},{35,3},{36,4},{37,5},{38,6},{39,7},{40,8},{41... | collective-permute-start | bytes 786440 | tf_op jit(solution)/shard_map/ppermute | solution.py:317
  48.0 18.6 %collective-permute-start.13 = (bf16[2,128,512]{2,1,0:T(8,128)(2,1)S(1)}, bf16[2,128,512]{2,1,0:T(8,128)(2,1)S(1)}, u32[]{:S(2)}, u32[]{:S(2)}) collective-permute-start(bf16[2,128,512]{2,1,0:T(8,128)(2,1)S(1)} %get-tuple-element.36), channel_id=1, source_target_pairs={{0,24},{1,25},{2,26},{3,27},{4,28},{5,29},{6,30},{7,31},{8,0},{9,1... | collective-permute-start | bytes 786440 | tf_op jit(solution)/shard_map/ppermute | solution.py:318
  51.9 20.9 %collective-permute-start.14 = (bf16[2,128,512]{2,1,0:T(8,128)(2,1)S(1)}, bf16[2,128,512]{2,1,0:T(8,128)(2,1)S(1)}, u32[]{:S(2)}, u32[]{:S(2)}) collective-permute-start(bf16[2,128,512]{2,1,0:T(8,128)(2,1)S(1)} %get-tuple-element.37), channel_id=1, source_target_pairs={{0,16},{1,17},{2,18},{3,19},{4,20},{5,21},{6,22},{7,23},{8,24},{9,... | collective-permute-start | bytes 786440 | tf_op jit(solution)/shard_map/ppermute | solution.py:318
  57.2 16.5 %collective-permute-start.15 = (bf16[2,128,512]{2,1,0:T(8,128)(2,1)S(1)}, bf16[2,128,512]{2,1,0:T(8,128)(2,1)S(1)}, u32[]{:S(2)}, u32[]{:S(2)}) collective-permute-start(bf16[2,128,512]{2,1,0:T(8,128)(2,1)S(1)} %get-tuple-element.38), channel_id=1, source_target_pairs={{0,8},{1,9},{2,10},{3,11},{4,12},{5,13},{6,14},{7,15},{8,16},{9,17... | collective-permute-start | bytes 786440 | tf_op jit(solution)/shard_map/ppermute | solution.py:318
  65.4 11.3 %collective-permute-start.10 = (bf16[2,128,512]{2,1,0:T(8,128)(2,1)S(1)}, bf16[2,128,512]{2,1,0:T(8,128)(2,1)S(1)}, u32[]{:S(2)}, u32[]{:S(2)}) collective-permute-start(bf16[2,128,512]{2,1,0:T(8,128)(2,1)S(1)} %get-tuple-element.33), channel_id=1, source_target_pairs={{0,16},{1,17},{2,18},{3,19},{4,20},{5,21},{6,22},{7,23},{8,24},{9,... | collective-permute-start | bytes 786440 | tf_op jit(solution)/shard_map/ppermute | solution.py:318
  66.7 13.1 %collective-permute-start.11 = (bf16[2,128,512]{2,1,0:T(8,128)(2,1)S(1)}, bf16[2,128,512]{2,1,0:T(8,128)(2,1)S(1)}, u32[]{:S(2)}, u32[]{:S(2)}) collective-permute-start(bf16[2,128,512]{2,1,0:T(8,128)(2,1)S(1)} %get-tuple-element.34), channel_id=1, source_target_pairs={{0,8},{1,9},{2,10},{3,11},{4,12},{5,13},{6,14},{7,15},{8,16},{9,17... | collective-permute-start | bytes 786440 | tf_op jit(solution)/shard_map/ppermute | solution.py:318
  66.7 13.1 %collective-permute-start.9 = (bf16[2,128,512]{2,1,0:T(8,128)(2,1)S(1)}, bf16[2,128,512]{2,1,0:T(8,128)(2,1)S(1)}, u32[]{:S(2)}, u32[]{:S(2)}) collective-permute-start(bf16[2,128,512]{2,1,0:T(8,128)(2,1)S(1)} %get-tuple-element.32), channel_id=1, source_target_pairs={{0,24},{1,25},{2,26},{3,27},{4,28},{5,29},{6,30},{7,31},{8,0},{9,1... | collective-permute-start | bytes 786440 | tf_op jit(solution)/shard_map/ppermute | solution.py:318
  76.6 7.0 %copy-start.4 = (s32[1,1024,1]{1,2,0:T(1,128)S(1)}, s32[1,1024,1]{1,2,0:T(1,128)}, u32[]{:S(2)}) copy-start(s32[1,1024,1]{1,2,0:T(1,128)} %param.9) | copy-start | bytes 12292
  82.6 2.2 %collective-permute-start.16 = (bf16[1024,256]{1,0:T(8,128)(2,1)S(1)}, bf16[1024,256]{1,0:T(8,128)(2,1)S(1)}, u32[]{:S(2)}, u32[]{:S(2)}) collective-permute-start(bf16[1024,256]{1,0:T(8,128)(2,1)S(1)} %get-tuple-element.40), channel_id=1, source_target_pairs={{0,1},{1,0},{2,3},{3,2},{4,5},{5,4},{6,7},{7,6},{8,9},{9,8},{10,11... | collective-permute-start | bytes 1572872 | tf_op jit(solution)/shard_map/ppermute | solution.py:323
  85.1 6.4 %collective-permute-start.17 = (bf16[512,128]{1,0:T(8,128)(2,1)S(1)}, bf16[512,128]{1,0:T(8,128)(2,1)S(1)}, u32[]{:S(2)}, u32[]{:S(2)}) collective-permute-start(bf16[512,128]{1,0:T(8,128)(2,1)S(1)} %get-tuple-element.42), channel_id=1, source_target_pairs={{0,2},{1,3},{2,0},{3,1},{4,6},{5,7},{6,4},{7,5},{8,10},{9,11},{10,... | collective-permute-start | bytes 393224 | tf_op jit(solution)/shard_map/ppermute | solution.py:331
  85.2 12.3 %collective-permute-start.18 = (bf16[512,128]{1,0:T(8,128)(2,1)S(1)}, bf16[512,128]{1,0:T(8,128)(2,1)S(1)}, u32[]{:S(2)}, u32[]{:S(2)}) collective-permute-start(bf16[512,128]{1,0:T(8,128)(2,1)S(1)} %get-tuple-element.43), channel_id=1, source_target_pairs={{0,4},{1,5},{2,6},{3,7},{4,0},{5,1},{6,2},{7,3},{8,12},{9,13},{10,... | collective-permute-start | bytes 393224 | tf_op jit(solution)/shard_map/ppermute | solution.py:331
  88.1 12.3 %collective-permute-start.19 = (bf16[512,128]{1,0:T(8,128)(2,1)S(1)}, bf16[512,128]{1,0:T(8,128)(2,1)S(1)}, u32[]{:S(2)}, u32[]{:S(2)}) collective-permute-start(bf16[512,128]{1,0:T(8,128)(2,1)S(1)} %get-tuple-element.44), channel_id=1, source_target_pairs={{0,6},{1,7},{2,4},{3,5},{4,2},{5,3},{6,0},{7,1},{8,14},{9,15},{10,... | collective-permute-start | bytes 393224 | tf_op jit(solution)/shard_map/ppermute | solution.py:331

commit v6 on v5

--- a/solution.py
+++ b/solution.py
@@ -246,10 +246,23 @@
 
 
 def unpack_kernel(routed, out):
-    for block in range(32):
+    for block in range(routed.shape[0]):
         values = routed[block].astype(jnp.float32)
         out[0, block, :32] = values[:, :64]
         out[0, block, 32:] = values[:, 64:]
+
+
+def unpack(routed):
+    blocks = 8
+    return pl.pallas_call(
+        unpack_kernel,
+        grid=(routed.shape[0] // blocks,),
+        in_specs=[pl.BlockSpec((blocks, 32, 128), lambda i: (i, 0, 0))],
+        out_specs=pl.BlockSpec((1, blocks, 64, 64), lambda i: (0, i, 0, 0)),
+        out_shape=jax.ShapeDtypeStruct((1, routed.shape[0], 64, 64), jnp.float32),
+        compiler_params=pltpu.CompilerParams(vmem_limit_bytes=24 << 20),
+        name="unpack",
+    )(routed)
 
 
 def call(kernel, out_shape, *operands):
@@ -333,7 +346,7 @@
         route_kernel, jax.ShapeDtypeStruct((32, 32, 128), jnp.bfloat16), place_hot, pieces[0], *(arrived[k] for k in (1, 2, 3))
     )
     routed = lax.all_to_all(buffer, "chan", split_axis=0, concat_axis=0, tiled=True)
-    return call(unpack_kernel, jax.ShapeDtypeStruct((1, 32, 64, 64), f32), routed)
+    return unpack(routed)
 
 
 def solution(mesh):

time: 127 us -> 127 us (level)
    pallas_call x0 -> x1, Pallas kernels: none -> 1.68 us  [unpack(): pl.pallas_call(unpack_kernel, grid=(routed.shape[0] // blocks,), in_specs...]
    pallas_call x3 -> x2, Pallas kernels: 2.79 us -> 1.68 us  [call(): pl.pallas_call(kernel, out_shape=out_shape, compiler_params=pltpu.Compile...]
where the time goes in v6:
time: 127 us
  waiting for transfers between devices  40.1 us (32%)
  starting transfers between devices  33.5 us (26%)
  blocking collectives  23.6 us (19%)
  Pallas kernels  17 us (13%)
  other arithmetic  8.47 us (7%)
  local copies, waits for them, and re-layouts  2.88 us (2%)
    ppermute x12, starting transfers between devices, on_device(): lax.ppermute(sources[d - 1], AXES, AROUND[d])  24.4 us
    all_to_all x1, blocking collectives, on_device(): lax.all_to_all(buffer, 'chan', split_axis=0, concat_axis=0, tiled=True)  23.6 us
    ppermute x1, waiting for transfers between devices, on_device(): crossed = [lax.ppermute(own[0], AXES, CROSS)]  16.5 us
    pallas_call x4, Pallas kernels, run_chunk(): pl.pallas_call(kernel, grid=(slots // ROWS,), in_specs=in_specs, out_spec...  11.5 us
    ppermute x3, waiting for transfers between devices, on_device(): lax.ppermute(pieces[k], AXES, OTHER_CHIP[k])  9.61 us
    ppermute x12, waiting for transfers between devices, on_device(): lax.ppermute(sources[d - 1], AXES, AROUND[d])  7.75 us
    ppermute x1, waiting for transfers between devices, on_device(): crossed.append(lax.ppermute(hold(own[1], cosine), AXES, CROSS))  5.49 us
    ppermute x3, starting transfers between devices, on_device(): lax.ppermute(pieces[k], AXES, OTHER_CHIP[k])  3.57 us
  transfers between devices with their start and end apart: 20, of which 11 were waited for; matrix products, arithmetic and copies ran while one was open for 7% of the time, Pallas kernels for 8%

profile of v6, /device:TPU:32, one launch (start us, length us, event | category | flops | bytes accessed | tf_op | source)
XLA Modules:
  0.0 127.1 jit_solution(17742840506822869551)
XLA Ops:
  0.0 1.6 %copy.9 = bf16[1,128,2,2048]{3,1,2,0:T(8,128)(2,1)S(1)} copy(bf16[1,128,2,2048]{3,2,1,0:T(2,128)(2,1)} %own.5) | data formatting | bytes 2097152 | tf_op args[0]
  1.6 1.3 %collective-permute-start = (bf16[2,128,512]{2,1,0:T(8,128)(2,1)S(1)}, bf16[2,128,512]{2,1,0:T(8,128)(2,1)S(1)}, u32[]{:S(2)}, u32[]{:S(2)}) collective-permute-start(bf16[2,128,512]{2,1,0:T(8,128)(2,1)S(1)} %first_part.1.after.own.rest_0_), channel_id=1, source_target_pairs={{32,0},{33,1},{34,2},{35,3},{36,4},{37,5},{38,6},{39,7},{40,8},{41... | collective-permute-start | bytes 786440 | tf_op jit(solution)/shard_map/ppermute | solution.py:286
  2.9 0.0 copy-start.1
  3.0 1.2 copy-done.1
  4.2 0.1 hold.6
  4.2 1.5 %multiply_reduce_fusion = f32[128]{0:T(128)S(1)} fusion(bf16[1,128,2,2048]{3,2,1,0:T(2,128)(2,1)S(1)} %hold.6), kind=kLoop, calls=%fused_computation.10 | loop fusion | flops 1572736 | bytes 1049088 | tf_op jit(solution)/shard_map/reduce_sum | solution.py:71
  5.8 0.3 fusion.28
  6.1 0.6 fusion.20
  6.7 0.1 reshape.281
  6.8 0.3 multiply_convert_fusion
  7.0 1.2 multiply_add_fusion
  8.2 0.3 fusion.2.after.rest_4_
  8.6 0.7 hold.7
  9.4 1.3 %collective-permute-start.1 = (bf16[2,144,512]{2,1,0:T(8,128)(2,1)}, bf16[2,144,512]{2,1,0:T(8,128)(2,1)}, u32[]{:S(2)}, u32[]{:S(2)}) collective-permute-start(bf16[2,144,512]{2,1,0:T(8,128)(2,1)} %hold.7), channel_id=1, source_target_pairs={{32,0},{33,1},{34,2},{35,3},{36,4},{37,5},{38,6},{39,7},{40,8},{41... | collective-permute-start | bytes 884744 | tf_op jit(solution)/shard_map/ppermute | solution.py:305
  10.7 1.7 %fusion.1.rest_5_ = bf16[2048,512]{1,0:T(8,128)(2,1)} fusion(f32[64,32,512]{2,1,0:T(8,128)S(1)} %get-tuple-element.48, f32[2048]{0:T(1024)S(1)} %neg.8), kind=kLoop, calls=%fused_computation.3 | loop fusion | flops 2097152 | bytes 6299648 | tf_op jit(solution)/shard_map/convert_element_type | solution.py:66
  12.3 16.5 %collective-permute-done.after.crossed = bf16[2,128,512]{2,1,0:T(8,128)(2,1)S(1)} collective-permute-done((bf16[2,128,512]{2,1,0:T(8,128)(2,1)S(1)}, bf16[2,128,512]{2,1,0:T(8,128)(2,1)S(1)}, u32[]{:S(2)}, u32[]{:S(2)}) %collective-permute-start) | collective-permute-done | bytes 262176 | tf_op jit(solution)/shard_map/ppermute | solution.py:286
  28.9 0.1 choose.5
  29.0 0.1 collective-permute-start.6
  29.1 3.5 %collective-permute-start.7 = (bf16[2,128,512]{2,1,0:T(8,128)(2,1)S(1)}, bf16[2,128,512]{2,1,0:T(8,128)(2,1)S(1)}, u32[]{:S(2)}, u32[]{:S(2)}) collective-permute-start(bf16[2,128,512]{2,1,0:T(8,128)(2,1)S(1)} %get-tuple-element.30), channel_id=1, source_target_pairs={{0,16},{1,17},{2,18},{3,19},{4,20},{5,21},{6,22},{7,23},{8,24},{9,... | collective-permute-start | bytes 786440 | tf_op jit(solution)/shard_map/ppermute | solution.py:331
  32.6 0.9 collective-permute-start.8
  33.5 0.2 fusion.9.first
  33.7 1.3 %collective-permute-start.12 = (bf16[2,128,512]{2,1,0:T(8,128)(2,1)S(1)}, bf16[2,128,512]{2,1,0:T(8,128)(2,1)S(1)}, u32[]{:S(2)}, u32[]{:S(2)}) collective-permute-start(bf16[2,128,512]{2,1,0:T(8,128)(2,1)S(1)} %get-tuple-element.35), channel_id=1, source_target_pairs={{32,0},{33,1},{34,2},{35,3},{36,4},{37,5},{38,6},{39,7},{40,8},{41... | collective-permute-start | bytes 786440 | tf_op jit(solution)/shard_map/ppermute | solution.py:330
  35.0 0.2 fusion.4.second
  35.3 5.5 %collective-permute-done.1.crossed = bf16[2,144,512]{2,1,0:T(8,128)(2,1)} collective-permute-done((bf16[2,144,512]{2,1,0:T(8,128)(2,1)}, bf16[2,144,512]{2,1,0:T(8,128)(2,1)}, u32[]{:S(2)}, u32[]{:S(2)}) %collective-permute-start.1) | collective-permute-done | bytes 294944 | tf_op jit(solution)/shard_map/ppermute | solution.py:305
  40.8 1.1 choose.4
  41.8 0.1 collective-permute-start.3
  41.9 3.7 %collective-permute-start.4 = (bf16[2,144,512]{2,1,0:T(8,128)(2,1)S(1)}, bf16[2,144,512]{2,1,0:T(8,128)(2,1)S(1)}, u32[]{:S(2)}, u32[]{:S(2)}) collective-permute-start(bf16[2,144,512]{2,1,0:T(8,128)(2,1)S(1)} %get-tuple-element.27), channel_id=1, source_target_pairs={{0,16},{1,17},{2,18},{3,19},{4,20},{5,21},{6,22},{7,23},{8,24},{9,... | collective-permute-start | bytes 884744 | tf_op jit(solution)/shard_map/ppermute | solution.py:331
  45.6 0.9 collective-permute-start.5
  46.5 1.4 %collective-permute-start.2 = (bf16[2,128,512]{2,1,0:T(8,128)(2,1)S(1)}, bf16[2,128,512]{2,1,0:T(8,128)(2,1)S(1)}, u32[]{:S(2)}, u32[]{:S(2)}) collective-permute-start(bf16[2,128,512]{2,1,0:T(8,128)(2,1)S(1)} %get-tuple-element.25), channel_id=1, source_target_pairs={{32,0},{33,1},{34,2},{35,3},{36,4},{37,5},{38,6},{39,7},{40,8},{41... | collective-permute-start | bytes 786440 | tf_op jit(solution)/shard_map/ppermute | solution.py:330
  47.9 0.0 collective-permute-done.12.crossed
  47.9 0.1 choose.7
  48.0 1.8 %collective-permute-start.13 = (bf16[2,128,512]{2,1,0:T(8,128)(2,1)S(1)}, bf16[2,128,512]{2,1,0:T(8,128)(2,1)S(1)}, u32[]{:S(2)}, u32[]{:S(2)}) collective-permute-start(bf16[2,128,512]{2,1,0:T(8,128)(2,1)S(1)} %get-tuple-element.36), channel_id=1, source_target_pairs={{0,24},{1,25},{2,26},{3,27},{4,28},{5,29},{6,30},{7,31},{8,0},{9,1... | collective-permute-start | bytes 786440 | tf_op jit(solution)/shard_map/ppermute | solution.py:331
  49.9 2.0 %collective-permute-done.3.rest_7_.rest_0_.rest_1_ = bf16[2,144,512]{2,1,0:T(8,128)(2,1)S(1)} collective-permute-done((bf16[2,144,512]{2,1,0:T(8,128)(2,1)S(1)}, bf16[2,144,512]{2,1,0:T(8,128)(2,1)S(1)}, u32[]{:S(2)}, u32[]{:S(2)}) %collective-permute-start.3) | collective-permute-done | bytes 294944 | tf_op jit(solution)/shard_map/ppermute | solution.py:331
  51.9 5.3 %collective-permute-start.14 = (bf16[2,128,512]{2,1,0:T(8,128)(2,1)S(1)}, bf16[2,128,512]{2,1,0:T(8,128)(2,1)S(1)}, u32[]{:S(2)}, u32[]{:S(2)}) collective-permute-start(bf16[2,128,512]{2,1,0:T(8,128)(2,1)S(1)} %get-tuple-element.37), channel_id=1, source_target_pairs={{0,16},{1,17},{2,18},{3,19},{4,20},{5,21},{6,22},{7,23},{8,24},{9,... | collective-permute-start | bytes 786440 | tf_op jit(solution)/shard_map/ppermute | solution.py:331
  57.2 3.6 %collective-permute-start.15 = (bf16[2,128,512]{2,1,0:T(8,128)(2,1)S(1)}, bf16[2,128,512]{2,1,0:T(8,128)(2,1)S(1)}, u32[]{:S(2)}, u32[]{:S(2)}) collective-permute-start(bf16[2,128,512]{2,1,0:T(8,128)(2,1)S(1)} %get-tuple-element.38), channel_id=1, source_target_pairs={{0,8},{1,9},{2,10},{3,11},{4,12},{5,13},{6,14},{7,15},{8,16},{9,17... | collective-permute-start | bytes 786440 | tf_op jit(solution)/shard_map/ppermute | solution.py:331
  60.8 1.7 %collective-permute-done.5.rest_9_.rest_2_.rest_3_ = bf16[2,144,512]{2,1,0:T(8,128)(2,1)S(1)} collective-permute-done((bf16[2,144,512]{2,1,0:T(8,128)(2,1)S(1)}, bf16[2,144,512]{2,1,0:T(8,128)(2,1)S(1)}, u32[]{:S(2)}, u32[]{:S(2)}) %collective-permute-start.5) | collective-permute-done | bytes 294944 | tf_op jit(solution)/shard_map/ppermute | solution.py:331
  62.5 2.9 %correlate.4.rest_3_.rest_6_ = f32[1024,512]{1,0:T(8,128)S(1)} custom-call(bf16[1024,128]{1,0:T(8,128)(2,1)S(1)} %fusion.9.first, bf16[1024,512]{1,0:T(8,128)(2,1)S(1)} %fusion.4.second, bf16[2,128,512]{2,1,0:T(8,128)(2,1)S(1)} %first_part.1.after.own.rest_0_, bf16[2,128,512]{2,1,0:T(8,128)(2,1)S(1)} %collective-permute-done.6.rest_1_.rest_0_, ...), custom_call_target="tpu_custom_call" | custom-call | flops 200000000 | bytes 1048576 | tf_op jit(solution)/shard_map/correlate/pallas_call | solution.py:150
  65.3 0.0 collective-permute-done.2.crossed
  65.3 0.1 choose.6
  65.4 1.2 collective-permute-start.10
  66.7 0.0 collective-permute-start.11
  66.7 0.0 collective-permute-done.13.rest_1_
  66.7 3.2 %collective-permute-start.9 = (bf16[2,128,512]{2,1,0:T(8,128)(2,1)S(1)}, bf16[2,128,512]{2,1,0:T(8,128)(2,1)S(1)}, u32[]{:S(2)}, u32[]{:S(2)}) collective-permute-start(bf16[2,128,512]{2,1,0:T(8,128)(2,1)S(1)} %get-tuple-element.32), channel_id=1, source_target_pairs={{0,24},{1,25},{2,26},{3,27},{4,28},{5,29},{6,30},{7,31},{8,0},{9,1... | collective-permute-start | bytes 786440 | tf_op jit(solution)/shard_map/ppermute | solution.py:331
  69.9 2.9 %correlate.5.rest_6_ = f32[1024,512]{1,0:T(8,128)S(1)} custom-call(bf16[1024,128]{1,0:T(8,128)(2,1)S(1)} %fusion.9.first, bf16[1024,512]{1,0:T(8,128)(2,1)S(1)} %fusion.4.second, bf16[2,144,512]{2,1,0:T(8,128)(2,1)S(1)} %fusion.10.own.rest_6_.rest_0_, bf16[2,144,512]{2,1,0:T(8,128)(2,1)S(1)} %collective-permute-done.3.rest_7_.rest_0_.rest_1_, ...), custom_call_target="tpu_custom_call" | custom-call | flops 200000000 | bytes 1048576 | tf_op jit(solution)/shard_map/correlate/pallas_call | solution.py:150
  72.8 0.9 collective-permute-done.15.rest_3_
  73.7 2.9 %correlate.6.rest_6_ = f32[1024,512]{1,0:T(8,128)S(1)} custom-call(bf16[1024,128]{1,0:T(8,128)(2,1)S(1)} %fusion.9.first, bf16[1024,512]{1,0:T(8,128)(2,1)S(1)} %fusion.4.second, bf16[2,128,512]{2,1,0:T(8,128)(2,1)S(1)} %get-tuple-element.45.rest_0_.own, bf16[2,128,512]{2,1,0:T(8,128)(2,1)S(1)} %collective-permute-done.13.rest_1_, ...), custom_call_target="tpu_custom_call" | custom-call | flops 200000000 | bytes 1048576 | tf_op jit(solution)/shard_map/correlate/pallas_call | solution.py:150
  76.6 0.0 copy-start.4
  76.6 0.1 collective-permute-done.10.rest_2_
  76.7 3.0 %collective-permute-done.11.rest_3_ = bf16[2,128,512]{2,1,0:T(8,128)(2,1)S(1)} collective-permute-done((bf16[2,128,512]{2,1,0:T(8,128)(2,1)S(1)}, bf16[2,128,512]{2,1,0:T(8,128)(2,1)S(1)}, u32[]{:S(2)}, u32[]{:S(2)}) %collective-permute-start.11) | collective-permute-done | bytes 262176 | tf_op jit(solution)/shard_map/ppermute | solution.py:331
  79.8 2.9 %correlate.7 = (f32[1024,256]{1,0:T(8,128)S(1)}, bf16[1024,256]{1,0:T(8,128)(2,1)S(1)}) custom-call(bf16[1024,128]{1,0:T(8,128)(2,1)S(1)} %fusion.9.first, bf16[1024,512]{1,0:T(8,128)(2,1)S(1)} %fusion.4.second, bf16[2,128,512]{2,1,0:T(8,128)(2,1)S(1)} %get-tuple-element.47.rest_0_.own, bf16[2,128,512]{2,1,0:T(8,128)(2,1)S(1)} %collective-permute-done.9.rest_1_, ...), custom_call_target="tpu_custom_call" | custom-call | flops 200000000 | bytes 1048576 | tf_op jit(solution)/shard_map/correlate/pallas_call | solution.py:150
  82.6 0.3 collective-permute-start.16
  83.6 0.5 fusion.7
  84.2 0.7 collective-permute-done.16.received
  84.9 0.2 split_kernel.1
  85.1 0.1 collective-permute-start.17
  85.2 2.9 %collective-permute-start.18 = (bf16[512,128]{1,0:T(8,128)(2,1)S(1)}, bf16[512,128]{1,0:T(8,128)(2,1)S(1)}, u32[]{:S(2)}, u32[]{:S(2)}) collective-permute-start(bf16[512,128]{1,0:T(8,128)(2,1)S(1)} %get-tuple-element.43), channel_id=1, source_target_pairs={{0,4},{1,5},{2,6},{3,7},{4,0},{5,1},{6,2},{7,3},{8,12},{9,13},{10,... | collective-permute-start | bytes 393224 | tf_op jit(solution)/shard_map/ppermute | solution.py:344
  88.1 0.6 collective-permute-start.19
  88.7 2.1 %fusion.hot = bf16[2048,1024]{1,0:T(8,128)(2,1)S(1)} fusion(s32[1024]{0:T(1024)S(1)} %add_select_fusion.2), kind=kLoop, calls=%fused_computation.1 | loop fusion | flops 4194304 | bytes 4198400 | tf_op jit(solution)/shard_map/convert_element_type | solution.py:303
  90.8 0.8 collective-permute-done.17.one
  91.5 5.9 %collective-permute-done.18.two = bf16[512,128]{1,0:T(8,128)(2,1)S(1)} collective-permute-done((bf16[512,128]{1,0:T(8,128)(2,1)S(1)}, bf16[512,128]{1,0:T(8,128)(2,1)S(1)}, u32[]{:S(2)}, u32[]{:S(2)}) %collective-permute-start.18) | collective-permute-done | bytes 131104 | tf_op jit(solution)/shard_map/ppermute | solution.py:344
  97.5 2.9 %collective-permute-done.19.three = bf16[512,128]{1,0:T(8,128)(2,1)S(1)} collective-permute-done((bf16[512,128]{1,0:T(8,128)(2,1)S(1)}, bf16[512,128]{1,0:T(8,128)(2,1)S(1)}, u32[]{:S(2)}, u32[]{:S(2)}) %collective-permute-start.19) | collective-permute-done | bytes 131104 | tf_op jit(solution)/shard_map/ppermute | solution.py:344
  100.4 1.4 %route_kernel.1 = bf16[32,32,128]{2,1,0:T(8,128)(2,1)S(1)} custom-call(bf16[2048,1024]{1,0:T(8,128)(2,1)S(1)} %fusion.hot, f32[512,128]{1,0:T(8,128)S(1)} %get-tuple-element.41.keep, bf16[512,128]{1,0:T(8,128)(2,1)S(1)} %collective-permute-done.17.one, bf16[512,128]{1,0:T(8,128)(2,1)S(1)} %collective-permute-done.18.two, ...), custom_call_target="tpu_custom_call" | custom-call | tf_op jit(solution)/shard_map/route_kernel/pallas_call | solution.py:269
  101.8 23.6 %all_to_all.5.routed = bf16[32,32,128]{2,1,0:T(8,128)(2,1)S(1)} all-to-all(bf16[32,32,128]{2,1,0:T(8,128)(2,1)S(1)} %route_kernel.1), channel_id=1, replica_groups=mesh['chan'=32,'win'=8] {'chan'}, dimensions={0} | all-to-all | bytes 524288 | tf_op jit(solution)/shard_map/all_to_all | solution.py:348
  125.4 1.7 %unpack.1 = f32[1,32,64,64]{3,2,1,0:T(8,128)} custom-call(bf16[32,32,128]{2,1,0:T(8,128)(2,1)S(1)} %all_to_all.5.routed), custom_call_target="tpu_custom_call" | custom-call | tf_op jit(solution)/shard_map/unpack/pallas_call | solution.py:257
  (25 shorter events, 0.1 us)
Async XLA Ops:
  1.6 27.3 %collective-permute-start = (bf16[2,128,512]{2,1,0:T(8,128)(2,1)S(1)}, bf16[2,128,512]{2,1,0:T(8,128)(2,1)S(1)}, u32[]{:S(2)}, u32[]{:S(2)}) collective-permute-start(bf16[2,128,512]{2,1,0:T(8,128)(2,1)S(1)} %first_part.1.after.own.rest_0_), channel_id=1, source_target_pairs={{32,0},{33,1},{34,2},{35,3},{36,4},{37,5},{38,6},{39,7},{40,8},{41... | collective-permute-start | bytes 786440 | tf_op jit(solution)/shard_map/ppermute | solution.py:286
  2.9 1.2 copy-start.1
  9.4 31.4 %collective-permute-start.1 = (bf16[2,144,512]{2,1,0:T(8,128)(2,1)}, bf16[2,144,512]{2,1,0:T(8,128)(2,1)}, u32[]{:S(2)}, u32[]{:S(2)}) collective-permute-start(bf16[2,144,512]{2,1,0:T(8,128)(2,1)} %hold.7), channel_id=1, source_target_pairs={{32,0},{33,1},{34,2},{35,3},{36,4},{37,5},{38,6},{39,7},{40,8},{41... | collective-permute-start | bytes 884744 | tf_op jit(solution)/shard_map/ppermute | solution.py:305
  28.9 4.6 %copy-start.2 = (s32[1,1024]{1,0:T(1,128)S(1)}, s32[1,1024]{1,0:T(1,128)}, u32[]{:S(2)}) copy-start(s32[1,1024]{1,0:T(1,128)} %own.3) | copy-start | bytes 12292
  28.9 6.1 %copy-start.3 = (s32[1,1024]{1,0:T(1,128)S(1)}, s32[1,1024]{1,0:T(1,128)}, u32[]{:S(2)}) copy-start(s32[1,1024]{1,0:T(1,128)} %own.4) | copy-start | bytes 12292
  29.0 13.0 %collective-permute-start.6 = (bf16[2,128,512]{2,1,0:T(8,128)(2,1)S(1)}, bf16[2,128,512]{2,1,0:T(8,128)(2,1)S(1)}, u32[]{:S(2)}, u32[]{:S(2)}) collective-permute-start(bf16[2,128,512]{2,1,0:T(8,128)(2,1)S(1)} %get-tuple-element.29), channel_id=1, source_target_pairs={{0,24},{1,25},{2,26},{3,27},{4,28},{5,29},{6,30},{7,31},{8,0},{9,1... | collective-permute-start | bytes 786440 | tf_op jit(solution)/shard_map/ppermute | solution.py:331
  29.1 16.6 %collective-permute-start.7 = (bf16[2,128,512]{2,1,0:T(8,128)(2,1)S(1)}, bf16[2,128,512]{2,1,0:T(8,128)(2,1)S(1)}, u32[]{:S(2)}, u32[]{:S(2)}) collective-permute-start(bf16[2,128,512]{2,1,0:T(8,128)(2,1)S(1)} %get-tuple-element.30), channel_id=1, source_target_pairs={{0,16},{1,17},{2,18},{3,19},{4,20},{5,21},{6,22},{7,23},{8,24},{9,... | collective-permute-start | bytes 786440 | tf_op jit(solution)/shard_map/ppermute | solution.py:331
  32.6 13.9 %collective-permute-start.8 = (bf16[2,128,512]{2,1,0:T(8,128)(2,1)S(1)}, bf16[2,128,512]{2,1,0:T(8,128)(2,1)S(1)}, u32[]{:S(2)}, u32[]{:S(2)}) collective-permute-start(bf16[2,128,512]{2,1,0:T(8,128)(2,1)S(1)} %get-tuple-element.31), channel_id=1, source_target_pairs={{0,8},{1,9},{2,10},{3,11},{4,12},{5,13},{6,14},{7,15},{8,16},{9,17... | collective-permute-start | bytes 786440 | tf_op jit(solution)/shard_map/ppermute | solution.py:331
  33.7 14.2 %collective-permute-start.12 = (bf16[2,128,512]{2,1,0:T(8,128)(2,1)S(1)}, bf16[2,128,512]{2,1,0:T(8,128)(2,1)S(1)}, u32[]{:S(2)}, u32[]{:S(2)}) collective-permute-start(bf16[2,128,512]{2,1,0:T(8,128)(2,1)S(1)} %get-tuple-element.35), channel_id=1, source_target_pairs={{32,0},{33,1},{34,2},{35,3},{36,4},{37,5},{38,6},{39,7},{40,8},{41... | collective-permute-start | bytes 786440 | tf_op jit(solution)/shard_map/ppermute | solution.py:330
  41.8 10.0 %collective-permute-start.3 = (bf16[2,144,512]{2,1,0:T(8,128)(2,1)S(1)}, bf16[2,144,512]{2,1,0:T(8,128)(2,1)S(1)}, u32[]{:S(2)}, u32[]{:S(2)}) collective-permute-start(bf16[2,144,512]{2,1,0:T(8,128)(2,1)S(1)} %get-tuple-element.26), channel_id=1, source_target_pairs={{0,24},{1,25},{2,26},{3,27},{4,28},{5,29},{6,30},{7,31},{8,0},{9,1... | collective-permute-start | bytes 884744 | tf_op jit(solution)/shard_map/ppermute | solution.py:331
  41.9 15.3 %collective-permute-start.4 = (bf16[2,144,512]{2,1,0:T(8,128)(2,1)S(1)}, bf16[2,144,512]{2,1,0:T(8,128)(2,1)S(1)}, u32[]{:S(2)}, u32[]{:S(2)}) collective-permute-start(bf16[2,144,512]{2,1,0:T(8,128)(2,1)S(1)} %get-tuple-element.27), channel_id=1, source_target_pairs={{0,16},{1,17},{2,18},{3,19},{4,20},{5,21},{6,22},{7,23},{8,24},{9,... | collective-permute-start | bytes 884744 | tf_op jit(solution)/shard_map/ppermute | solution.py:331
  45.6 16.8 %collective-permute-start.5 = (bf16[2,144,512]{2,1,0:T(8,128)(2,1)S(1)}, bf16[2,144,512]{2,1,0:T(8,128)(2,1)S(1)}, u32[]{:S(2)}, u32[]{:S(2)}) collective-permute-start(bf16[2,144,512]{2,1,0:T(8,128)(2,1)S(1)} %get-tuple-element.28), channel_id=1, source_target_pairs={{0,8},{1,9},{2,10},{3,11},{4,12},{5,13},{6,14},{7,15},{8,16},{9,17... | collective-permute-start | bytes 884744 | tf_op jit(solution)/shard_map/ppermute | solution.py:331
  46.5 15.9 %copy-start = (bf16[2048,512]{1,0:T(8,128)(2,1)S(1)}, bf16[2048,512]{1,0:T(8,128)(2,1)}, u32[]{:S(2)}) copy-start(bf16[2048,512]{1,0:T(8,128)(2,1)} %fusion.1.rest_5_) | copy-start | bytes 6291460
  46.5 18.8 %collective-permute-start.2 = (bf16[2,128,512]{2,1,0:T(8,128)(2,1)S(1)}, bf16[2,128,512]{2,1,0:T(8,128)(2,1)S(1)}, u32[]{:S(2)}, u32[]{:S(2)}) collective-permute-start(bf16[2,128,512]{2,1,0:T(8,128)(2,1)S(1)} %get-tuple-element.25), channel_id=1, source_target_pairs={{32,0},{33,1},{34,2},{35,3},{36,4},{37,5},{38,6},{39,7},{40,8},{41... | collective-permute-start | bytes 786440 | tf_op jit(solution)/shard_map/ppermute | solution.py:330
  48.0 18.6 %collective-permute-start.13 = (bf16[2,128,512]{2,1,0:T(8,128)(2,1)S(1)}, bf16[2,128,512]{2,1,0:T(8,128)(2,1)S(1)}, u32[]{:S(2)}, u32[]{:S(2)}) collective-permute-start(bf16[2,128,512]{2,1,0:T(8,128)(2,1)S(1)} %get-tuple-element.36), channel_id=1, source_target_pairs={{0,24},{1,25},{2,26},{3,27},{4,28},{5,29},{6,30},{7,31},{8,0},{9,1... | collective-permute-start | bytes 786440 | tf_op jit(solution)/shard_map/ppermute | solution.py:331
  51.9 20.9 %collective-permute-start.14 = (bf16[2,128,512]{2,1,0:T(8,128)(2,1)S(1)}, bf16[2,128,512]{2,1,0:T(8,128)(2,1)S(1)}, u32[]{:S(2)}, u32[]{:S(2)}) collective-permute-start(bf16[2,128,512]{2,1,0:T(8,128)(2,1)S(1)} %get-tuple-element.37), channel_id=1, source_target_pairs={{0,16},{1,17},{2,18},{3,19},{4,20},{5,21},{6,22},{7,23},{8,24},{9,... | collective-permute-start | bytes 786440 | tf_op jit(solution)/shard_map/ppermute | solution.py:331
  57.2 16.5 %collective-permute-start.15 = (bf16[2,128,512]{2,1,0:T(8,128)(2,1)S(1)}, bf16[2,128,512]{2,1,0:T(8,128)(2,1)S(1)}, u32[]{:S(2)}, u32[]{:S(2)}) collective-permute-start(bf16[2,128,512]{2,1,0:T(8,128)(2,1)S(1)} %get-tuple-element.38), channel_id=1, source_target_pairs={{0,8},{1,9},{2,10},{3,11},{4,12},{5,13},{6,14},{7,15},{8,16},{9,17... | collective-permute-start | bytes 786440 | tf_op jit(solution)/shard_map/ppermute | solution.py:331
  65.4 11.3 %collective-permute-start.10 = (bf16[2,128,512]{2,1,0:T(8,128)(2,1)S(1)}, bf16[2,128,512]{2,1,0:T(8,128)(2,1)S(1)}, u32[]{:S(2)}, u32[]{:S(2)}) collective-permute-start(bf16[2,128,512]{2,1,0:T(8,128)(2,1)S(1)} %get-tuple-element.33), channel_id=1, source_target_pairs={{0,16},{1,17},{2,18},{3,19},{4,20},{5,21},{6,22},{7,23},{8,24},{9,... | collective-permute-start | bytes 786440 | tf_op jit(solution)/shard_map/ppermute | solution.py:331
  66.7 13.1 %collective-permute-start.11 = (bf16[2,128,512]{2,1,0:T(8,128)(2,1)S(1)}, bf16[2,128,512]{2,1,0:T(8,128)(2,1)S(1)}, u32[]{:S(2)}, u32[]{:S(2)}) collective-permute-start(bf16[2,128,512]{2,1,0:T(8,128)(2,1)S(1)} %get-tuple-element.34), channel_id=1, source_target_pairs={{0,8},{1,9},{2,10},{3,11},{4,12},{5,13},{6,14},{7,15},{8,16},{9,17... | collective-permute-start | bytes 786440 | tf_op jit(solution)/shard_map/ppermute | solution.py:331
  66.7 13.1 %collective-permute-start.9 = (bf16[2,128,512]{2,1,0:T(8,128)(2,1)S(1)}, bf16[2,128,512]{2,1,0:T(8,128)(2,1)S(1)}, u32[]{:S(2)}, u32[]{:S(2)}) collective-permute-start(bf16[2,128,512]{2,1,0:T(8,128)(2,1)S(1)} %get-tuple-element.32), channel_id=1, source_target_pairs={{0,24},{1,25},{2,26},{3,27},{4,28},{5,29},{6,30},{7,31},{8,0},{9,1... | collective-permute-start | bytes 786440 | tf_op jit(solution)/shard_map/ppermute | solution.py:331
  76.6 7.0 %copy-start.4 = (s32[1,1024,1]{1,2,0:T(1,128)S(1)}, s32[1,1024,1]{1,2,0:T(1,128)}, u32[]{:S(2)}) copy-start(s32[1,1024,1]{1,2,0:T(1,128)} %param.9) | copy-start | bytes 12292
  82.6 2.2 %collective-permute-start.16 = (bf16[1024,256]{1,0:T(8,128)(2,1)S(1)}, bf16[1024,256]{1,0:T(8,128)(2,1)S(1)}, u32[]{:S(2)}, u32[]{:S(2)}) collective-permute-start(bf16[1024,256]{1,0:T(8,128)(2,1)S(1)} %get-tuple-element.40), channel_id=1, source_target_pairs={{0,1},{1,0},{2,3},{3,2},{4,5},{5,4},{6,7},{7,6},{8,9},{9,8},{10,11... | collective-permute-start | bytes 1572872 | tf_op jit(solution)/shard_map/ppermute | solution.py:336
  85.1 6.4 %collective-permute-start.17 = (bf16[512,128]{1,0:T(8,128)(2,1)S(1)}, bf16[512,128]{1,0:T(8,128)(2,1)S(1)}, u32[]{:S(2)}, u32[]{:S(2)}) collective-permute-start(bf16[512,128]{1,0:T(8,128)(2,1)S(1)} %get-tuple-element.42), channel_id=1, source_target_pairs={{0,2},{1,3},{2,0},{3,1},{4,6},{5,7},{6,4},{7,5},{8,10},{9,11},{10,... | collective-permute-start | bytes 393224 | tf_op jit(solution)/shard_map/ppermute | solution.py:344
  85.2 12.3 %collective-permute-start.18 = (bf16[512,128]{1,0:T(8,128)(2,1)S(1)}, bf16[512,128]{1,0:T(8,128)(2,1)S(1)}, u32[]{:S(2)}, u32[]{:S(2)}) collective-permute-start(bf16[512,128]{1,0:T(8,128)(2,1)S(1)} %get-tuple-element.43), channel_id=1, source_target_pairs={{0,4},{1,5},{2,6},{3,7},{4,0},{5,1},{6,2},{7,3},{8,12},{9,13},{10,... | collective-permute-start | bytes 393224 | tf_op jit(solution)/shard_map/ppermute | solution.py:344
  88.1 12.3 %collective-permute-start.19 = (bf16[512,128]{1,0:T(8,128)(2,1)S(1)}, bf16[512,128]{1,0:T(8,128)(2,1)S(1)}, u32[]{:S(2)}, u32[]{:S(2)}) collective-permute-start(bf16[512,128]{1,0:T(8,128)(2,1)S(1)} %get-tuple-element.44), channel_id=1, source_target_pairs={{0,6},{1,7},{2,4},{3,5},{4,2},{5,3},{6,0},{7,1},{8,14},{9,15},{10,... | collective-permute-start | bytes 393224 | tf_op jit(solution)/shard_map/ppermute | solution.py:344
